TPU v7x, 32 devices: a whole 2x2x4 slice. The times are simulated.
32 devices in a mesh: scen: 2 (over y), gx: 4 (over z), gy: 4 (over x, core).
Axes of the slice: x: 2, y: 2, z: 4, core: 2. Of those that a mesh axis runs over, the one named last changes fastest.
Arguments:
- ocean_eta: float32 [512, 512], P(('scen', 'gx'), 'gy'), parts along dimension 0, may hold values from -1 to 1
- ocean_mx: float32 [512, 512], P(('scen', 'gx'), 'gy'), parts along dimension 0, may hold values from -1.5 to 1.5
- ocean_ny: float32 [512, 512], P(('scen', 'gx'), 'gy'), parts along dimension 0, may hold values from -1.5 to 1.5
- ocean_depth: float32 [512, 512], P(('scen', 'gx'), 'gy'), parts along dimension 0, may hold values from 0.1 to 2
- ocean_class: int32 [512, 512], P(('scen', 'gx'), 'gy'), parts along dimension 0, may hold values from 0 to 5
- manning: float32 [6], replicated, may hold values from 0.05 to 0.8
- fine_eta: float32 [1536, 1536], P(('scen', 'gx'), 'gy'), parts along dimension 0, may hold values from -1 to 1
- fine_qx: float32 [1536, 1536], P(('scen', 'gx'), 'gy'), parts along dimension 0, may hold values from -1 to 1
- fine_qy: float32 [1536, 1536], P(('scen', 'gx'), 'gy'), parts along dimension 0, may hold values from -1 to 1
- fine_depth: float32 [1536, 1536], P(('scen', 'gx'), 'gy'), parts along dimension 0, may hold values from -0.2 to 1
- fine_wet: int32 [1536, 1536], P(('scen', 'gx'), 'gy'), parts along dimension 0, may hold values 0 or 1
- fine_class: int32 [1536, 1536], P(('scen', 'gx'), 'gy'), parts along dimension 0, may hold values from 0 to 5
- fine_offset: int32 [4], P('scen'), parts along dimension 0, may hold values from 1 to 63, as said below
Outputs:
- new_ocean_eta: float32 [512, 512], P(('scen', 'gx'), 'gy'), parts along dimension 0
- new_ocean_mx: float32 [512, 512], P(('scen', 'gx'), 'gy'), parts along dimension 0
- new_ocean_ny: float32 [512, 512], P(('scen', 'gx'), 'gy'), parts along dimension 0
- new_fine_eta: float32 [1536, 1536], P(('scen', 'gx'), 'gy'), parts along dimension 0
- new_fine_qx: float32 [1536, 1536], P(('scen', 'gx'), 'gy'), parts along dimension 0
- new_fine_qy: float32 [1536, 1536], P(('scen', 'gx'), 'gy'), parts along dimension 0
There are 2 independent parts, one for each index of `scen`. A program takes and returns all parts, laid end to end along the dimension named above; an argument that names none is the same for every part. Nothing has to cross between parts.
Inputs may be any that keep to these rules, and one draw needn't show every extreme that they name: `fine_offset`: one coastal grid has offset 1 and another has offset 64 - 1.
All inputs are finite; a program needn't handle non-finite values. No bound on the sum of `fine_wet` on one device may be relied on, other than what follows from the above.
Results may differ from a plain program's by a relative error of at most 0.0003.
Values sent between devices are 32-bit elements; how exact they have to be, the bound alone decides.
No kernel may reach another device: no remote copies, remote signals or barrier semaphores. Data moves between devices by JAX's collectives and lax.ppermute only.
A program may use at most 64 MiB of HBM per device.

v0:
```python
import jax
import jax.numpy as jnp
from jax import lax
from jax.sharding import PartitionSpec as P

R = 3
ITERS = 4


COURANT = 0.45
FLOOR = 0.25
EXPO = 7.0 / 3.0


def shifted(value, axis, steps):
    count = lax.axis_size(axis)
    initial, last = (max(0, -steps), min(count, count - steps))
    return lax.ppermute(value, axis, [(source, source + steps) for source in range(initial, last)])


def friction_of(classes, table):
    result = jnp.zeros(classes.shape, jnp.float32)
    for level_id in range(table.shape[0]):
        result = result + jnp.where(classes == level_id, table[level_id], jnp.float32(0.0))
    return result


def momentum(flux, eta, eta_next, depth, depth_next, kfric, kfric_next, openness):
    total = 0.5 * (jnp.maximum(depth + eta, 0.0) + jnp.maximum(depth_next + eta_next, 0.0))
    drag = 1.0 + COURANT * 0.5 * (kfric + kfric_next) * jnp.abs(flux) / jnp.power(
        jnp.maximum(total, FLOOR), EXPO
    )
    return openness * (flux - COURANT * total * (eta_next - eta)) / drag


def level(eta, flux_x, flux_y, west_row, south_col):
    flux_west = jnp.concatenate([west_row, flux_x[:-1]], 0)
    flux_south = jnp.concatenate([south_col, flux_y[:, :-1]], 1)
    return eta - COURANT * (flux_x - flux_west + flux_y - flux_south)


def flows(eta, flux_x, flux_y, depth, kfric, north_rows, east_cols, open_x, open_y):
    eta_n0 = jnp.concatenate([eta[1:], north_rows[0]], 0)
    depth_n0 = jnp.concatenate([depth[1:], north_rows[1]], 0)
    kfric_n0 = jnp.concatenate([kfric[1:], north_rows[2]], 0)
    eta_n1 = jnp.concatenate([eta[:, 1:], east_cols[0]], 1)
    depth_n1 = jnp.concatenate([depth[:, 1:], east_cols[1]], 1)
    kfric_n1 = jnp.concatenate([kfric[:, 1:], east_cols[2]], 1)
    new_x = momentum(flux_x, eta, eta_n0, depth, depth_n0, kfric, kfric_n0, open_x)
    new_y = momentum(flux_y, eta, eta_n1, depth, depth_n1, kfric, kfric_n1, open_y)
    return (new_x, new_y)


def ocean_steps(eta, flux_x, flux_y, depth, kfric, gx_index, gy_index, gx_count, gy_count):
    rows, cols = eta.shape
    row_glob = gx_index * rows + jnp.arange(rows, dtype=jnp.int32)
    col_glob = gy_index * cols + jnp.arange(cols, dtype=jnp.int32)
    open_x = (row_glob < rows * gx_count - 1).astype(jnp.float32)[:, None]
    open_y = (col_glob < cols * gy_count - 1).astype(jnp.float32)[None, :]
    bed_rows = shifted(jnp.stack([depth[:1], kfric[:1]]), "gx", -1)
    bed_cols = shifted(jnp.stack([depth[:, :1], kfric[:, :1]]), "gy", -1)
    for step in range(ITERS):
        west_row = shifted(flux_x[-1:], "gx", 1)
        south_col = shifted(flux_y[:, -1:], "gy", 1)
        eta = level(eta, flux_x, flux_y, west_row, south_col)
        north_eta = shifted(eta[:1], "gx", -1)
        east_eta = shifted(eta[:, :1], "gy", -1)
        flux_x, flux_y = flows(
            eta,
            flux_x,
            flux_y,
            depth,
            kfric,
            (north_eta, bed_rows[0], bed_rows[1]),
            (east_eta, bed_cols[0], bed_cols[1]),
            open_x,
            open_y,
        )
    return (eta, flux_x, flux_y)


def coastal_steps(eta, flux_x, flux_y, depth, kfric, wet, west, east, first_dev, last_dev):
    rows, cols = eta.shape
    fsteps = R * ITERS
    width = 0
    bed_rows = shifted(jnp.stack([depth[:1], kfric[:1], wet[:1]]), "gx", -1)
    inside = jnp.where(last_dev, jnp.float32(0.0), jnp.float32(1.0))
    face_x = wet * jnp.concatenate([wet[1:], bed_rows[2] * inside], 0)
    bed_cols = shifted(jnp.stack([depth[:, :1], kfric[:, :1], wet[:, :1]]), "gy", -1)
    face_y = wet * jnp.concatenate([wet[:, 1:], bed_cols[2]], 1)
    for step in range(fsteps):
        from_west = shifted(flux_x[-1:], "gx", 1)
        west_row = jnp.where(first_dev, west, from_west)
        south_col = shifted(flux_y[:, -1:], "gy", 1)
        eta = level(eta, flux_x, flux_y, west_row, south_col)
        north_eta = shifted(eta[:1], "gx", -1)
        east_eta = shifted(eta[:, :1], "gy", -1)
        flux_x, flux_y = flows(
            eta,
            flux_x,
            flux_y,
            depth,
            kfric,
            (north_eta, bed_rows[0], bed_rows[1]),
            (east_eta, bed_cols[0], bed_cols[1]),
            face_x,
            face_y,
        )
        flux_x = jnp.where(last_dev, jnp.concatenate([flux_x[:-1], east], 0), flux_x)
    inner = (slice(0, rows), slice(width, width + cols))
    return (eta, flux_x, flux_y)


def shards(
    ocean_eta,
    ocean_mx,
    ocean_ny,
    ocean_depth,
    ocean_class,
    manning,
    fine_eta,
    fine_qx,
    fine_qy,
    fine_depth,
    fine_wet,
    fine_class,
    fine_offset,
):
    rows, cols = ocean_eta.shape
    gx_index = lax.axis_index("gx")
    gy_index = lax.axis_index("gy")
    gx_count = lax.axis_size("gx")
    gy_count = lax.axis_size("gy")
    block_size = min(16, gx_count // 2)
    grid_index = gx_index // block_size
    slot_index = gx_index - grid_index * block_size
    first_dev = slot_index == 0
    last_dev = slot_index == block_size - 1
    grid_ids = jnp.arange(fine_offset.shape[0], dtype=jnp.int32)
    own_offset = jnp.sum(jnp.where(grid_ids == grid_index, fine_offset, 0))
    left_grid = (gx_index - 1) // block_size
    left_offset = jnp.sum(jnp.where(grid_ids == left_grid, fine_offset, 0))
    west_src = lax.dynamic_slice_in_dim(ocean_mx, own_offset - 1, 1, 0)
    east_src = ocean_mx[-1:]
    wet = fine_wet.astype(jnp.float32)
    west = jnp.repeat(west_src, R, axis=1) * wet[:1]
    east = jnp.repeat(east_src, R, axis=1) * wet[-1:]
    fkfric = friction_of(fine_class, manning)
    okfric = friction_of(ocean_class, manning)
    eta, flux_x, flux_y = ocean_steps(
        ocean_eta, ocean_mx, ocean_ny, ocean_depth, okfric, gx_index, gy_index, gx_count, gy_count
    )
    feta, fqx, fqy = coastal_steps(
        fine_eta, fine_qx, fine_qy, fine_depth, fkfric, wet, west, east, first_dev, last_dev
    )
    means = jnp.mean(feta.reshape(rows, R, cols, R), axis=(1, 3))
    doubled = jnp.concatenate([means, means], 0)
    rolled = lax.dynamic_slice_in_dim(doubled, rows - own_offset, rows, 0)
    arrived = shifted(rolled, "gx", 1)
    row_ids = jnp.arange(rows, dtype=jnp.int32)[:, None]
    from_left = (row_ids < left_offset) & (gx_index >= 1)
    eta = jnp.where(row_ids >= own_offset, rolled, jnp.where(from_left, arrived, eta))
    return (eta, flux_x, flux_y, feta, fqx, fqy)


def solution(mesh):
    in_specs = (
        P(("scen", "gx"), "gy"),
        P(("scen", "gx"), "gy"),
        P(("scen", "gx"), "gy"),
        P(("scen", "gx"), "gy"),
        P(("scen", "gx"), "gy"),
        P(),
        P(("scen", "gx"), "gy"),
        P(("scen", "gx"), "gy"),
        P(("scen", "gx"), "gy"),
        P(("scen", "gx"), "gy"),
        P(("scen", "gx"), "gy"),
        P(("scen", "gx"), "gy"),
        P("scen"),
    )
    out_specs = (
        P(("scen", "gx"), "gy"),
        P(("scen", "gx"), "gy"),
        P(("scen", "gx"), "gy"),
        P(("scen", "gx"), "gy"),
        P(("scen", "gx"), "gy"),
        P(("scen", "gx"), "gy"),
    )
    return jax.shard_map(shards, mesh=mesh, in_specs=in_specs, out_specs=out_specs, check_vma=False)
```

profile of v0, /device:TPU:1, one launch (start us, length us, event | category | flops | bytes accessed | tf_op | source)
XLA Modules:
  0.0 320.4 jit_solution(17672746284919275057)
XLA Ops:
  1.5 4.0 %collective-permute-start = (f32[1,384]{1,0:T(1,128)S(1)}, f32[1,384]{1,0:T(1,128)S(1)}, u32[]{:S(2)}, u32[]{:S(2)}) collective-permute-start(f32[1,384]{1,0:T(1,128)S(1)} %slice.654), channel_id=1, source_target_pairs={{0,4},{4,8},{8,12},{1,5},{5,9},{9,13},{2,6},{6,10},{10,14},{3,7},{... | collective-permute-start | bytes 4616 | tf_op jit(solution)/shard_map/ppermute | solution.py:18
  13.0 4.8 %select_add_fusion = f32[192,384]{1,0:T(8,128)S(1)} fusion(s32[192,384]{1,0:T(8,128)} %param.24, f32[]{:T(128)} %bitcast.7, f32[]{:T(128)} %bitcast.6, f32[]{:T(128)} %bitcast.5, f32[]{:T(128)} %bitcast.4, f32[]{:T(128)} %bitcast.3, f32[]{:T(128)} %bitcast.2), kind=kLoop, calls=%fused_computation.152 | loop fusion | flops 1253376 | bytes 589848 | tf_op jit(solution)/shard_map/add | solution.py:24
  40.8 5.5 %add_divide_fusion.23 = (f32[192,384]{1,0:T(8,128)S(1)}, f32[192,384]{1,0:T(8,128)S(1)}, f32[192,384]{1,0:T(8,128)S(1)}) fusion(f32[192,384]{1,0:T(8,128)} %param.20, f32[192,384]{1,0:T(8,128)S(1)} %fusion.15, f32[1,384]{1,0:T(1,128)S(1)} %collective-permute-done.3, f32[191,384]{1,0:T(8,128)} %slice.836, f32[192,384]{1,0:T(8,128)} %param.22, ...), kind=kLoop, calls=%fused_computation.150 | loop fusion | flops 3096576 | bytes 3538968 | tf_op jit(solution)/shard_map/div | solution.py:33
  50.4 5.6 %add_divide_fusion.22 = (f32[192,384]{1,0:T(8,128)S(1)}, f32[192,384]{1,0:T(8,128)S(1)}, f32[192,384]{1,0:T(8,128)S(1)}, f32[192,384]{1,0:T(8,128)S(1)}) fusion(f32[192,384]{1,0:T(8,128)S(1)} %copy-done.2, f32[192,384]{1,0:T(8,128)S(1)} %fusion.15, f32[192,1]{1,0:T(8,128)} %collective-permute-done.6, f32[192,383]{1,0:T(8,128)} %slice.849, ...), kind=kLoop, calls=%fused_computation.149 | loop fusion | flops 3096576 | bytes 3833880 | tf_op jit(solution)/shard_map/div | solution.py:33
  56.1 4.8 %collective-permute-start.7 = (f32[192,1]{1,0:T(8,128)S(1)}, f32[192,1]{1,0:T(8,128)S(1)}, u32[]{:S(2)}, u32[]{:S(2)}) collective-permute-start(f32[192,1]{1,0:T(8,128)S(1)} %slice.853), channel_id=1, source_target_pairs={{0,1},{1,2},{2,3},{4,5},{5,6},{6,7},{8,9},{9,10},{10,11},{12,13},{... | collective-permute-start | bytes 2312 | tf_op jit(solution)/shard_map/ppermute | solution.py:18
  66.1 4.5 %collective-permute-done.10 = f32[192,1]{1,0:T(8,128)S(1)} collective-permute-done((f32[192,1]{1,0:T(8,128)S(1)}, f32[192,1]{1,0:T(8,128)S(1)}, u32[]{:S(2)}, u32[]{:S(2)}) %collective-permute-start.10) | collective-permute-done | bytes 800 | tf_op jit(solution)/shard_map/ppermute | solution.py:18
  71.3 4.3 %collective-permute-start.9 = (f32[1,384]{1,0:T(1,128)S(1)}, f32[1,384]{1,0:T(1,128)S(1)}, u32[]{:S(2)}, u32[]{:S(2)}) collective-permute-start(f32[1,384]{1,0:T(1,128)S(1)} %slice.858), channel_id=1, source_target_pairs={{0,4},{4,8},{8,12},{1,5},{5,9},{9,13},{2,6},{6,10},{10,14},{3,7},{... | collective-permute-start | bytes 4616 | tf_op jit(solution)/shard_map/ppermute | solution.py:18
  92.2 4.3 %collective-permute-start.13 = (f32[1,384]{1,0:T(1,128)S(1)}, f32[1,384]{1,0:T(1,128)S(1)}, u32[]{:S(2)}, u32[]{:S(2)}) collective-permute-start(f32[1,384]{1,0:T(1,128)S(1)} %slice.867), channel_id=1, source_target_pairs={{0,4},{4,8},{8,12},{1,5},{5,9},{9,13},{2,6},{6,10},{10,14},{3,7},{... | collective-permute-start | bytes 4616 | tf_op jit(solution)/shard_map/ppermute | solution.py:18
  105.6 4.5 %collective-permute-done.18 = f32[192,1]{1,0:T(8,128)S(1)} collective-permute-done((f32[192,1]{1,0:T(8,128)S(1)}, f32[192,1]{1,0:T(8,128)S(1)}, u32[]{:S(2)}, u32[]{:S(2)}) %collective-permute-start.18) | collective-permute-done | bytes 800 | tf_op jit(solution)/shard_map/ppermute | solution.py:18
  110.8 4.3 %collective-permute-start.17 = (f32[1,384]{1,0:T(1,128)S(1)}, f32[1,384]{1,0:T(1,128)S(1)}, u32[]{:S(2)}, u32[]{:S(2)}) collective-permute-start(f32[1,384]{1,0:T(1,128)S(1)} %slice.876), channel_id=1, source_target_pairs={{0,4},{4,8},{8,12},{1,5},{5,9},{9,13},{2,6},{6,10},{10,14},{3,7},{... | collective-permute-start | bytes 4616 | tf_op jit(solution)/shard_map/ppermute | solution.py:18
  124.0 4.4 %collective-permute-done.22 = f32[192,1]{1,0:T(8,128)S(1)} collective-permute-done((f32[192,1]{1,0:T(8,128)S(1)}, f32[192,1]{1,0:T(8,128)S(1)}, u32[]{:S(2)}, u32[]{:S(2)}) %collective-permute-start.22) | collective-permute-done | bytes 800 | tf_op jit(solution)/shard_map/ppermute | solution.py:18
  129.0 4.9 %collective-permute-start.21 = (f32[1,384]{1,0:T(1,128)S(1)}, f32[1,384]{1,0:T(1,128)S(1)}, u32[]{:S(2)}, u32[]{:S(2)}) collective-permute-start(f32[1,384]{1,0:T(1,128)S(1)} %slice.885), channel_id=1, source_target_pairs={{0,4},{4,8},{8,12},{1,5},{5,9},{9,13},{2,6},{6,10},{10,14},{3,7},{... | collective-permute-start | bytes 4616 | tf_op jit(solution)/shard_map/ppermute | solution.py:18
  148.2 4.3 %collective-permute-start.25 = (f32[1,384]{1,0:T(1,128)S(1)}, f32[1,384]{1,0:T(1,128)S(1)}, u32[]{:S(2)}, u32[]{:S(2)}) collective-permute-start(f32[1,384]{1,0:T(1,128)S(1)} %slice.894), channel_id=1, source_target_pairs={{0,4},{4,8},{8,12},{1,5},{5,9},{9,13},{2,6},{6,10},{10,14},{3,7},{... | collective-permute-start | bytes 4616 | tf_op jit(solution)/shard_map/ppermute | solution.py:18
  170.5 4.3 %collective-permute-start.29 = (f32[1,384]{1,0:T(1,128)S(1)}, f32[1,384]{1,0:T(1,128)S(1)}, u32[]{:S(2)}, u32[]{:S(2)}) collective-permute-start(f32[1,384]{1,0:T(1,128)S(1)} %slice.903), channel_id=1, source_target_pairs={{0,4},{4,8},{8,12},{1,5},{5,9},{9,13},{2,6},{6,10},{10,14},{3,7},{... | collective-permute-start | bytes 4616 | tf_op jit(solution)/shard_map/ppermute | solution.py:18
  189.4 4.3 %collective-permute-start.33 = (f32[1,384]{1,0:T(1,128)S(1)}, f32[1,384]{1,0:T(1,128)S(1)}, u32[]{:S(2)}, u32[]{:S(2)}) collective-permute-start(f32[1,384]{1,0:T(1,128)S(1)} %slice.912), channel_id=1, source_target_pairs={{0,4},{4,8},{8,12},{1,5},{5,9},{9,13},{2,6},{6,10},{10,14},{3,7},{... | collective-permute-start | bytes 4616 | tf_op jit(solution)/shard_map/ppermute | solution.py:18
  212.0 4.9 %collective-permute-start.37 = (f32[1,384]{1,0:T(1,128)S(1)}, f32[1,384]{1,0:T(1,128)S(1)}, u32[]{:S(2)}, u32[]{:S(2)}) collective-permute-start(f32[1,384]{1,0:T(1,128)S(1)} %slice.921), channel_id=1, source_target_pairs={{0,4},{4,8},{8,12},{1,5},{5,9},{9,13},{2,6},{6,10},{10,14},{3,7},{... | collective-permute-start | bytes 4616 | tf_op jit(solution)/shard_map/ppermute | solution.py:18
  217.0 4.5 %add_divide_fusion.31 = (f32[64,128]{1,0:T(8,128)S(1)}, f32[64,128]{1,0:T(8,128)S(1)}, f32[64,128]{1,0:T(8,128)S(1)}, f32[64,128]{1,0:T(8,128)S(1)}, f32[64,128]{1,0:T(8,128)S(1)}) fusion(f32[64,128]{1,0:T(8,128)S(1)} %copy-done.7, f32[64,128]{1,0:T(8,128)S(1)} %fusion.66, f32[1,128]{1,0:T(1,128)S(1)} %collective-permute-done.52, f32[63,128]{1,0:T(8,128)S(1)} %slice.947, ...), kind=kLoop, calls=%fused_computation.206 | loop fusion | flops 483328 | bytes 525080 | tf_op jit(solution)/shard_map/div | solution.py:33
  240.0 4.3 %collective-permute-start.41 = (f32[1,384]{1,0:T(1,128)S(1)}, f32[1,384]{1,0:T(1,128)S(1)}, u32[]{:S(2)}, u32[]{:S(2)}) collective-permute-start(f32[1,384]{1,0:T(1,128)S(1)} %slice.930), channel_id=1, source_target_pairs={{0,4},{4,8},{8,12},{1,5},{5,9},{9,13},{2,6},{6,10},{10,14},{3,7},{... | collective-permute-start | bytes 4616 | tf_op jit(solution)/shard_map/ppermute | solution.py:18
  248.5 4.7 %collective-permute-start.60 = (f32[64,1]{1,0:T(8,128)S(1)}, f32[64,1]{1,0:T(8,128)S(1)}, u32[]{:S(2)}, u32[]{:S(2)}) collective-permute-start(f32[64,1]{1,0:T(8,128)S(1)} %slice.967), channel_id=1, source_target_pairs={{0,1},{1,2},{2,3},{4,5},{5,6},{6,7},{8,9},{9,10},{10,11},{12,13},{... | collective-permute-start | bytes 776 | tf_op jit(solution)/shard_map/ppermute | solution.py:18
  265.7 4.3 %collective-permute-start.45 = (f32[1,384]{1,0:T(1,128)S(1)}, f32[1,384]{1,0:T(1,128)S(1)}, u32[]{:S(2)}, u32[]{:S(2)}) collective-permute-start(f32[1,384]{1,0:T(1,128)S(1)} %slice.939), channel_id=1, source_target_pairs={{0,4},{4,8},{8,12},{1,5},{5,9},{9,13},{2,6},{6,10},{10,14},{3,7},{... | collective-permute-start | bytes 4616 | tf_op jit(solution)/shard_map/ppermute | solution.py:18
  273.6 4.7 %collective-permute-start.64 = (f32[64,1]{1,0:T(8,128)S(1)}, f32[64,1]{1,0:T(8,128)S(1)}, u32[]{:S(2)}, u32[]{:S(2)}) collective-permute-start(f32[64,1]{1,0:T(8,128)S(1)} %slice.975), channel_id=1, source_target_pairs={{0,1},{1,2},{2,3},{4,5},{5,6},{6,7},{8,9},{9,10},{10,11},{12,13},{... | collective-permute-start | bytes 776 | tf_op jit(solution)/shard_map/ppermute | solution.py:18
  282.2 13.4 %reshape.63 = f32[64,3,128,3]{3,2,1,0:T(8,128)} reshape(f32[192,384]{1,0:T(8,128)S(1)} %fusion.61) | data formatting | bytes 589824 | tf_op jit(solution)/shard_map/reshape | solution.py:156
  298.9 5.7 %reduce_sum.28 = f32[64,128]{1,0:T(8,128)S(1)} reduce(f32[64,3,128,3]{3,2,1,0:T(8,128)} %reshape.63, f32[]{:T(128)} %constant.135.clone.1), dimensions={1,3}, to_apply=%region_1.2 | reduce | flops 65536 | bytes 327684 | tf_op jit(solution)/shard_map/reduce_sum | solution.py:156
  304.9 4.1 %collective-permute-start.48 = (f32[64,128]{1,0:T(8,128)S(1)}, f32[64,128]{1,0:T(8,128)S(1)}, u32[]{:S(2)}, u32[]{:S(2)}) collective-permute-start(f32[64,128]{1,0:T(8,128)S(1)} %fusion.62), channel_id=1, source_target_pairs={{0,4},{4,8},{8,12},{1,5},{5,9},{9,13},{2,6},{6,10},{10,14},{3,7},{... | collective-permute-start | bytes 98312 | tf_op jit(solution)/shard_map/ppermute | solution.py:18
  (345 shorter events, 196.1 us)
Async XLA Ops:
  1.5 29.3 %collective-permute-start = (f32[1,384]{1,0:T(1,128)S(1)}, f32[1,384]{1,0:T(1,128)S(1)}, u32[]{:S(2)}, u32[]{:S(2)}) collective-permute-start(f32[1,384]{1,0:T(1,128)S(1)} %slice.654), channel_id=1, source_target_pairs={{0,4},{4,8},{8,12},{1,5},{5,9},{9,13},{2,6},{6,10},{10,14},{3,7},{... | collective-permute-start | bytes 4616 | tf_op jit(solution)/shard_map/ppermute | solution.py:18
  6.5 24.3 %collective-permute-start.1 = (f32[192,1]{1,0:T(8,128)S(1)}, f32[192,1]{1,0:T(8,128)S(1)}, u32[]{:S(2)}, u32[]{:S(2)}) collective-permute-start(f32[192,1]{1,0:T(8,128)S(1)} %slice.656), channel_id=1, source_target_pairs={{0,1},{1,2},{2,3},{4,5},{5,6},{6,7},{8,9},{9,10},{10,11},{12,13},{... | collective-permute-start | bytes 2312 | tf_op jit(solution)/shard_map/ppermute | solution.py:18
  19.0 20.1 %collective-permute-start.5 = (f32[3,192,1]{1,2,0:T(1,128)S(1)}, f32[3,192,1]{1,2,0:T(1,128)S(1)}, u32[]{:S(2)}, u32[]{:S(2)}) collective-permute-start(f32[3,192,1]{1,2,0:T(1,128)S(1)} %pad_maximum_fusion.49), channel_id=1, source_target_pairs={{1,0},{2,1},{3,2},{5,4},{6,5},{7,6},{9,8},{10,9},{11,10},{13,12},{... | collective-permute-start | bytes 6920 | tf_op jit(solution)/shard_map/ppermute | solution.py:18
  37.1 13.2 %collective-permute-start.6 = (f32[192,1]{1,0:T(8,128)}, f32[192,1]{1,0:T(8,128)}, u32[]{:S(2)}, u32[]{:S(2)}) collective-permute-start(f32[192,1]{1,0:T(8,128)} %slice.850), channel_id=1, source_target_pairs={{1,0},{2,1},{3,2},{5,4},{6,5},{7,6},{9,8},{10,9},{11,10},{13,12},{... | collective-permute-start | bytes 2312 | tf_op jit(solution)/shard_map/ppermute | solution.py:18
  46.4 14.5 %collective-permute-start.4 = (f32[1,384]{1,0:T(1,128)S(1)}, f32[1,384]{1,0:T(1,128)S(1)}, u32[]{:S(2)}, u32[]{:S(2)}) collective-permute-start(f32[1,384]{1,0:T(1,128)S(1)} %slice.842), channel_id=1, source_target_pairs={{0,4},{4,8},{8,12},{1,5},{5,9},{9,13},{2,6},{6,10},{10,14},{3,7},{... | collective-permute-start | bytes 4616 | tf_op jit(solution)/shard_map/ppermute | solution.py:18
  71.3 10.5 %collective-permute-start.9 = (f32[1,384]{1,0:T(1,128)S(1)}, f32[1,384]{1,0:T(1,128)S(1)}, u32[]{:S(2)}, u32[]{:S(2)}) collective-permute-start(f32[1,384]{1,0:T(1,128)S(1)} %slice.858), channel_id=1, source_target_pairs={{0,4},{4,8},{8,12},{1,5},{5,9},{9,13},{2,6},{6,10},{10,14},{3,7},{... | collective-permute-start | bytes 4616 | tf_op jit(solution)/shard_map/ppermute | solution.py:18
  75.5 108.5 %collective-permute-start.49 = (f32[1,128]{1,0:T(1,128)}, f32[1,128]{1,0:T(1,128)}, u32[]{:S(2)}, u32[]{:S(2)}) collective-permute-start(f32[1,128]{1,0:T(1,128)} %get-tuple-element.59), channel_id=1, source_target_pairs={{0,4},{4,8},{8,12},{1,5},{5,9},{9,13},{2,6},{6,10},{10,14},{3,7},{... | collective-permute-start | bytes 1544 | tf_op jit(solution)/shard_map/ppermute | solution.py:18
  115.1 91.6 %collective-permute-start.51 = (f32[2,1,128]{2,1,0:T(1,128)S(1)}, f32[2,1,128]{2,1,0:T(1,128)}, u32[]{:S(2)}, u32[]{:S(2)}) collective-permute-start(f32[2,1,128]{2,1,0:T(1,128)S(1)} %pad_maximum_fusion.50), channel_id=1, source_target_pairs={{4,0},{8,4},{12,8},{5,1},{9,5},{13,9},{6,2},{10,6},{14,10},{7,3},{... | collective-permute-start | bytes 3080 | tf_op jit(solution)/shard_map/ppermute | solution.py:18
  141.9 51.9 %collective-permute-start.54 = (f32[2,64,1]{1,2,0:T(1,128)}, f32[2,64,1]{1,2,0:T(1,128)}, u32[]{:S(2)}, u32[]{:S(2)}) collective-permute-start(f32[2,64,1]{1,2,0:T(1,128)} %pad_maximum_fusion.51), channel_id=1, source_target_pairs={{1,0},{2,1},{3,2},{5,4},{6,5},{7,6},{9,8},{10,9},{11,10},{13,12},{... | collective-permute-start | bytes 1544 | tf_op jit(solution)/shard_map/ppermute | solution.py:18
  158.8 10.0 %collective-permute-start.28 = (f32[1,384]{1,0:T(1,128)S(1)}, f32[1,384]{1,0:T(1,128)S(1)}, u32[]{:S(2)}, u32[]{:S(2)}) collective-permute-start(f32[1,384]{1,0:T(1,128)S(1)} %slice.901), channel_id=1, source_target_pairs={{4,0},{8,4},{12,8},{5,1},{9,5},{13,9},{6,2},{10,6},{14,10},{7,3},{... | collective-permute-start | bytes 4616 | tf_op jit(solution)/shard_map/ppermute | solution.py:18
  166.8 15.4 %collective-permute-start.50 = (f32[64,1]{1,0:T(8,128)}, f32[64,1]{1,0:T(8,128)}, u32[]{:S(2)}, u32[]{:S(2)}) collective-permute-start(f32[64,1]{1,0:T(8,128)} %slice.784), channel_id=1, source_target_pairs={{0,1},{1,2},{2,3},{4,5},{5,6},{6,7},{8,9},{9,10},{10,11},{12,13},{... | collective-permute-start | bytes 776 | tf_op jit(solution)/shard_map/ppermute | solution.py:18
  189.4 12.2 %collective-permute-start.33 = (f32[1,384]{1,0:T(1,128)S(1)}, f32[1,384]{1,0:T(1,128)S(1)}, u32[]{:S(2)}, u32[]{:S(2)}) collective-permute-start(f32[1,384]{1,0:T(1,128)S(1)} %slice.912), channel_id=1, source_target_pairs={{0,4},{4,8},{8,12},{1,5},{5,9},{9,13},{2,6},{6,10},{10,14},{3,7},{... | collective-permute-start | bytes 4616 | tf_op jit(solution)/shard_map/ppermute | solution.py:18
  194.7 22.3 %collective-permute-start.52 = (f32[1,128]{1,0:T(1,128)S(1)}, f32[1,128]{1,0:T(1,128)S(1)}, u32[]{:S(2)}, u32[]{:S(2)}) collective-permute-start(f32[1,128]{1,0:T(1,128)S(1)} %slice.948), channel_id=1, source_target_pairs={{4,0},{8,4},{12,8},{5,1},{9,5},{13,9},{6,2},{10,6},{14,10},{7,3},{... | collective-permute-start | bytes 1544 | tf_op jit(solution)/shard_map/ppermute | solution.py:18
  196.0 21.0 %collective-permute-start.55 = (f32[64,1]{1,0:T(8,128)S(1)}, f32[64,1]{1,0:T(8,128)S(1)}, u32[]{:S(2)}, u32[]{:S(2)}) collective-permute-start(f32[64,1]{1,0:T(8,128)S(1)} %bitcast.129), channel_id=1, source_target_pairs={{1,0},{2,1},{3,2},{5,4},{6,5},{7,6},{9,8},{10,9},{11,10},{13,12},{... | collective-permute-start | bytes 776 | tf_op jit(solution)/shard_map/ppermute | solution.py:18
  212.0 17.5 %collective-permute-start.37 = (f32[1,384]{1,0:T(1,128)S(1)}, f32[1,384]{1,0:T(1,128)S(1)}, u32[]{:S(2)}, u32[]{:S(2)}) collective-permute-start(f32[1,384]{1,0:T(1,128)S(1)} %slice.921), channel_id=1, source_target_pairs={{0,4},{4,8},{8,12},{1,5},{5,9},{9,13},{2,6},{6,10},{10,14},{3,7},{... | collective-permute-start | bytes 4616 | tf_op jit(solution)/shard_map/ppermute | solution.py:18
  221.4 13.2 %collective-permute-start.53 = (f32[1,128]{1,0:T(1,128)S(1)}, f32[1,128]{1,0:T(1,128)S(1)}, u32[]{:S(2)}, u32[]{:S(2)}) collective-permute-start(f32[1,128]{1,0:T(1,128)S(1)} %slice.951), channel_id=1, source_target_pairs={{0,4},{4,8},{8,12},{1,5},{5,9},{9,13},{2,6},{6,10},{10,14},{3,7},{... | collective-permute-start | bytes 1544 | tf_op jit(solution)/shard_map/ppermute | solution.py:18
  240.0 15.3 %collective-permute-start.41 = (f32[1,384]{1,0:T(1,128)S(1)}, f32[1,384]{1,0:T(1,128)S(1)}, u32[]{:S(2)}, u32[]{:S(2)}) collective-permute-start(f32[1,384]{1,0:T(1,128)S(1)} %slice.930), channel_id=1, source_target_pairs={{0,4},{4,8},{8,12},{1,5},{5,9},{9,13},{2,6},{6,10},{10,14},{3,7},{... | collective-permute-start | bytes 4616 | tf_op jit(solution)/shard_map/ppermute | solution.py:18
  245.1 15.2 %collective-permute-start.58 = (f32[1,128]{1,0:T(1,128)S(1)}, f32[1,128]{1,0:T(1,128)S(1)}, u32[]{:S(2)}, u32[]{:S(2)}) collective-permute-start(f32[1,128]{1,0:T(1,128)S(1)} %slice.963), channel_id=1, source_target_pairs={{0,4},{4,8},{8,12},{1,5},{5,9},{9,13},{2,6},{6,10},{10,14},{3,7},{... | collective-permute-start | bytes 1544 | tf_op jit(solution)/shard_map/ppermute | solution.py:18
  248.5 11.8 %collective-permute-start.60 = (f32[64,1]{1,0:T(8,128)S(1)}, f32[64,1]{1,0:T(8,128)S(1)}, u32[]{:S(2)}, u32[]{:S(2)}) collective-permute-start(f32[64,1]{1,0:T(8,128)S(1)} %slice.967), channel_id=1, source_target_pairs={{0,1},{1,2},{2,3},{4,5},{5,6},{6,7},{8,9},{9,10},{10,11},{12,13},{... | collective-permute-start | bytes 776 | tf_op jit(solution)/shard_map/ppermute | solution.py:18
  265.7 14.6 %collective-permute-start.45 = (f32[1,384]{1,0:T(1,128)S(1)}, f32[1,384]{1,0:T(1,128)S(1)}, u32[]{:S(2)}, u32[]{:S(2)}) collective-permute-start(f32[1,384]{1,0:T(1,128)S(1)} %slice.939), channel_id=1, source_target_pairs={{0,4},{4,8},{8,12},{1,5},{5,9},{9,13},{2,6},{6,10},{10,14},{3,7},{... | collective-permute-start | bytes 4616 | tf_op jit(solution)/shard_map/ppermute | solution.py:18
  270.2 41.1 %collective-permute-start.62 = (f32[1,128]{1,0:T(1,128)S(1)}, f32[1,128]{1,0:T(1,128)S(1)}, u32[]{:S(2)}, u32[]{:S(2)}) collective-permute-start(f32[1,128]{1,0:T(1,128)S(1)} %slice.971), channel_id=1, source_target_pairs={{0,4},{4,8},{8,12},{1,5},{5,9},{9,13},{2,6},{6,10},{10,14},{3,7},{... | collective-permute-start | bytes 1544 | tf_op jit(solution)/shard_map/ppermute | solution.py:18
  273.6 37.6 %collective-permute-start.64 = (f32[64,1]{1,0:T(8,128)S(1)}, f32[64,1]{1,0:T(8,128)S(1)}, u32[]{:S(2)}, u32[]{:S(2)}) collective-permute-start(f32[64,1]{1,0:T(8,128)S(1)} %slice.975), channel_id=1, source_target_pairs={{0,1},{1,2},{2,3},{4,5},{5,6},{6,7},{8,9},{9,10},{10,11},{12,13},{... | collective-permute-start | bytes 776 | tf_op jit(solution)/shard_map/ppermute | solution.py:18
  295.6 13.4 %collective-permute-start.67 = (f32[1,384]{1,0:T(1,128)S(1)}, f32[1,384]{1,0:T(1,128)S(1)}, u32[]{:S(2)}, u32[]{:S(2)}) collective-permute-start(f32[1,384]{1,0:T(1,128)S(1)} %slice.982), channel_id=1, source_target_pairs={{4,0},{8,4},{12,8},{5,1},{9,5},{13,9},{6,2},{10,6},{14,10},{7,3},{... | collective-permute-start | bytes 4616 | tf_op jit(solution)/shard_map/ppermute | solution.py:18
  297.0 12.0 %collective-permute-start.68 = (f32[192,1]{1,0:T(8,128)S(1)}, f32[192,1]{1,0:T(8,128)}, u32[]{:S(2)}, u32[]{:S(2)}) collective-permute-start(f32[192,1]{1,0:T(8,128)S(1)} %slice.985), channel_id=1, source_target_pairs={{1,0},{2,1},{3,2},{5,4},{6,5},{7,6},{9,8},{10,9},{11,10},{13,12},{... | collective-permute-start | bytes 2312 | tf_op jit(solution)/shard_map/ppermute | solution.py:18
  (62 other events, 991.6 us)
where the time goes:
time: 324 us; the launch traced here: 320 us
  starting transfers between devices  175 us (54%)
  other arithmetic  54.1 us (17%)
  waiting for transfers between devices  51 us (16%)
  local copies, waits for them, and re-layouts  35 us (11%)
  between operations  5.28 us (2%)
    ppermute x69, starting transfers between devices, shifted(): lax.ppermute(value, axis, [(source, source + steps) for source in range(i...  175 us
    ppermute x69, waiting for transfers between devices, shifted(): lax.ppermute(value, axis, [(source, source + steps) for source in range(i...  51 us
    div x17, other arithmetic, momentum(): return openness * (flux - COURANT * total * (eta_next - eta)) / drag  27.7 us
    reshape x1, local copies, waits for them, and re-layouts, shards(): means = jnp.mean(feta.reshape(rows, R, cols, R), axis=(1, 3))  13.4 us
    add x2, other arithmetic, friction_of(): result + jnp.where(classes == level_id, table[level_id], jnp.float32(0.0))  8.47 us
  transfers between devices with their start and end apart: 69, of which 23 were waited for; matrix products, arithmetic and copies ran while one was open for 27% of the time, Pallas kernels for 0%

commit v1 on v0

v1 whole, which is shorter than its diff:
```python
import functools

import jax
import jax.numpy as jnp
from jax import lax
from jax.experimental import pallas as pl
from jax.experimental.pallas import tpu as pltpu
from jax.sharding import PartitionSpec as P

R = 3
ITERS = 4
FSTEPS = R * ITERS
COURANT = 0.45
FLOOR = 0.25
SA = COURANT**2 / 2
SB = COURANT**3 / 2
POWER = -7.0 / 3.0
TFLOOR = 2 * SA * FLOOR
KSCALE = 0.5 * COURANT * (2 * SA) ** (7.0 / 3.0) / SB
CLOSED = 3.0e38
LANES = 128
HALO = 16
OLANE = 6 * 16
VMEM = pl.BlockSpec(memory_space=pltpu.VMEM)
SMEM = pl.BlockSpec(memory_space=pltpu.SMEM)
F32 = jnp.float32


def swap_even(value, axis):
    count = lax.axis_size(axis)
    return lax.ppermute(value, axis, [(i, i ^ 1) for i in range(count) if i ^ 1 < count])


def swap_odd(value, axis):
    count = lax.axis_size(axis)
    pairs = [(i, ((i + 1) ^ 1) - 1) for i in range(1, count)]
    return lax.ppermute(value, axis, [(a, b) for a, b in pairs if b < count])


def friction(classes, table):
    result = jnp.full(classes.shape, table[0], F32)
    for level_id in range(1, table.shape[0]):
        result = jnp.where(classes == level_id, table[level_id], result)
    return result


def fine_fields(refs, rows, cols, table):
    eta, qx, qy, depth, wet, classes = refs
    return (
        eta[rows, cols] * SA,
        qx[rows, cols] * SB,
        qy[rows, cols] * SB,
        depth[rows, cols] * SA,
        friction(classes[rows, cols], table),
        wet[rows, cols].astype(F32),
    )


def ocean_fields(refs, rows, cols, table):
    eta, mx, ny, depth, classes = refs
    return (
        eta[rows, cols] * SA,
        mx[rows, cols] * SB,
        ny[rows, cols] * SB,
        depth[rows, cols] * SA,
        friction(classes[rows, cols], table),
    )


def roll_to(value, start, target):
    return pltpu.roll(value, (target - start) % LANES, 1)


def pack_columns_kernel(fine_cols, *refs):
    table, fine, ocean, (even_out, odd_out) = refs[0], refs[1:7], refs[7:12], refs[12:14]
    rows, cols = fine[0].shape
    ocean_rows = ocean[0].shape[0]
    lane = lax.broadcasted_iota(jnp.int32, (8, LANES), 1)
    is_even = lax.rem(lax.axis_index("gy"), 2) == 0
    for r in range(rows // 8):
        row = pl.ds(8 * r, 8)
        west = jnp.zeros((8, LANES), F32)
        east = jnp.zeros((8, LANES), F32)
        if 8 * r < ocean_rows:
            for j, value in enumerate(ocean_fields(ocean, row, pl.ds(0, LANES), table)):
                west = jnp.where(lane >= OLANE + 4 * j, roll_to(value, 0, OLANE + 4 * j), west)
                east = jnp.where(lane >= OLANE + 4 * j, roll_to(value, LANES - 4, OLANE + 4 * j), east)
        first = fine_fields(fine, row, pl.ds(0, LANES), table)
        last = fine_fields(fine, row, pl.ds(cols - LANES, LANES), table)
        for f in range(5, -1, -1):
            west = jnp.where(lane < 16 * f + 16, roll_to(first[f], 0, 16 * f), west)
            east = jnp.where(lane < 16 * f + 16, roll_to(last[f], LANES - 16, 16 * f), east)
        even_out[row, :] = jnp.where(is_even, east, west)
        odd_out[row, :] = jnp.where(is_even, west, east)


def pack_rows_kernel(pairs_only, *refs):
    table, fine, ocean, (gy_even, gy_odd) = refs[0], refs[1:7], refs[7:12], refs[12:14]
    even_out, odd_out = refs[14:16]
    rows, cols = fine[0].shape
    tiles = cols // LANES
    ocean_rows = ocean[0].shape[0]
    is_even = lax.rem(lax.axis_index("gx"), 2) == 0
    fine_rows = (6 * tiles + 2) * HALO

    def choose(base, with_fine, out, low):
        at = 0
        if with_fine:
            for f_tile in range(tiles):
                cols_at = pl.ds(f_tile * LANES, LANES)
                for half in range(HALO // 8):
                    top = fine_fields(fine, pl.ds(8 * half, 8), cols_at, table)
                    bottom = fine_fields(fine, pl.ds(rows - HALO + 8 * half, 8), cols_at, table)
                    for f in range(6):
                        place = (f * tiles + f_tile) * HALO + 8 * half
                        out[pl.ds(place, 8), :] = jnp.where(low, bottom[f], top[f])
            for k, src in enumerate((gy_even, gy_odd)):
                for half in range(HALO // 8):
                    place = (6 * tiles + k) * HALO + 8 * half
                    out[pl.ds(place, 8), :] = jnp.where(
                        low, src[pl.ds(rows - HALO + 8 * half, 8), :], src[pl.ds(8 * half, 8), :]
                    )
            at = fine_rows
        top = ocean_fields(ocean, pl.ds(0, 8), pl.ds(0, LANES), table)
        bottom = ocean_fields(ocean, pl.ds(ocean_rows - 8, 8), pl.ds(0, LANES), table)
        for j in range(5):
            out[pl.ds(at + 8 * j, 8), :] = jnp.where(low, bottom[j], top[j])
        for k, src in enumerate((gy_even, gy_odd)):
            out[pl.ds(at + 8 * (5 + k), 8), :] = jnp.where(
                low, src[pl.ds(ocean_rows - 8, 8), :], src[pl.ds(0, 8), :]
            )

    choose(0, True, even_out, is_even)
    choose(0, not pairs_only, odd_out, jnp.logical_not(is_even))


def lane_next(values):
    lane = lax.broadcasted_iota(jnp.int32, values[0].shape, 1)
    rolled = [pltpu.roll(v, LANES - 1, 1) for v in values]
    if len(values) == 1:
        return rolled
    return [jnp.where(lane == LANES - 1, rolled[(t + 1) % len(values)], rolled[t]) for t in range(len(values))]


def lane_prev(values):
    lane = lax.broadcasted_iota(jnp.int32, values[0].shape, 1)
    rolled = [pltpu.roll(v, 1, 1) for v in values]
    if len(values) == 1:
        return rolled
    return [jnp.where(lane == 0, rolled[t - 1], rolled[t]) for t in range(len(values))]


def new_flux(flux, eta, eta_next, wet, wet_next, opened, drag):
    total = wet + wet_next
    power = jnp.exp2(POWER * jnp.log2(jnp.maximum(total, TFLOOR)))
    denom = opened + (drag * jnp.abs(flux)) * power
    return (flux - total * (eta_next - eta)) / denom


def prepare_faces(tiles, n, kf, wf, kx, ky, ox, oy, open_x=None, open_y=None):
    for t in range(tiles):
        wrap = pl.ds(8 + 8 * n, 8)
        kf[t, wrap, :] = kf[t, pl.ds(8, 8), :]
        if wf is not None:
            wf[t, wrap, :] = wf[t, pl.ds(8, 8), :]
    for r in range(n):
        here, after = pl.ds(8 + 8 * r, 8), pl.ds(9 + 8 * r, 8)
        k = [kf[t, here, :] for t in range(tiles)]
        k_next = lane_next(k)
        if wf is not None:
            w = [wf[t, here, :] for t in range(tiles)]
            w_next = lane_next(w)
        for t in range(tiles):
            kx[t, here, :] = KSCALE * (k[t] + kf[t, after, :])
            ky[t, here, :] = KSCALE * (k[t] + k_next[t])
            if wf is not None:
                ox[t, here, :] = jnp.where(w[t] * wf[t, after, :] > 0.5, 1.0, CLOSED)
                oy[t, here, :] = jnp.where(w[t] * w_next[t] > 0.5, 1.0, CLOSED)


def level_pass(tiles, n, e, g, x, y, d):
    for r in range(n):
        here, before = pl.ds(8 + 8 * r, 8), pl.ds(7 + 8 * r, 8)
        south = [y[t, here, :] for t in range(tiles)]
        south_prev = lane_prev(south)
        for t in range(tiles):
            flow = (x[t, here, :] - x[t, before, :]) + (south[t] - south_prev[t])
            eta = e[t, here, :] - flow
            wet = jnp.maximum(d[t, here, :] + eta, 0.0)
            e[t, here, :] = eta
            g[t, here, :] = wet
            if r == 0:
                e[t, pl.ds(8 + 8 * n, 8), :] = eta
                g[t, pl.ds(8 + 8 * n, 8), :] = wet


def flux_pass(tiles, n, e, g, x, y, kx, ky, ox, oy, fix):
    for r in range(n):
        here, after = pl.ds(8 + 8 * r, 8), pl.ds(9 + 8 * r, 8)
        eta = [e[t, here, :] for t in range(tiles)]
        wet = [g[t, here, :] for t in range(tiles)]
        eta_next, wet_next = lane_next(eta), lane_next(wet)
        for t in range(tiles):
            fx = new_flux(
                x[t, here, :], eta[t], e[t, after, :], wet[t], g[t, after, :], ox[t, here, :], kx[t, here, :]
            )
            fx = fix(r, t, fx)
            x[t, here, :] = fx
            if r == n - 1:
                x[t, pl.ds(0, 8), :] = fx
            y[t, here, :] = new_flux(
                y[t, here, :], eta[t], eta_next[t], wet[t], wet_next[t], oy[t, here, :], ky[t, here, :]
            )


def dot(a, b):
    return lax.dot_general(
        a, b, (((1,), (0,)), ((), ())), precision=lax.Precision.HIGHEST, preferred_element_type=F32
    )


def iota(shape, dim):
    return lax.broadcasted_iota(jnp.int32, shape, dim)


def place_of(block_size):
    gx = lax.axis_index("gx")
    slot = lax.rem(gx, block_size)
    return gx, lax.div(gx, block_size), slot == 0, slot == block_size - 1


def fine_kernel(block_size, *refs):
    table, offsets, fine, ocean_mx = refs[0], refs[1], refs[2:8], refs[8]
    gy_even, gy_odd, gx_even, gx_odd = refs[9:13]
    out_eta, out_x, out_y, out_means = refs[13:17]
    e, g, x, y, d, kf, wf, kx, ky, ox, oy, edges = refs[17:29]
    rows, cols = fine[0].shape
    own = cols // LANES
    tiles = own + 1
    pairs_only = block_size == 2
    n = rows // 8 + (HALO // 8) * (1 if pairs_only else 2)
    gx, grid, first, last = place_of(block_size)
    gx_is_even = lax.rem(gx, 2) == 0
    gy_is_even = lax.rem(lax.axis_index("gy"), 2) == 0
    lane = iota((8, LANES), 1)
    sub = iota((8, LANES), 0)

    def unpack(from_even, from_odd, f):
        from_east = jnp.where(gy_is_even, from_even, from_odd)
        from_west = jnp.where(gy_is_even, from_odd, from_even)
        east = roll_to(from_east, 16 * f, 0)
        west = roll_to(from_west, 16 * f, LANES - 16)
        return jnp.where(lane < 16, east, jnp.where(lane >= LANES - 16, west, 0.0))

    dest = (e, x, y, d, kf, wf)
    for r in range(rows // 8):
        src, here = pl.ds(8 * r, 8), pl.ds(8 + 8 * r, 8)
        for t in range(own):
            for f, value in enumerate(fine_fields(fine, src, pl.ds(t * LANES, LANES), table)):
                dest[f][t, here, :] = value
        for f in range(6):
            dest[f][own, here, :] = unpack(gy_even[src, :], gy_odd[src, :], f)

    def halo_rows(messages, base):
        for half in range(HALO // 8):
            here = pl.ds(8 + base + 8 * half, 8)

            def take(block):
                picked = [m[pl.ds(block * HALO + 8 * half, 8), :] for m in messages]
                return picked[0] if len(picked) == 1 else jnp.where(gx_is_even, picked[0], picked[1])

            for f in range(6):
                for t in range(own):
                    dest[f][t, here, :] = take(f * own + t)
                dest[f][own, here, :] = unpack(take(6 * own), take(6 * own + 1), f)

    if pairs_only:
        halo_rows([gx_even], rows)
    else:
        halo_rows([gx_even, gx_odd], rows)
        halo_rows([gx_odd, gx_even], rows + HALO)

    ocean_rows = ocean_mx.shape[0]
    own_offset = offsets[grid]
    at = own_offset - 1
    mx_own = ocean_mx[...] * SB
    from_east = jnp.where(gy_is_even, gy_even[0:ocean_rows, :], gy_odd[0:ocean_rows, :])
    from_west = jnp.where(gy_is_even, gy_odd[0:ocean_rows, :], gy_even[0:ocean_rows, :])
    lanes = iota((ocean_rows, LANES), 1)
    mx_halo = jnp.where(
        lanes < 4, roll_to(from_east, OLANE + 4, 0), roll_to(from_west, OLANE + 4, LANES - 4)
    )
    picks = iota((8, ocean_rows), 1) == jnp.where(iota((8, ocean_rows), 0) == 0, at, ocean_rows - 1)
    picks = picks.astype(F32)
    source = jnp.concatenate([dot(picks, mx_own), dot(picks, mx_halo)], 1)
    fine_lane = iota((2 * LANES, tiles * LANES), 1)
    ocean_lane = iota((2 * LANES, tiles * LANES), 0)
    width = own * LANES
    wanted = jnp.where(
        fine_lane < width + 64,
        lax.div(fine_lane, R),
        2 * LANES - 1 - lax.div(tiles * LANES - 1 - fine_lane, R),
    )
    spread = dot(source, (ocean_lane == wanted).astype(F32))
    for t in range(tiles):
        cut = spread[:, t * LANES : (t + 1) * LANES]
        wet_first = wf[t, pl.ds(8, 8), :]
        wet_last = wf[t, pl.ds(8 + rows - 8, 8), :]
        edges[0, t, :, :] = jnp.broadcast_to(cut[0:1, :] * wet_first[0:1, :], (8, LANES))
        edges[1, t, :, :] = jnp.broadcast_to(cut[1:2, :] * wet_last[7:8, :], (8, LANES))

    prepare_faces(tiles, n, kf, wf, kx, ky, ox, oy)

    west_mask = (sub == 7) & first
    east_mask = (sub == 7) & last

    def fix(r, t, fx):
        if r == rows // 8 - 1:
            fx = jnp.where(east_mask, edges[1, t, :, :], fx)
        if r == n - 1:
            fx = jnp.where(west_mask, edges[0, t, :, :], fx)
        return fx

    for t in range(tiles):
        start = jnp.where(west_mask, edges[0, t, :, :], x[t, pl.ds(8 * n, 8), :])
        x[t, pl.ds(0, 8), :] = start

    def step(_, carry):
        level_pass(tiles, n, e, g, x, y, d)
        flux_pass(tiles, n, e, g, x, y, kx, ky, ox, oy, fix)
        return carry

    lax.fori_loop(0, FSTEPS, step, 0)

    for r in range(rows // 8):
        to, here = pl.ds(8 * r, 8), pl.ds(8 + 8 * r, 8)
        for t in range(own):
            at_cols = pl.ds(t * LANES, LANES)
            out_eta[to, at_cols] = e[t, here, :] * (1.0 / SA)
            out_x[to, at_cols] = x[t, here, :] * (1.0 / SB)
            out_y[to, at_cols] = y[t, here, :] * (1.0 / SB)

    coarse_row = lax.rem(lax.div(iota((ocean_rows, rows), 1), R) + own_offset, ocean_rows)
    gather_rows = (coarse_row == iota((ocean_rows, rows), 0)).astype(F32)
    gather_cols = (lax.div(iota((cols, LANES), 0), R) == iota((cols, LANES), 1)).astype(F32)
    out_means[...] = dot(dot(gather_rows, out_eta[...]), gather_cols) * (1.0 / (R * R))


def ocean_kernel(pairs_only, *refs):
    table, ocean = refs[0], refs[1:6]
    gy_even, gy_odd, gx_even, gx_odd = refs[6:10]
    out_eta, out_x, out_y = refs[10:13]
    e, g, x, y, d, kf, kx, ky, ox, oy = refs[13:23]
    rows, cols = ocean[0].shape
    tiles = 2
    n = rows // 8 + 1
    gx, gy = lax.axis_index("gx"), lax.axis_index("gy")
    gx_is_even = lax.rem(gx, 2) == 0
    gy_is_even = lax.rem(gy, 2) == 0
    lane = iota((8, LANES), 1)
    sub = iota((8, LANES), 0)

    def unpack(from_even, from_odd, j):
        from_east = jnp.where(gy_is_even, from_even, from_odd)
        from_west = jnp.where(gy_is_even, from_odd, from_even)
        east = roll_to(from_east, OLANE + 4 * j, 0)
        west = roll_to(from_west, OLANE + 4 * j, LANES - 4)
        return jnp.where(lane < 4, east, jnp.where(lane >= LANES - 4, west, 0.0))

    dest = (e, x, y, d, kf)
    for r in range(rows // 8):
        src, here = pl.ds(8 * r, 8), pl.ds(8 + 8 * r, 8)
        for j, value in enumerate(ocean_fields(ocean, src, pl.ds(0, LANES), table)):
            dest[j][0, here, :] = value
            dest[j][1, here, :] = unpack(gy_even[src, :], gy_odd[src, :], j)

    def take(block):
        start_even = gx_even.shape[0] - 56
        start_odd = gx_odd.shape[0] - 56
        first = gx_even[pl.ds(start_even + 8 * block, 8), :]
        second = gx_odd[pl.ds(start_odd + 8 * block, 8), :]
        after = jnp.where(gx_is_even, first, second)
        before = jnp.where(gx_is_even, second, first)
        return jnp.where(sub < 4, after, before)

    here = pl.ds(8 + rows, 8)
    for j in range(5):
        dest[j][0, here, :] = take(j)
        dest[j][1, here, :] = unpack(take(5), take(6), j)

    prepare_faces(tiles, n, kf, None, kx, ky, None, None)
    rows_total, cols_total = rows * lax.axis_size("gx"), cols * lax.axis_size("gy")
    for r in range(n):
        here = pl.ds(8 + 8 * r, 8)
        row = sub + 8 * r
        row = jnp.where(row >= rows + 4, row - (rows + 8), row) + gx * rows
        for t in range(tiles):
            col = lane if t == 0 else jnp.where(lane < 64, lane + LANES, lane - LANES)
            col = col + gy * cols
            ox[t, here, :] = jnp.where((row >= 0) & (row < rows_total - 1), 1.0, CLOSED)
            oy[t, here, :] = jnp.where((col >= 0) & (col < cols_total - 1), 1.0, CLOSED)
    for t in range(tiles):
        x[t, pl.ds(0, 8), :] = x[t, pl.ds(8 * n, 8), :]

    def step(_, carry):
        level_pass(tiles, n, e, g, x, y, d)
        flux_pass(tiles, n, e, g, x, y, kx, ky, ox, oy, lambda r, t, fx: fx)
        return carry

    lax.fori_loop(0, ITERS, step, 0)
    for r in range(rows // 8):
        to, here = pl.ds(8 * r, 8), pl.ds(8 + 8 * r, 8)
        out_eta[to, :] = e[0, here, :] * (1.0 / SA)
        out_x[to, :] = x[0, here, :] * (1.0 / SB)
        out_y[to, :] = y[0, here, :] * (1.0 / SB)


def paste_kernel(block_size, *refs):
    offsets, eta, rolled, arrived, out = refs
    gx, grid, _, _ = place_of(block_size)
    own_offset = offsets[grid]
    left_offset = jnp.where(gx >= 1, offsets[lax.div(jnp.maximum(gx - 1, 0), block_size)], 0)
    row = iota(eta.shape, 0)
    out[...] = jnp.where(
        row >= own_offset, rolled[...], jnp.where(row < left_offset, arrived[...], eta[...])
    )


def shape(*dims):
    return jax.ShapeDtypeStruct(dims, F32)


def params():
    return pltpu.CompilerParams(vmem_limit_bytes=48 * 1024 * 1024)


def cost(ops, size):
    return pl.CostEstimate(flops=ops, bytes_accessed=size, transcendentals=0)


def shards(
    ocean_eta,
    ocean_mx,
    ocean_ny,
    ocean_depth,
    ocean_class,
    manning,
    fine_eta,
    fine_qx,
    fine_qy,
    fine_depth,
    fine_wet,
    fine_class,
    fine_offset,
):
    ocean_rows, ocean_cols = ocean_eta.shape
    rows, cols = fine_eta.shape
    own = cols // LANES
    gx_count = lax.axis_size("gx")
    block_size = min(16, gx_count // 2)
    pairs_only = block_size == 2
    fine = (fine_eta, fine_qx, fine_qy, fine_depth, fine_wet, fine_class)
    ocean = (ocean_eta, ocean_mx, ocean_ny, ocean_depth, ocean_class)

    gy_even, gy_odd = pl.pallas_call(
        functools.partial(pack_columns_kernel, cols),
        out_shape=(shape(rows, LANES), shape(rows, LANES)),
        in_specs=[SMEM] + [VMEM] * 11,
        out_specs=(VMEM, VMEM),
        compiler_params=params(),
        name="pack_columns",
    )(manning, *fine, *ocean)
    gy_even = swap_even(gy_even, "gy")
    gy_odd = swap_odd(gy_odd, "gy")

    fine_rows = (6 * own + 2) * HALO
    gx_even, gx_odd = pl.pallas_call(
        functools.partial(pack_rows_kernel, pairs_only),
        out_shape=(shape(fine_rows + 56, LANES), shape(56 + (0 if pairs_only else fine_rows), LANES)),
        in_specs=[SMEM] + [VMEM] * 13,
        out_specs=(VMEM, VMEM),
        compiler_params=params(),
        name="pack_rows",
    )(manning, *fine, *ocean, gy_even, gy_odd)
    gx_even = swap_even(gx_even, "gx")
    gx_odd = swap_odd(gx_odd, "gx")

    n = rows // 8 + (HALO // 8) * (1 if pairs_only else 2)
    tiles = own + 1
    scratch = [pltpu.VMEM((tiles, 8 * n + 16, LANES), F32)] * 11 + [pltpu.VMEM((2, tiles, 8, LANES), F32)]
    feta, fqx, fqy, rolled = pl.pallas_call(
        functools.partial(fine_kernel, block_size),
        out_shape=(shape(rows, cols),) * 3 + (shape(ocean_rows, ocean_cols),),
        in_specs=[SMEM, SMEM] + [VMEM] * 11,
        out_specs=(VMEM,) * 4,
        scratch_shapes=scratch,
        compiler_params=params(),
        name="coastal",
    )(manning, fine_offset, *fine, ocean_mx, gy_even, gy_odd, gx_even, gx_odd)
    arrived = lax.ppermute(rolled, "gx", [(i, i + 1) for i in range(gx_count - 1)])

    n = ocean_rows // 8 + 1
    eta, mx, ny = pl.pallas_call(
        functools.partial(ocean_kernel, pairs_only),
        out_shape=(shape(ocean_rows, ocean_cols),) * 3,
        in_specs=[SMEM] + [VMEM] * 9,
        out_specs=(VMEM,) * 3,
        scratch_shapes=[pltpu.VMEM((2, 8 * n + 16, LANES), F32)] * 10,
        compiler_params=params(),
        name="ocean",
    )(manning, *ocean, gy_even, gy_odd, gx_even, gx_odd)

    eta = pl.pallas_call(
        functools.partial(paste_kernel, block_size),
        out_shape=shape(ocean_rows, ocean_cols),
        in_specs=[SMEM] + [VMEM] * 3,
        out_specs=VMEM,
        compiler_params=params(),
        name="paste",
    )(fine_offset, eta, rolled, arrived)
    return (eta, mx, ny, feta, fqx, fqy)


def solution(mesh):
    tile = P(("scen", "gx"), "gy")
    in_specs = (tile,) * 5 + (P(),) + (tile,) * 6 + (P("scen"),)
    return jax.shard_map(shards, mesh=mesh, in_specs=in_specs, out_specs=(tile,) * 6, check_vma=False)
```

time: 324 us -> 44.8 us (0.14)
  starting transfers between devices: 175 us -> 12.2 us
  other arithmetic: 54.1 us -> 0 us
  waiting for transfers between devices: 51 us -> 4.79 us
  local copies, waits for them, and re-layouts: 35 us -> 10.2 us
  Pallas kernels: 0 us -> 15.9 us
  between operations: 5.28 us -> 0.75 us
    ppermute x69 -> x5, starting transfers between devices: 175 us -> 12.2 us  [the longest x2 5.26 us: swap_odd(): return lax.ppermute(value, axis, [(a, b) for a, b in pairs if b < count])]
    ppermute x69 -> x5, waiting for transfers between devices: 51 us -> 4.79 us  [the longest x2 2.57 us: swap_odd(): return lax.ppermute(value, axis, [(a, b) for a, b in pairs if b < count])]
    div x18 -> x0, other arithmetic: 27.7 us -> none  [the longest x17 27.7 us: momentum(): return openness * (flux - COURANT * total * (eta_next - eta)) / drag]
    slice x108 -> x0, local copies, waits for them, and re-layouts: 17.1 us -> none  [the longest x16 2.64 us: flows(): eta_n1 = jnp.concatenate([eta[:, 1:], east_cols[0]], 1)]
    pallas_call x0 -> x5, Pallas kernels: none -> 15.9 us  [the longest x1 11 us: shards(): pl.pallas_call(functools.partial(fine_kernel, block_size), out_shape=(sha...]
    reshape x1 -> x0, local copies, waits for them, and re-layouts: 13.4 us -> none  [shards(): means = jnp.mean(feta.reshape(rows, R, cols, R), axis=(1, 3))]
    unnamed x34, local copies, waits for them, and re-layouts: 0.72 us -> 10.2 us
    add x2 -> x0, other arithmetic: 8.47 us -> none  [friction_of(): result + jnp.where(classes == level_id, table[level_id], jnp.float32(0.0))]
  transfers between devices with their start and end apart: 69 -> 5, of which waited for: 23 -> 2; matrix products, arithmetic and copies ran while one was open for 27% -> 0% of each run, Pallas kernels for 0% -> 5%
where the time goes in v1:
time: 44.8 us; the launch traced here: 43.9 us
  Pallas kernels  15.9 us (35%)
  starting transfers between devices  12.2 us (27%)
  local copies, waits for them, and re-layouts  10.2 us (23%)
  waiting for transfers between devices  4.79 us (11%)
  between operations  0.75 us (2%)
    pallas_call x1, Pallas kernels, shards(): pl.pallas_call(functools.partial(fine_kernel, block_size), out_shape=(sha...  11 us
    unnamed x34, local copies, waits for them, and re-layouts  10.2 us
    ppermute x2, starting transfers between devices, swap_odd(): return lax.ppermute(value, axis, [(a, b) for a, b in pairs if b < count])  5.26 us
    ppermute x1, starting transfers between devices, shards(): lax.ppermute(rolled, 'gx', [(i, i + 1) for i in range(gx_count - 1)])  4.76 us
    ppermute x2, waiting for transfers between devices, swap_odd(): return lax.ppermute(value, axis, [(a, b) for a, b in pairs if b < count])  2.57 us
    ppermute x2, starting transfers between devices, swap_even(): lax.ppermute(value, axis, [(i, i ^ 1) for i in range(count) if i ^ 1 < co...  2.22 us
    ppermute x2, waiting for transfers between devices, swap_even(): lax.ppermute(value, axis, [(i, i ^ 1) for i in range(count) if i ^ 1 < co...  2.21 us
    pallas_call x1, Pallas kernels, shards(): pl.pallas_call(functools.partial(ocean_kernel, pairs_only), out_shape=(sh...  2.2 us
  transfers between devices with their start and end apart: 5, of which 2 were waited for; matrix products, arithmetic and copies ran while one was open for 0% of the time, Pallas kernels for 5%

profile of v1, /device:TPU:1, one launch (start us, length us, event | category | flops | bytes accessed | tf_op | source)
XLA Modules:
  0.0 43.9 jit_solution(2489159116939061973)
XLA Ops:
  0.6 1.0 %copy-done = f32[192,384]{1,0:T(8,128)S(1)} copy-done((f32[192,384]{1,0:T(8,128)S(1)}, f32[192,384]{1,0:T(8,128)}, u32[]{:S(2)}) %copy-start) | copy-done | bytes 294936
  1.6 1.0 %copy-done.1 = f32[192,384]{1,0:T(8,128)S(1)} copy-done((f32[192,384]{1,0:T(8,128)S(1)}, f32[192,384]{1,0:T(8,128)}, u32[]{:S(2)}) %copy-start.1) | copy-done | bytes 294936
  2.6 1.0 %copy-done.2 = f32[192,384]{1,0:T(8,128)S(1)} copy-done((f32[192,384]{1,0:T(8,128)S(1)}, f32[192,384]{1,0:T(8,128)}, u32[]{:S(2)}) %copy-start.2) | copy-done | bytes 294936
  3.5 1.0 %copy-done.3 = f32[192,384]{1,0:T(8,128)S(1)} copy-done((f32[192,384]{1,0:T(8,128)S(1)}, f32[192,384]{1,0:T(8,128)}, u32[]{:S(2)}) %copy-start.3) | copy-done | bytes 294936
  4.5 1.0 %copy-done.4 = s32[192,384]{1,0:T(8,128)S(1)} copy-done((s32[192,384]{1,0:T(8,128)S(1)}, s32[192,384]{1,0:T(8,128)}, u32[]{:S(2)}) %copy-start.4) | copy-done | bytes 294936
  5.4 1.0 %copy-done.5 = s32[192,384]{1,0:T(8,128)S(1)} copy-done((s32[192,384]{1,0:T(8,128)S(1)}, s32[192,384]{1,0:T(8,128)}, u32[]{:S(2)}) %copy-start.5) | copy-done | bytes 294936
  6.4 0.8 %copy-done.6 = f32[64,128]{1,0:T(8,128)S(1)} copy-done((f32[64,128]{1,0:T(8,128)S(1)}, f32[64,128]{1,0:T(8,128)}, u32[]{:S(2)}) %copy-start.6) | copy-done | bytes 32792
  7.2 0.8 %copy-done.8 = f32[64,128]{1,0:T(8,128)S(1)} copy-done((f32[64,128]{1,0:T(8,128)S(1)}, f32[64,128]{1,0:T(8,128)}, u32[]{:S(2)}) %copy-start.8) | copy-done | bytes 32792
  7.9 0.8 %copy-done.9 = f32[64,128]{1,0:T(8,128)S(1)} copy-done((f32[64,128]{1,0:T(8,128)S(1)}, f32[64,128]{1,0:T(8,128)}, u32[]{:S(2)}) %copy-start.9) | copy-done | bytes 32792
  8.7 0.8 %copy-done.11 = f32[64,128]{1,0:T(8,128)S(1)} copy-done((f32[64,128]{1,0:T(8,128)S(1)}, f32[64,128]{1,0:T(8,128)}, u32[]{:S(2)}) %copy-start.11) | copy-done | bytes 32792
  9.4 0.8 %copy-done.13 = s32[64,128]{1,0:T(8,128)S(1)} copy-done((s32[64,128]{1,0:T(8,128)S(1)}, s32[64,128]{1,0:T(8,128)}, u32[]{:S(2)}) %copy-start.13) | copy-done | bytes 32792
  10.2 0.7 %copy-done.15 = f32[6]{0:T(128)S(1)} copy-done((f32[6]{0:T(128)S(1)}, f32[6]{0:T(128)}, u32[]{:S(2)}) %copy-start.15) | copy-done | bytes 48
  10.9 1.0 %pack_columns.1 = (f32[192,128]{1,0:T(8,128)S(1)}, f32[192,128]{1,0:T(8,128)S(1)}) custom-call(f32[6]{0:T(128)S(1)} %copy-done.15, f32[192,384]{1,0:T(8,128)S(1)} %copy-done, f32[192,384]{1,0:T(8,128)S(1)} %copy-done.1, f32[192,384]{1,0:T(8,128)S(1)} %copy-done.2, f32[192,384]{1,0:T(8,128)S(1)} %copy-done.3, s32[192,384]{1,0:T(8,128)S(1)} %copy-done.4, ...), custom_call_target="tpu_custom_call" | custom-call | tf_op jit(solution)/shard_map/pack_columns/pallas_call | solution.py:465
  11.8 0.1 collective-permute-start
  12.0 4.5 %collective-permute-start.1 = (f32[192,128]{1,0:T(8,128)S(1)}, f32[192,128]{1,0:T(8,128)S(1)}, u32[]{:S(2)}, u32[]{:S(2)}) collective-permute-start(f32[192,128]{1,0:T(8,128)S(1)} %get-tuple-element.18), channel_id=1, source_target_pairs={{1,2},{2,1},{5,6},{6,5},{9,10},{10,9},{13,14},{14,13},{17,18},{18,... | collective-permute-start | bytes 294920 | tf_op jit(solution)/shard_map/ppermute | solution.py:37
  16.4 2.6 %collective-permute-done.1.refs_13_.refs_7_.refs_10_ = f32[192,128]{1,0:T(8,128)S(1)} collective-permute-done((f32[192,128]{1,0:T(8,128)S(1)}, f32[192,128]{1,0:T(8,128)S(1)}, u32[]{:S(2)}, u32[]{:S(2)}) %collective-permute-start.1) | collective-permute-done | bytes 98336 | tf_op jit(solution)/shard_map/ppermute | solution.py:37
  19.0 0.6 %pack_rows.1 = (f32[376,128]{1,0:T(8,128)S(1)}, f32[56,128]{1,0:T(8,128)S(1)}) custom-call(f32[6]{0:T(128)S(1)} %copy-done.15, f32[192,384]{1,0:T(8,128)S(1)} %copy-done, f32[192,384]{1,0:T(8,128)S(1)} %copy-done.1, f32[192,384]{1,0:T(8,128)S(1)} %copy-done.2, f32[192,384]{1,0:T(8,128)S(1)} %copy-done.3, s32[192,384]{1,0:T(8,128)S(1)} %copy-done.4, ...), custom_call_target="tpu_custom_call" | custom-call | tf_op jit(solution)/shard_map/pack_rows/pallas_call | solution.py:477
  19.6 2.1 %collective-permute-start.2 = (f32[376,128]{1,0:T(8,128)S(1)}, f32[376,128]{1,0:T(8,128)S(1)}, u32[]{:S(2)}, u32[]{:S(2)}) collective-permute-start(f32[376,128]{1,0:T(8,128)S(1)} %get-tuple-element.19), channel_id=1, source_target_pairs={{0,4},{4,0},{8,12},{12,8},{1,5},{5,1},{9,13},{13,9},{2,6},{6,2},{1... | collective-permute-start | bytes 577544 | tf_op jit(solution)/shard_map/ppermute | solution.py:31
  21.7 0.8 %collective-permute-start.3 = (f32[56,128]{1,0:T(8,128)S(1)}, f32[56,128]{1,0:T(8,128)S(1)}, u32[]{:S(2)}, u32[]{:S(2)}) collective-permute-start(f32[56,128]{1,0:T(8,128)S(1)} %get-tuple-element.20), channel_id=1, source_target_pairs={{4,8},{8,4},{5,9},{9,5},{6,10},{10,6},{7,11},{11,7},{20,24},{24,20... | collective-permute-start | bytes 86024 | tf_op jit(solution)/shard_map/ppermute | solution.py:37
  22.5 2.2 %collective-permute-done.2.refs_8_.refs_11_ = f32[376,128]{1,0:T(8,128)S(1)} collective-permute-done((f32[376,128]{1,0:T(8,128)S(1)}, f32[376,128]{1,0:T(8,128)S(1)}, u32[]{:S(2)}, u32[]{:S(2)}) %collective-permute-start.2) | collective-permute-done | bytes 192544 | tf_op jit(solution)/shard_map/ppermute | solution.py:31
  24.7 11.0 %coastal.1 = (f32[192,384]{1,0:T(8,128)}, f32[192,384]{1,0:T(8,128)}, f32[192,384]{1,0:T(8,128)}, f32[64,128]{1,0:T(8,128)S(1)}) custom-call(f32[6]{0:T(128)S(1)} %copy-done.15, s32[2]{0:T(128)S(1)} %copy-done.16, f32[192,384]{1,0:T(8,128)S(1)} %copy-done, f32[192,384]{1,0:T(8,128)S(1)} %copy-done.1, f32[192,384]{1,0:T(8,128)S(1)} %copy-done.2, ...), custom_call_target="tpu_custom_call" | custom-call | tf_op jit(solution)/shard_map/coastal/pallas_call | solution.py:491
  35.7 4.8 %collective-permute-start.4 = (f32[64,128]{1,0:T(8,128)S(1)}, f32[64,128]{1,0:T(8,128)S(1)}, u32[]{:S(2)}, u32[]{:S(2)}) collective-permute-start(f32[64,128]{1,0:T(8,128)S(1)} %get-tuple-element.22.refs_2_), channel_id=1, source_target_pairs={{0,4},{4,8},{8,12},{1,5},{5,9},{9,13},{2,6},{6,10},{10,14},{3,7},{... | collective-permute-start | bytes 98312 | tf_op jit(solution)/shard_map/ppermute | solution.py:500
  40.5 2.2 %ocean.1 = (f32[64,128]{1,0:T(8,128)S(1)}, f32[64,128]{1,0:T(8,128)}, f32[64,128]{1,0:T(8,128)}) custom-call(f32[6]{0:T(128)S(1)} %copy-done.15, f32[64,128]{1,0:T(8,128)S(1)} %copy-done.8, f32[64,128]{1,0:T(8,128)S(1)} %copy-done.7, f32[64,128]{1,0:T(8,128)S(1)} %copy-done.10, f32[64,128]{1,0:T(8,128)S(1)} %copy-done.12, s32[64,128]{1,0:T(8,128)S(1)} %copy-done.14, ...), custom_call_target="tpu_custom_call" | custom-call | tf_op jit(solution)/shard_map/ocean/pallas_call | solution.py:503
  42.7 1.2 %paste.1 = f32[64,128]{1,0:T(8,128)} custom-call(s32[2]{0:T(128)S(1)} %copy-done.16, f32[64,128]{1,0:T(8,128)S(1)} %get-tuple-element.21.refs_1_, f32[64,128]{1,0:T(8,128)S(1)} %get-tuple-element.22.refs_2_, f32[64,128]{1,0:T(8,128)S(1)} %collective-permute-done.4.refs_3_), custom_call_target="tpu_custom_call" | custom-call | tf_op jit(solution)/shard_map/paste/pallas_call | solution.py:513
  (25 shorter events, 0.0 us)
Async XLA Ops:
  0.6 1.0 %copy-start = (f32[192,384]{1,0:T(8,128)S(1)}, f32[192,384]{1,0:T(8,128)}, u32[]{:S(2)}) copy-start(f32[192,384]{1,0:T(8,128)} %refs_2_.7) | copy-start | bytes 884740
  1.6 1.0 %copy-start.1 = (f32[192,384]{1,0:T(8,128)S(1)}, f32[192,384]{1,0:T(8,128)}, u32[]{:S(2)}) copy-start(f32[192,384]{1,0:T(8,128)} %refs_3_.7) | copy-start | bytes 884740
  2.6 1.0 %copy-start.2 = (f32[192,384]{1,0:T(8,128)S(1)}, f32[192,384]{1,0:T(8,128)}, u32[]{:S(2)}) copy-start(f32[192,384]{1,0:T(8,128)} %refs_4_.7) | copy-start | bytes 884740
  3.5 1.0 %copy-start.3 = (f32[192,384]{1,0:T(8,128)S(1)}, f32[192,384]{1,0:T(8,128)}, u32[]{:S(2)}) copy-start(f32[192,384]{1,0:T(8,128)} %refs_5_.7) | copy-start | bytes 884740
  4.5 1.0 %copy-start.4 = (s32[192,384]{1,0:T(8,128)S(1)}, s32[192,384]{1,0:T(8,128)}, u32[]{:S(2)}) copy-start(s32[192,384]{1,0:T(8,128)} %refs_6_.5) | copy-start | bytes 884740
  5.4 1.0 %copy-start.5 = (s32[192,384]{1,0:T(8,128)S(1)}, s32[192,384]{1,0:T(8,128)}, u32[]{:S(2)}) copy-start(s32[192,384]{1,0:T(8,128)} %refs_7_.5) | copy-start | bytes 884740
  6.4 0.8 %copy-start.6 = (f32[64,128]{1,0:T(8,128)S(1)}, f32[64,128]{1,0:T(8,128)}, u32[]{:S(2)}) copy-start(f32[64,128]{1,0:T(8,128)} %refs_8_.5) | copy-start | bytes 98308
  7.2 0.8 %copy-start.8 = (f32[64,128]{1,0:T(8,128)S(1)}, f32[64,128]{1,0:T(8,128)}, u32[]{:S(2)}) copy-start(f32[64,128]{1,0:T(8,128)} %refs_1_.6) | copy-start | bytes 98308
  7.9 0.8 %copy-start.9 = (f32[64,128]{1,0:T(8,128)S(1)}, f32[64,128]{1,0:T(8,128)}, u32[]{:S(2)}) copy-start(f32[64,128]{1,0:T(8,128)} %refs_3_.6) | copy-start | bytes 98308
  8.7 0.8 %copy-start.11 = (f32[64,128]{1,0:T(8,128)S(1)}, f32[64,128]{1,0:T(8,128)}, u32[]{:S(2)}) copy-start(f32[64,128]{1,0:T(8,128)} %refs_4_.6) | copy-start | bytes 98308
  9.4 0.8 %copy-start.13 = (s32[64,128]{1,0:T(8,128)S(1)}, s32[64,128]{1,0:T(8,128)}, u32[]{:S(2)}) copy-start(s32[64,128]{1,0:T(8,128)} %refs_5_.6) | copy-start | bytes 98308
  10.2 0.7 %copy-start.15 = (f32[6]{0:T(128)S(1)}, f32[6]{0:T(128)}, u32[]{:S(2)}) copy-start(f32[6]{0:T(128)} %refs_0_.8) | copy-start | bytes 76
  11.8 4.6 %collective-permute-start = (f32[192,128]{1,0:T(8,128)S(1)}, f32[192,128]{1,0:T(8,128)S(1)}, u32[]{:S(2)}, u32[]{:S(2)}) collective-permute-start(f32[192,128]{1,0:T(8,128)S(1)} %get-tuple-element.17), channel_id=1, source_target_pairs={{0,1},{1,0},{2,3},{3,2},{4,5},{5,4},{6,7},{7,6},{8,9},{9,8},{10,11... | collective-permute-start | bytes 294920 | tf_op jit(solution)/shard_map/ppermute | solution.py:31
  12.0 12.8 %copy-start.7 = (f32[64,128]{1,0:T(8,128)S(1)}, f32[64,128]{1,0:T(8,128)}, u32[]{:S(2)}) copy-start(f32[64,128]{1,0:T(8,128)} %refs_8_.5) | copy-start | bytes 98308
  12.0 7.1 %collective-permute-start.1 = (f32[192,128]{1,0:T(8,128)S(1)}, f32[192,128]{1,0:T(8,128)S(1)}, u32[]{:S(2)}, u32[]{:S(2)}) collective-permute-start(f32[192,128]{1,0:T(8,128)S(1)} %get-tuple-element.18), channel_id=1, source_target_pairs={{1,2},{2,1},{5,6},{6,5},{9,10},{10,9},{13,14},{14,13},{17,18},{18,... | collective-permute-start | bytes 294920 | tf_op jit(solution)/shard_map/ppermute | solution.py:37
  19.6 5.1 %copy-start.16 = (s32[2]{0:T(128)S(1)}, s32[2]{0:T(128)}, u32[]{:S(2)}) copy-start(s32[2]{0:T(128)} %refs_0_.9) | copy-start | bytes 28
  19.6 5.1 %collective-permute-start.2 = (f32[376,128]{1,0:T(8,128)S(1)}, f32[376,128]{1,0:T(8,128)S(1)}, u32[]{:S(2)}, u32[]{:S(2)}) collective-permute-start(f32[376,128]{1,0:T(8,128)S(1)} %get-tuple-element.19), channel_id=1, source_target_pairs={{0,4},{4,0},{8,12},{12,8},{1,5},{5,1},{9,13},{13,9},{2,6},{6,2},{1... | collective-permute-start | bytes 577544 | tf_op jit(solution)/shard_map/ppermute | solution.py:31
  21.7 18.8 %copy-start.10 = (f32[64,128]{1,0:T(8,128)S(1)}, f32[64,128]{1,0:T(8,128)}, u32[]{:S(2)}) copy-start(f32[64,128]{1,0:T(8,128)} %refs_3_.6) | copy-start | bytes 98308
  21.7 18.8 %copy-start.12 = (f32[64,128]{1,0:T(8,128)S(1)}, f32[64,128]{1,0:T(8,128)}, u32[]{:S(2)}) copy-start(f32[64,128]{1,0:T(8,128)} %refs_4_.6) | copy-start | bytes 98308
  21.7 18.8 %copy-start.14 = (s32[64,128]{1,0:T(8,128)S(1)}, s32[64,128]{1,0:T(8,128)}, u32[]{:S(2)}) copy-start(s32[64,128]{1,0:T(8,128)} %refs_5_.6) | copy-start | bytes 98308
  21.7 0.8 %collective-permute-start.3 = (f32[56,128]{1,0:T(8,128)S(1)}, f32[56,128]{1,0:T(8,128)S(1)}, u32[]{:S(2)}, u32[]{:S(2)}) collective-permute-start(f32[56,128]{1,0:T(8,128)S(1)} %get-tuple-element.20), channel_id=1, source_target_pairs={{4,8},{8,4},{5,9},{9,5},{6,10},{10,6},{7,11},{11,7},{20,24},{24,20... | collective-permute-start | bytes 86024 | tf_op jit(solution)/shard_map/ppermute | solution.py:37
  35.7 7.0 %collective-permute-start.4 = (f32[64,128]{1,0:T(8,128)S(1)}, f32[64,128]{1,0:T(8,128)S(1)}, u32[]{:S(2)}, u32[]{:S(2)}) collective-permute-start(f32[64,128]{1,0:T(8,128)S(1)} %get-tuple-element.22.refs_2_), channel_id=1, source_target_pairs={{0,4},{4,8},{8,12},{1,5},{5,9},{9,13},{2,6},{6,10},{10,14},{3,7},{... | collective-permute-start | bytes 98312 | tf_op jit(solution)/shard_map/ppermute | solution.py:500

commit v2 on v1

v2 whole, which is shorter than its diff:
```python
import functools

import jax
import jax.numpy as jnp
from jax import lax
from jax.experimental import pallas as pl
from jax.experimental.pallas import tpu as pltpu
from jax.sharding import PartitionSpec as P

R = 3
ITERS = 4
FSTEPS = R * ITERS
COURANT = 0.45
FLOOR = 0.25
SA = COURANT**2 / 2
SB = COURANT**3 / 2
POWER = -7.0 / 3.0
TFLOOR = 2 * SA * FLOOR
KSCALE = 0.5 * COURANT * (2 * SA) ** (7.0 / 3.0) / SB
CLOSED = 3.0e38
LANES = 128
HALO = 16
OLANE = 6 * 16
REACH = FSTEPS
VMEM = pl.BlockSpec(memory_space=pltpu.VMEM)
SMEM = pl.BlockSpec(memory_space=pltpu.SMEM)
ANY = pl.BlockSpec(memory_space=pltpu.HBM)
F32 = jnp.float32


def swap_even(value, axis):
    count = lax.axis_size(axis)
    return lax.ppermute(value, axis, [(i, i ^ 1) for i in range(count) if i ^ 1 < count])


def swap_odd(value, axis):
    count = lax.axis_size(axis)
    pairs = [(i, ((i + 1) ^ 1) - 1) for i in range(1, count)]
    return lax.ppermute(value, axis, [(a, b) for a, b in pairs if b < count])


def friction(classes, table):
    result = jnp.full(classes.shape, table[0], F32)
    for level_id in range(1, table.shape[0]):
        result = jnp.where(classes == level_id, table[level_id], result)
    return result


def field_of(refs, f, rows, cols, table):
    value = refs[f][rows, cols]
    if f < 4:
        return value * (SA, SB, SB, SA)[f]
    return friction(value, table) if f == 4 else value.astype(F32)


def fine_fields(refs, rows, cols, table):
    eta, qx, qy, depth, wet, classes = refs
    return tuple(field_of((eta, qx, qy, depth, classes, wet), f, rows, cols, table) for f in range(6))


def ocean_field(refs, j, rows, cols, table):
    value = refs[j][rows, cols]
    return value * (SA, SB, SB, SA)[j] if j < 4 else friction(value, table)


def ocean_fields(refs, rows, cols, table):
    return tuple(ocean_field(refs, j, rows, cols, table) for j in range(5))


def roll_to(value, start, target):
    return pltpu.roll(value, (target - start) % LANES, 1)


def copy_in(pairs, sems):
    copies = [pltpu.make_async_copy(src, dst, sems.at[i]) for i, (src, dst) in enumerate(pairs)]
    for copy in copies:
        copy.start()
    for copy in copies:
        copy.wait()


def pack_rows_kernel(pairs_only, *refs):
    table, fine, ocean = refs[0], refs[1:7], refs[7:12]
    outs = refs[12:14]
    held, held_int, ocean_in, ocean_class, sems = refs[14:]
    rows, cols = fine[0].shape
    tiles = cols // LANES
    ocean_rows = ocean[0].shape[0]
    is_even = lax.rem(lax.axis_index("gx"), 2) == 0
    pairs = []
    for side in range(1 if pairs_only else 2):
        last = is_even if side == 0 else jnp.logical_not(is_even)
        at = pl.multiple_of(jnp.where(last, rows - HALO, 0), 8)
        for f in range(6):
            target = held.at[f, side] if f < 4 else held_int.at[f - 4, side]
            pairs.append((fine[f].at[pl.ds(at, HALO), :], target))
    for j in range(5):
        pairs.append((ocean[j], ocean_in.at[j] if j < 4 else ocean_class))
    copy_in(pairs, sems)

    for side, out in enumerate(outs):
        last = is_even if side == 0 else jnp.logical_not(is_even)
        base = out.shape[0] - 5 * ITERS
        if base > 0:
            sources = [held.at[f, side] for f in range(4)] + [held_int.at[f, side] for f in range(2)]
            for t in range(tiles):
                at_cols = pl.ds(t * LANES, LANES)
                low = fine_fields(sources, pl.ds(HALO - REACH, REACH), at_cols, table)
                top = fine_fields(sources, pl.ds(0, REACH), at_cols, table)
                for f in range(6):
                    out[pl.ds((f * tiles + t) * REACH, REACH), :] = jnp.where(last, low[f], top[f])
        sources = [ocean_in.at[j] for j in range(4)] + [ocean_class]
        low = ocean_fields(sources, pl.ds(ocean_rows - ITERS, ITERS), pl.ds(0, LANES), table)
        top = ocean_fields(sources, pl.ds(0, ITERS), pl.ds(0, LANES), table)
        for j in range(5):
            out[pl.ds(base + j * ITERS, ITERS), :] = jnp.where(last, low[j], top[j])


def halo_blocks(pairs_only, messages, block, gx_is_even):
    rows = [message[pl.ds(block * REACH, REACH), :] for message in messages[: 1 if pairs_only else 2]]
    gap = jnp.zeros((HALO - REACH, LANES), F32)
    if pairs_only:
        return [jnp.where(gx_is_even, jnp.concatenate([rows[0], gap], 0), jnp.concatenate([gap, rows[0]], 0))]
    after = jnp.where(gx_is_even, rows[0], rows[1])
    before = jnp.where(gx_is_even, rows[1], rows[0])
    return [jnp.concatenate([after, gap], 0), jnp.concatenate([gap, before], 0)]


def ocean_halo(messages, j, gx_is_even):
    even, odd = (m[pl.ds(m.shape[0] - (5 - j) * ITERS, ITERS), :] for m in messages)
    return jnp.where(gx_is_even, jnp.concatenate([even, odd], 0), jnp.concatenate([odd, even], 0))


def packed_columns(parts):
    lane = iota((8, LANES), 1)
    west = jnp.zeros((8, LANES), F32)
    east = jnp.zeros((8, LANES), F32)
    for at, wide, from_west, from_east in parts:
        inside = (lane >= at) & (lane < at + wide)
        west = jnp.where(inside, roll_to(from_west, 0, at), west)
        east = jnp.where(inside, roll_to(from_east, LANES - wide, at), east)
    is_even = lax.rem(lax.axis_index("gy"), 2) == 0
    return jnp.where(is_even, east, west), jnp.where(is_even, west, east)


def columns_parts(first, last, ocean_values):
    parts = [(16 * f, 16, first[f], last[f]) for f in range(6)]
    return parts + [(OLANE + ITERS * j, ITERS, v, v) for j, v in enumerate(ocean_values)]


def strip_lanes(first, last):
    lane = iota((8, LANES), 1)
    moved = jnp.where(lane < 64, roll_to(last, LANES - 32, 32), 0.0)
    return jnp.where(lane < 32, first, moved)


def prepare_kernel(*refs):
    table, fine, ocean = refs[0], refs[1:7], refs[7:12]
    even_out, odd_out, strip = refs[12:]
    rows, cols = fine[0].shape
    ocean_rows = ocean[0].shape[0]
    for r in range(rows // 8):
        row = pl.ds(8 * r, 8)
        first = fine_fields(fine, row, pl.ds(0, LANES), table)
        last = fine_fields(fine, row, pl.ds(cols - LANES, LANES), table)
        values = ocean_fields(ocean, row, pl.ds(0, LANES), table) if 8 * r < ocean_rows else ()
        even_out[row, :], odd_out[row, :] = packed_columns(columns_parts(first, last, values))
        for f in range(6):
            strip[f, row, :] = strip_lanes(first[f], last[f])


def pack_columns_kernel(pairs_only, tiles, ocean_rows, *refs):
    own, messages, outs = refs[:2], refs[2:4], refs[4:6]
    rows = own[0].shape[0]
    gx_is_even = lax.rem(lax.axis_index("gx"), 2) == 0
    extra = pl.ds(ocean_rows, 8)
    values = [ocean_halo(messages, j, gx_is_even) for j in range(5)]
    parts = [(OLANE + ITERS * j, ITERS, v, v) for j, v in enumerate(values)]
    ocean_lanes = iota((8, LANES), 1) >= OLANE
    for out, mine, value in zip(outs, own, packed_columns(parts)):
        out[0:rows, :] = mine[...]
        out[extra, :] = jnp.where(ocean_lanes, value, mine[extra, :])
    halos = [
        [halo_blocks(pairs_only, messages, f * tiles + t, gx_is_even) for t in (0, tiles - 1)] for f in range(6)
    ]
    for r in range(rows // 8, outs[0].shape[0] // 8):
        side, half = divmod(r - rows // 8, HALO // 8)
        first, last = (
            [halos[f][end][side][8 * half : 8 * half + 8] for f in range(6)] for end in range(2)
        )
        for out, value in zip(outs, packed_columns(columns_parts(first, last, ()))):
            out[pl.ds(8 * r, 8), :] = value


def lane_next(values, ring=True):
    lane = lax.broadcasted_iota(jnp.int32, values[0].shape, 1)
    rolled = [pltpu.roll(v, LANES - 1, 1) for v in values]
    count = len(values)
    if count == 1:
        return rolled
    inner = [jnp.where(lane == LANES - 1, rolled[t + 1], rolled[t]) for t in range(count - 1)]
    end = jnp.where(lane == LANES - 1, rolled[0], rolled[-1]) if ring else rolled[-1]
    return inner + [end]


def lane_prev(values, ring=True):
    lane = lax.broadcasted_iota(jnp.int32, values[0].shape, 1)
    rolled = [pltpu.roll(v, 1, 1) for v in values]
    count = len(values)
    if count == 1:
        return rolled
    start = jnp.where(lane == 0, rolled[-1] if ring else 0.0, rolled[0])
    return [start] + [jnp.where(lane == 0, rolled[t - 1], rolled[t]) for t in range(1, count)]


def new_flux(flux, eta, eta_next, wet, wet_next, opened, drag):
    total = wet + wet_next
    power = jnp.exp2(POWER * jnp.log2(jnp.maximum(total, TFLOOR)))
    denom = opened + (drag * jnp.abs(flux)) * power
    return (flux - total * (eta_next - eta)) / denom


def prepare_faces(tiles, n, kf, wf, kx, ky, ox, oy, ring=True):
    for t in range(tiles):
        wrap = pl.ds(8 + 8 * n, 8)
        kf[t, wrap, :] = kf[t, pl.ds(8, 8), :]
        if wf is not None:
            wf[t, wrap, :] = wf[t, pl.ds(8, 8), :]
    for r in range(n):
        here, after = pl.ds(8 + 8 * r, 8), pl.ds(9 + 8 * r, 8)
        k = [kf[t, here, :] for t in range(tiles)]
        k_next = lane_next(k)
        if wf is not None:
            w = [wf[t, here, :] for t in range(tiles)]
            w_next = lane_next(w)
        for t in range(tiles):
            kx[t, here, :] = KSCALE * (k[t] + kf[t, after, :])
            ky[t, here, :] = KSCALE * (k[t] + k_next[t])
            if wf is not None:
                ox[t, here, :] = jnp.where(w[t] * wf[t, after, :] > 0.5, 1.0, CLOSED)
                open_y = w[t] * w_next[t] > 0.5
                if not ring and t == tiles - 1:
                    open_y = open_y & (iota((8, LANES), 1) < LANES - 1)
                oy[t, here, :] = jnp.where(open_y, 1.0, CLOSED)


def level_pass(tiles, n, e, g, x, y, d, ring=True):
    for r in range(n):
        here, before = pl.ds(8 + 8 * r, 8), pl.ds(7 + 8 * r, 8)
        south = [y[t, here, :] for t in range(tiles)]
        south_prev = lane_prev(south, ring)
        for t in range(tiles):
            flow = (x[t, here, :] - x[t, before, :]) + (south[t] - south_prev[t])
            eta = e[t, here, :] - flow
            wet = jnp.maximum(d[t, here, :] + eta, 0.0)
            e[t, here, :] = eta
            g[t, here, :] = wet
            if r == 0:
                e[t, pl.ds(8 + 8 * n, 8), :] = eta
                g[t, pl.ds(8 + 8 * n, 8), :] = wet


def flux_pass(tiles, n, e, g, x, y, kx, ky, ox, oy, fix, ring=True):
    for r in range(n):
        here, after = pl.ds(8 + 8 * r, 8), pl.ds(9 + 8 * r, 8)
        eta = [e[t, here, :] for t in range(tiles)]
        wet = [g[t, here, :] for t in range(tiles)]
        eta_next, wet_next = lane_next(eta, ring), lane_next(wet, ring)
        for t in range(tiles):
            fx = new_flux(
                x[t, here, :], eta[t], e[t, after, :], wet[t], g[t, after, :], ox[t, here, :], kx[t, here, :]
            )
            fx = fix(r, t, fx)
            x[t, here, :] = fx
            if r == n - 1:
                x[t, pl.ds(0, 8), :] = fx
            y[t, here, :] = new_flux(
                y[t, here, :], eta[t], eta_next[t], wet[t], wet_next[t], oy[t, here, :], ky[t, here, :]
            )


def dot(a, b):
    return lax.dot_general(
        a, b, (((1,), (0,)), ((), ())), precision=lax.Precision.HIGHEST, preferred_element_type=F32
    )


def iota(shape, dim):
    return lax.broadcasted_iota(jnp.int32, shape, dim)


def place_of(block_size):
    gx = lax.axis_index("gx")
    slot = lax.rem(gx, block_size)
    return gx, lax.div(gx, block_size), slot == 0, slot == block_size - 1


def grid_edges(mx_tiles, own_offset, ocean_rows, spread_to, wf, rows, edges):
    picks = iota((8, ocean_rows), 1) == jnp.where(iota((8, ocean_rows), 0) == 0, own_offset - 1, ocean_rows - 1)
    picks = picks.astype(F32)
    source = jnp.concatenate([dot(picks, tile) for tile in mx_tiles], 1)
    spread = dot(source, spread_to.astype(F32))
    for t in range(edges.shape[1]):
        cut = spread[:, t * LANES : (t + 1) * LANES]
        wet_first = wf[t, pl.ds(8, 8), :]
        wet_last = wf[t, pl.ds(rows, 8), :]
        edges[0, t, :, :] = jnp.broadcast_to(cut[0:1, :] * wet_first[0:1, :], (8, LANES))
        edges[1, t, :, :] = jnp.broadcast_to(cut[1:2, :] * wet_last[7:8, :], (8, LANES))


def run_coastal(tiles, n, rows, first, last, state, edges, ring):
    e, g, x, y, d, kx, ky, ox, oy = state
    sub = iota((8, LANES), 0)
    west_mask = (sub == 7) & first
    east_mask = (sub == 7) & last

    def fix(r, t, fx):
        if r == rows // 8 - 1:
            fx = jnp.where(east_mask, edges[1, t, :, :], fx)
        if r == n - 1:
            fx = jnp.where(west_mask, edges[0, t, :, :], fx)
        return fx

    for t in range(tiles):
        x[t, pl.ds(0, 8), :] = jnp.where(west_mask, edges[0, t, :, :], x[t, pl.ds(8 * n, 8), :])

    def step(_, carry):
        level_pass(tiles, n, e, g, x, y, d, ring)
        flux_pass(tiles, n, e, g, x, y, kx, ky, ox, oy, fix, ring)
        return carry

    lax.fori_loop(0, FSTEPS, step, 0)


def interior_kernel(block_size, *refs):
    table, offsets, fine, ocean_mx = refs[0], refs[1], refs[2:8], refs[8]
    pairs_only = block_size == 2
    count = 1 if pairs_only else 2
    messages = refs[9:11]
    outs, out_means = refs[11:14], refs[14]
    e, g, x, y, d, kf, wf, kx, ky, ox, oy, edges = refs[15:]
    rows, cols = fine[0].shape
    tiles = cols // LANES
    n = rows // 8 + (HALO // 8) * count
    gx, grid, first, last = place_of(block_size)
    gx_is_even = lax.rem(gx, 2) == 0
    dest = (e, x, y, d, kf, wf)
    for r in range(rows // 8):
        src, here = pl.ds(8 * r, 8), pl.ds(8 + 8 * r, 8)
        for t in range(tiles):
            for f, value in enumerate(fine_fields(fine, src, pl.ds(t * LANES, LANES), table)):
                dest[f][t, here, :] = value
    for f in range(6):
        for t in range(tiles):
            for side, block in enumerate(halo_blocks(pairs_only, messages, f * tiles + t, gx_is_even)):
                dest[f][t, pl.ds(8 + rows + HALO * side, HALO), :] = block

    ocean_rows = ocean_mx.shape[0]
    spread_to = iota((LANES, cols), 0) == lax.div(iota((LANES, cols), 1), R)
    grid_edges([ocean_mx[...] * SB], offsets[grid], ocean_rows, spread_to, wf, rows, edges)
    prepare_faces(tiles, n, kf, wf, kx, ky, ox, oy, False)
    run_coastal(tiles, n, rows, first, last, (e, g, x, y, d, kx, ky, ox, oy), edges, False)
    for r in range(rows // 8):
        to, here = pl.ds(8 * r, 8), pl.ds(8 + 8 * r, 8)
        for t in range(tiles):
            at_cols = pl.ds(t * LANES, LANES)
            outs[0][to, at_cols] = e[t, here, :] * (1.0 / SA)
            outs[1][to, at_cols] = x[t, here, :] * (1.0 / SB)
            outs[2][to, at_cols] = y[t, here, :] * (1.0 / SB)
    gather_cols = (lax.div(iota((cols, LANES), 0), R) == iota((cols, LANES), 1)).astype(F32)
    out_means[...] = coarse_means(outs[0][...], gather_cols, offsets[grid], ocean_rows)


def coarse_means(eta, gather_cols, own_offset, ocean_rows):
    shape = (ocean_rows, eta.shape[0])
    coarse_row = lax.rem(lax.div(iota(shape, 1), R) + own_offset, ocean_rows)
    gather_rows = (coarse_row == iota(shape, 0)).astype(F32)
    return dot(dot(gather_rows, eta), gather_cols) * (1.0 / (R * R))


def border_kernel(block_size, cols, *refs):
    offsets, strip, ocean_mx, messages = refs[0], refs[1], refs[2], refs[3:5]
    gy_even, gy_odd, inner_means = refs[5:8]
    outs, out_means = refs[8:11], refs[11]
    e, g, x, y, d, kf, wf, kx, ky, ox, oy, edges = refs[12:]
    pairs_only = block_size == 2
    rows = strip.shape[1]
    own = cols // LANES
    n = rows // 8 + (HALO // 8) * (1 if pairs_only else 2)
    gx, grid, first, last = place_of(block_size)
    gx_is_even = lax.rem(gx, 2) == 0
    gy_is_even = lax.rem(lax.axis_index("gy"), 2) == 0
    lane = iota((8, LANES), 1)
    dest = (e, x, y, d, kf, wf)
    halos = [
        [halo_blocks(pairs_only, messages, f * own + t, gx_is_even) for t in (0, own - 1)] for f in range(6)
    ]
    for r in range(n):
        src, here = pl.ds(8 * r, 8), pl.ds(8 + 8 * r, 8)
        if 8 * r < rows:
            mine = [strip[f, src, :] for f in range(6)]
        else:
            side, half = divmod(r - rows // 8, HALO // 8)
            cut = slice(8 * half, 8 * half + 8)
            mine = [strip_lanes(halos[f][0][side][cut], halos[f][1][side][cut]) for f in range(6)]
        from_even, from_odd = gy_even[src, :], gy_odd[src, :]
        from_east = jnp.where(gy_is_even, from_even, from_odd)
        from_west = jnp.where(gy_is_even, from_odd, from_even)
        for f in range(6):
            east = roll_to(from_east, 16 * f, 64)
            west = roll_to(from_west, 16 * f, LANES - 16)
            value = jnp.where((lane >= 64) & (lane < 80), east, mine[f])
            dest[f][0, here, :] = jnp.where(lane < LANES - 16, value, west)

    ocean_rows = ocean_mx.shape[0]
    from_even, from_odd = gy_even[0:ocean_rows, :], gy_odd[0:ocean_rows, :]
    from_east = jnp.where(gy_is_even, from_even, from_odd)
    from_west = jnp.where(gy_is_even, from_odd, from_even)
    lanes = iota((ocean_rows, LANES), 1)
    mx_halo = jnp.where(
        lanes < ITERS,
        roll_to(from_east, OLANE + ITERS, 0),
        roll_to(from_west, OLANE + ITERS, LANES - ITERS),
    )
    to = iota((2 * LANES, LANES), 1)
    wanted = jnp.where(to < 32, lax.div(to, R), lax.div(to + (cols - 64), R))
    wanted = jnp.where(to < 64, wanted, jnp.where(to < 80, LANES + lax.div(to - 64, R), 0))
    wanted = jnp.where(to < LANES - 16, wanted, 2 * LANES - 1 - lax.div(LANES - 1 - to, R))
    spread_to = iota((2 * LANES, LANES), 0) == wanted
    grid_edges([ocean_mx[...] * SB, mx_halo], offsets[grid], ocean_rows, spread_to, wf, rows, edges)
    prepare_faces(1, n, kf, wf, kx, ky, ox, oy)
    run_coastal(1, n, rows, first, last, (e, g, x, y, d, kx, ky, ox, oy), edges, True)

    for i, (held, scale) in enumerate(((e, 1.0 / SA), (x, 1.0 / SB), (y, 1.0 / SB))):
        outs[i][...] = held[0, 8 : 8 + rows, :] * scale
    source, target = iota((LANES, LANES), 0), iota((LANES, LANES), 1)
    column = jnp.where(source < 32, source, source + (cols - 64))
    inside = (source < FSTEPS) | ((source >= 64 - FSTEPS) & (source < 64))
    gather = ((lax.div(column, R) == target) & inside).astype(F32)
    means = coarse_means(outs[0][...], gather, offsets[grid], ocean_rows)
    col = iota((ocean_rows, LANES), 1)
    out_means[...] = jnp.where((col < ITERS) | (col >= LANES - ITERS), means, inner_means[...])


def finish_coastal(inner, strips, final, outs, sems):
    rows, cols = final.shape[1:]
    own = cols // LANES
    lane = iota((8, LANES), 1)
    copies = [pltpu.make_async_copy(final.at[i], outs[i], sems.at[i]) for i in range(3)]
    for i in range(3):
        for r in range(rows // 8):
            to = pl.ds(8 * r, 8)
            value = strips[i][to, :]
            for t in range(own):
                at_cols = pl.ds(t * LANES, LANES)
                kept = inner[i][to, at_cols]
                if t == 0:
                    kept = jnp.where(lane < FSTEPS, value, kept)
                if t == own - 1:
                    kept = jnp.where(lane >= LANES - FSTEPS, roll_to(value, 32, LANES - 32), kept)
                final[i, to, at_cols] = kept
        copies[i].start()
    return copies


def finish_kernel(*refs):
    table, ocean = refs[0], refs[1:6]
    gy_even, gy_odd, gx_even, gx_odd = refs[6:10]
    inner, strips = refs[10:13], refs[13:16]
    fine_outs, (out_eta, out_x, out_y) = refs[16:19], refs[19:22]
    final, sems = refs[22:24]
    e, g, x, y, d, kf, kx, ky, ox, oy = refs[24:]
    copies = finish_coastal(inner, strips, final, fine_outs, sems)
    rows, cols = ocean[0].shape
    tiles = 2
    n = rows // 8 + 1
    gx, gy = lax.axis_index("gx"), lax.axis_index("gy")
    gx_is_even = lax.rem(gx, 2) == 0
    gy_is_even = lax.rem(gy, 2) == 0
    lane = iota((8, LANES), 1)
    sub = iota((8, LANES), 0)

    def unpack(from_even, from_odd, j):
        from_east = jnp.where(gy_is_even, from_even, from_odd)
        from_west = jnp.where(gy_is_even, from_odd, from_even)
        east = roll_to(from_east, OLANE + ITERS * j, 0)
        west = roll_to(from_west, OLANE + ITERS * j, LANES - 4)
        return jnp.where(lane < 4, east, jnp.where(lane >= LANES - 4, west, 0.0))

    dest = (e, x, y, d, kf)
    for r in range(rows // 8):
        src, here = pl.ds(8 * r, 8), pl.ds(8 + 8 * r, 8)
        for j, value in enumerate(ocean_fields(ocean, src, pl.ds(0, LANES), table)):
            dest[j][0, here, :] = value
            dest[j][1, here, :] = unpack(gy_even[src, :], gy_odd[src, :], j)

    here, halo = pl.ds(8 + rows, 8), pl.ds(rows, 8)
    for j in range(5):
        dest[j][0, here, :] = ocean_halo((gx_even, gx_odd), j, gx_is_even)
        dest[j][1, here, :] = unpack(gy_even[halo, :], gy_odd[halo, :], j)

    prepare_faces(tiles, n, kf, None, kx, ky, None, None)
    rows_total, cols_total = rows * lax.axis_size("gx"), cols * lax.axis_size("gy")
    for r in range(n):
        here = pl.ds(8 + 8 * r, 8)
        row = sub + 8 * r
        row = jnp.where(row >= rows + 4, row - (rows + 8), row) + gx * rows
        for t in range(tiles):
            col = lane if t == 0 else jnp.where(lane < 64, lane + LANES, lane - LANES)
            col = col + gy * cols
            ox[t, here, :] = jnp.where((row >= 0) & (row < rows_total - 1), 1.0, CLOSED)
            oy[t, here, :] = jnp.where((col >= 0) & (col < cols_total - 1), 1.0, CLOSED)
    for t in range(tiles):
        x[t, pl.ds(0, 8), :] = x[t, pl.ds(8 * n, 8), :]

    def step(_, carry):
        level_pass(tiles, n, e, g, x, y, d)
        flux_pass(tiles, n, e, g, x, y, kx, ky, ox, oy, lambda r, t, fx: fx)
        return carry

    lax.fori_loop(0, ITERS, step, 0)
    for r in range(rows // 8):
        to, here = pl.ds(8 * r, 8), pl.ds(8 + 8 * r, 8)
        out_eta[to, :] = e[0, here, :] * (1.0 / SA)
        out_x[to, :] = x[0, here, :] * (1.0 / SB)
        out_y[to, :] = y[0, here, :] * (1.0 / SB)
    for copy in copies:
        copy.wait()


def paste_kernel(block_size, *refs):
    offsets, eta, rolled, arrived, out = refs
    gx, grid, _, _ = place_of(block_size)
    own_offset = offsets[grid]
    left_offset = jnp.where(gx >= 1, offsets[lax.div(jnp.maximum(gx - 1, 0), block_size)], 0)
    row = iota(eta.shape, 0)
    out[...] = jnp.where(
        row >= own_offset, rolled[...], jnp.where(row < left_offset, arrived[...], eta[...])
    )


def shape(*dims):
    return jax.ShapeDtypeStruct(dims, F32)


def params():
    return pltpu.CompilerParams(vmem_limit_bytes=48 * 1024 * 1024)


def shards(
    ocean_eta,
    ocean_mx,
    ocean_ny,
    ocean_depth,
    ocean_class,
    manning,
    fine_eta,
    fine_qx,
    fine_qy,
    fine_depth,
    fine_wet,
    fine_class,
    fine_offset,
):
    ocean_rows, ocean_cols = ocean_eta.shape
    rows, cols = fine_eta.shape
    own = cols // LANES
    gx_count = lax.axis_size("gx")
    block_size = min(16, gx_count // 2)
    pairs_only = block_size == 2
    fine = (fine_eta, fine_qx, fine_qy, fine_depth, fine_wet, fine_class)
    ocean = (ocean_eta, ocean_mx, ocean_ny, ocean_depth, ocean_class)

    def vmem(*dims, dtype=F32):
        return pltpu.VMEM(dims, dtype)

    count = 1 if pairs_only else 2
    both = 6 * own * REACH + 5 * ITERS
    gx_even, gx_odd = pl.pallas_call(
        functools.partial(pack_rows_kernel, pairs_only),
        out_shape=(shape(both, LANES), shape(5 * ITERS if pairs_only else both, LANES)),
        in_specs=[SMEM] + [ANY] * 11,
        out_specs=(VMEM,) * 2,
        scratch_shapes=[
            vmem(4, count, HALO, cols),
            vmem(2, count, HALO, cols, dtype=jnp.int32),
            vmem(4, ocean_rows, ocean_cols),
            vmem(ocean_rows, ocean_cols, dtype=jnp.int32),
            pltpu.SemaphoreType.DMA((6 * count + 5,)),
        ],
        name="pack_rows",
    )(manning, *fine, *ocean)
    gx_even = swap_even(gx_even, "gx")
    gx_odd = swap_odd(gx_odd, "gx")

    own_even, own_odd, strip = pl.pallas_call(
        prepare_kernel,
        out_shape=(shape(rows, LANES),) * 2 + (shape(6, rows, LANES),),
        in_specs=[SMEM] + [VMEM] * 11,
        out_specs=(VMEM,) * 3,
        compiler_params=params(),
        cost_estimate=pl.CostEstimate(flops=0, bytes_accessed=5_000_000, transcendentals=0),
        name="prepare",
    )(manning, *fine, *ocean)

    n = rows // 8 + (HALO // 8) * count
    gy_even, gy_odd = pl.pallas_call(
        functools.partial(pack_columns_kernel, pairs_only, own, ocean_rows),
        out_shape=(shape(8 * n, LANES),) * 2,
        in_specs=[VMEM] * 4,
        out_specs=(VMEM,) * 2,
        compiler_params=params(),
        name="pack_columns",
    )(own_even, own_odd, gx_even, gx_odd)
    gy_even = swap_even(gy_even, "gy")
    gy_odd = swap_odd(gy_odd, "gy")

    *inner, means = pl.pallas_call(
        functools.partial(interior_kernel, block_size),
        out_shape=(shape(rows, cols),) * 3 + (shape(ocean_rows, ocean_cols),),
        in_specs=[SMEM, SMEM] + [VMEM] * 9,
        out_specs=(VMEM,) * 4,
        scratch_shapes=[vmem(own, 8 * n + 16, LANES)] * 11 + [vmem(2, own, 8, LANES)],
        compiler_params=params(),
        cost_estimate=pl.CostEstimate(flops=0, bytes_accessed=20_000_000, transcendentals=0),
        name="interior",
    )(manning, fine_offset, *fine, ocean_mx, gx_even, gx_odd)

    *strips, rolled = pl.pallas_call(
        functools.partial(border_kernel, block_size, cols),
        out_shape=(shape(rows, LANES),) * 3 + (shape(ocean_rows, ocean_cols),),
        in_specs=[SMEM] + [VMEM] * 7,
        out_specs=(VMEM,) * 4,
        scratch_shapes=[vmem(1, 8 * n + 16, LANES)] * 11 + [vmem(2, 1, 8, LANES)],
        compiler_params=params(),
        name="border",
    )(fine_offset, strip, ocean_mx, gx_even, gx_odd, gy_even, gy_odd, means)
    arrived = lax.ppermute(rolled, "gx", [(i, i + 1) for i in range(gx_count - 1)])

    n = ocean_rows // 8 + 1
    feta, fqx, fqy, eta, mx, ny = pl.pallas_call(
        finish_kernel,
        out_shape=(shape(rows, cols),) * 3 + (shape(ocean_rows, ocean_cols),) * 3,
        in_specs=[SMEM] + [VMEM] * 15,
        out_specs=(ANY,) * 3 + (VMEM,) * 3,
        scratch_shapes=[vmem(3, rows, cols), pltpu.SemaphoreType.DMA((3,))] + [vmem(2, 8 * n + 16, LANES)] * 10,
        compiler_params=params(),
        cost_estimate=pl.CostEstimate(flops=0, bytes_accessed=5_000_000, transcendentals=0),
        name="finish",
    )(manning, *ocean, gy_even, gy_odd, gx_even, gx_odd, *inner, *strips)

    eta = pl.pallas_call(
        functools.partial(paste_kernel, block_size),
        out_shape=shape(ocean_rows, ocean_cols),
        in_specs=[SMEM] + [VMEM] * 3,
        out_specs=VMEM,
        compiler_params=params(),
        name="paste",
    )(fine_offset, eta, rolled, arrived)
    return (eta, mx, ny, feta, fqx, fqy)


def solution(mesh):
    tile = P(("scen", "gx"), "gy")
    in_specs = (tile,) * 5 + (P(),) + (tile,) * 6 + (P("scen"),)
    return jax.shard_map(shards, mesh=mesh, in_specs=in_specs, out_specs=(tile,) * 6, check_vma=False)
```

time: 44.8 us -> 33.5 us (0.75); the launches traced: 43.9 us -> 33.3 us
  local copies, waits for them, and re-layouts: 10.2 us -> 0.06 us
  waiting for transfers between devices: 4.79 us -> 1.37 us
  Pallas kernels: 15.9 us -> 18.7 us
    unnamed x34 -> x26, local copies, waits for them, and re-layouts: 10.2 us -> 0.06 us
    ppermute x2, waiting for transfers between devices: 2.57 us -> 0.01 us  [swap_odd(): return lax.ppermute(value, axis, [(a, b) for a, b in pairs if b < count])]
    pallas_call x1, Pallas kernels: 0.58 us -> 2.52 us  [shards(): pl.pallas_call(functools.partial(pack_rows_kernel, pairs_only), out_shape...]
    ppermute x2, starting transfers between devices: 5.26 us -> 3.83 us  [swap_odd(): return lax.ppermute(value, axis, [(a, b) for a, b in pairs if b < count])]
    ppermute x2, starting transfers between devices: 2.22 us -> 3.49 us  [swap_even(): lax.ppermute(value, axis, [(i, i ^ 1) for i in range(count) if i ^ 1 < co...]
    pallas_call x3 -> x5, Pallas kernels: 14.2 us -> 15 us  [the longest x1 7.52 us: shards(): pl.pallas_call(functools.partial(interior_kernel, block_size), out_shape=...]
    ppermute x2, waiting for transfers between devices: 2.21 us -> 1.37 us  [swap_even(): lax.ppermute(value, axis, [(i, i ^ 1) for i in range(count) if i ^ 1 < co...]
  transfers between devices with their start and end apart: 5 -> 5, of which waited for: 2 -> 1; matrix products, arithmetic and copies ran while one was open for 0% -> 0% of each run, Pallas kernels for 5% -> 33%
where the time goes in v2:
time: 33.5 us; the launch traced here: 33.3 us
  Pallas kernels  18.7 us (56%)
  starting transfers between devices  12.2 us (36%)
  waiting for transfers between devices  1.37 us (4%)
  between operations  0.95 us (3%)
    pallas_call x1, Pallas kernels, shards(): pl.pallas_call(functools.partial(interior_kernel, block_size), out_shape=...  7.52 us
    ppermute x1, starting transfers between devices, shards(): lax.ppermute(rolled, 'gx', [(i, i + 1) for i in range(gx_count - 1)])  4.86 us
    pallas_call x1, Pallas kernels, shards(): pl.pallas_call(functools.partial(border_kernel, block_size, cols), out_sh...  3.95 us
    ppermute x2, starting transfers between devices, swap_odd(): return lax.ppermute(value, axis, [(a, b) for a, b in pairs if b < count])  3.83 us
    ppermute x2, starting transfers between devices, swap_even(): lax.ppermute(value, axis, [(i, i ^ 1) for i in range(count) if i ^ 1 < co...  3.49 us
    pallas_call x1, Pallas kernels, shards(): pl.pallas_call(functools.partial(pack_rows_kernel, pairs_only), out_shape...  2.52 us
    pallas_call x1, Pallas kernels, shards(): pl.pallas_call(finish_kernel, out_shape=(shape(rows, cols),) * 3 + (shape...  2.35 us
    ppermute x2, waiting for transfers between devices, swap_even(): lax.ppermute(value, axis, [(i, i ^ 1) for i in range(count) if i ^ 1 < co...  1.37 us
  transfers between devices with their start and end apart: 5, of which 1 were waited for; matrix products, arithmetic and copies ran while one was open for 0% of the time, Pallas kernels for 33%

profile of v2, /device:TPU:1, one launch (start us, length us, event | category | flops | bytes accessed | tf_op | source)
XLA Modules:
  0.0 33.3 jit_solution(1301853065569201257)
XLA Ops:
  0.6 0.0 copy-start.6
  0.6 0.0 copy-start.5
  0.7 0.0 copy-start.4
  0.7 0.0 copy-start.3
  0.7 0.0 copy-start.2
  0.7 2.5 %pack_rows.1 = (f32[236,128]{1,0:T(8,128)}, f32[20,128]{1,0:T(8,128)}) custom-call(f32[6]{0:T(128)} %refs_0_.10, f32[192,384]{1,0:T(8,128)} %refs_2_.7, f32[192,384]{1,0:T(8,128)} %refs_3_.6, f32[192,384]{1,0:T(8,128)} %refs_4_.6, f32[192,384]{1,0:T(8,128)} %refs_5_.6, s32[192,384]{1,0:T(8,128)} %refs_6_.5, s32[192,384]{1,0:T(8,128)} %refs_7_.5, ...), custom_call_target="tpu_custom_call" | custom-call | tf_op jit(solution)/shard_map/pack_rows/pallas_call | solution.py:579
  3.3 0.0 copy-start.11
  3.3 2.2 %collective-permute-start = (f32[236,128]{1,0:T(8,128)}, f32[236,128]{1,0:T(8,128)S(1)}, u32[]{:S(2)}, u32[]{:S(2)}) collective-permute-start(f32[236,128]{1,0:T(8,128)} %get-tuple-element.29), channel_id=1, source_target_pairs={{0,4},{4,0},{8,12},{12,8},{1,5},{5,1},{9,13},{13,9},{2,6},{6,2},{1... | collective-permute-start | bytes 362504 | tf_op jit(solution)/shard_map/ppermute | solution.py:33
  5.5 0.7 %collective-permute-start.1 = (f32[20,128]{1,0:T(8,128)}, f32[20,128]{1,0:T(8,128)S(1)}, u32[]{:S(2)}, u32[]{:S(2)}) collective-permute-start(f32[20,128]{1,0:T(8,128)} %get-tuple-element.30), channel_id=1, source_target_pairs={{4,8},{8,4},{5,9},{9,5},{6,10},{10,6},{7,11},{11,7},{20,24},{24,20... | collective-permute-start | bytes 30728 | tf_op jit(solution)/shard_map/ppermute | solution.py:39
  6.3 1.1 %prepare.1 = (f32[192,128]{1,0:T(8,128)S(1)}, f32[192,128]{1,0:T(8,128)S(1)}, f32[6,192,128]{2,1,0:T(8,128)S(1)}) custom-call(f32[6]{0:T(128)S(1)} %copy-done.11, f32[192,384]{1,0:T(8,128)S(1)} %copy-done, f32[192,384]{1,0:T(8,128)S(1)} %copy-done.1, f32[192,384]{1,0:T(8,128)S(1)} %copy-done.2, f32[192,384]{1,0:T(8,128)S(1)} %copy-done.3, ...), custom_call_target="tpu_custom_call" | custom-call | bytes 5000000 | tf_op jit(solution)/shard_map/prepare/pallas_call | solution.py:596
  7.4 0.0 collective-permute-done.1.refs_3_.refs_10_.refs_4_.refs_9_
  7.4 1.4 %collective-permute-done.refs_2_.refs_9_.refs_3_.refs_8_ = f32[236,128]{1,0:T(8,128)S(1)} collective-permute-done((f32[236,128]{1,0:T(8,128)}, f32[236,128]{1,0:T(8,128)S(1)}, u32[]{:S(2)}, u32[]{:S(2)}) %collective-permute-start) | collective-permute-done | bytes 120864 | tf_op jit(solution)/shard_map/ppermute | solution.py:33
  8.7 0.1 pack_columns.1
  8.9 0.0 copy-start.12
  8.9 1.3 %collective-permute-start.2 = (f32[208,128]{1,0:T(8,128)S(1)}, f32[208,128]{1,0:T(8,128)S(1)}, u32[]{:S(2)}, u32[]{:S(2)}) collective-permute-start(f32[208,128]{1,0:T(8,128)S(1)} %get-tuple-element.31), channel_id=1, source_target_pairs={{0,1},{1,0},{2,3},{3,2},{4,5},{5,4},{6,7},{7,6},{8,9},{9,8},{10,11... | collective-permute-start | bytes 319496 | tf_op jit(solution)/shard_map/ppermute | solution.py:33
  10.2 3.2 %collective-permute-start.3 = (f32[208,128]{1,0:T(8,128)S(1)}, f32[208,128]{1,0:T(8,128)S(1)}, u32[]{:S(2)}, u32[]{:S(2)}) collective-permute-start(f32[208,128]{1,0:T(8,128)S(1)} %get-tuple-element.32), channel_id=1, source_target_pairs={{1,2},{2,1},{5,6},{6,5},{9,10},{10,9},{13,14},{14,13},{17,18},{18,... | collective-permute-start | bytes 319496 | tf_op jit(solution)/shard_map/ppermute | solution.py:39
  13.4 7.5 %interior.1 = (f32[192,384]{1,0:T(8,128)S(1)}, f32[192,384]{1,0:T(8,128)S(1)}, f32[192,384]{1,0:T(8,128)S(1)}, f32[64,128]{1,0:T(8,128)S(1)}) custom-call(f32[6]{0:T(128)S(1)} %copy-done.11, s32[2]{0:T(128)S(1)} %copy-done.12, f32[192,384]{1,0:T(8,128)S(1)} %copy-done, f32[192,384]{1,0:T(8,128)S(1)} %copy-done.1, f32[192,384]{1,0:T(8,128)S(1)} %copy-done.2, ...), custom_call_target="tpu_custom_call" | custom-call | bytes 20000000 | tf_op jit(solution)/shard_map/interior/pallas_call | solution.py:618
  20.9 0.0 collective-permute-done.2.refs_5_.refs_6_
  20.9 0.0 collective-permute-done.3.refs_6_.refs_7_
  20.9 3.9 %border.1 = (f32[192,128]{1,0:T(8,128)S(1)}, f32[192,128]{1,0:T(8,128)S(1)}, f32[192,128]{1,0:T(8,128)S(1)}, f32[64,128]{1,0:T(8,128)S(1)}) custom-call(s32[2]{0:T(128)S(1)} %copy-done.12, f32[6,192,128]{2,1,0:T(8,128)S(1)} %get-tuple-element.36.refs_1_, f32[64,128]{1,0:T(8,128)S(1)} %copy-done.6, ...), custom_call_target="tpu_custom_call" | custom-call | tf_op jit(solution)/shard_map/border/pallas_call | solution.py:629
  24.9 4.9 %collective-permute-start.4 = (f32[64,128]{1,0:T(8,128)S(1)}, f32[64,128]{1,0:T(8,128)S(1)}, u32[]{:S(2)}, u32[]{:S(2)}) collective-permute-start(f32[64,128]{1,0:T(8,128)S(1)} %get-tuple-element.42.refs_2_), channel_id=1, source_target_pairs={{0,4},{4,8},{8,12},{1,5},{5,9},{9,13},{2,6},{6,10},{10,14},{3,7},{... | collective-permute-start | bytes 98312 | tf_op jit(solution)/shard_map/ppermute | solution.py:638
  29.7 2.3 %finish.1 = (f32[192,384]{1,0:T(8,128)}, f32[192,384]{1,0:T(8,128)}, f32[192,384]{1,0:T(8,128)}, f32[64,128]{1,0:T(8,128)S(1)}, f32[64,128]{1,0:T(8,128)}, /*index=5*/f32[64,128]{1,0:T(8,128)}) custom-call(f32[6]{0:T(128)S(1)} %copy-done.11, f32[64,128]{1,0:T(8,128)S(1)} %copy-done.7, f32[64,128]{1,0:T(8,128)S(1)} %copy-done.6, f32[64,128]{1,0:T(8,128)S(1)} %copy-done.8, ...), custom_call_target="tpu_custom_call" | custom-call | bytes 5000000 | tf_op jit(solution)/shard_map/finish/pallas_call | solution.py:641
  32.1 0.0 collective-permute-done.4.refs_3_
  32.1 1.2 %paste.1 = f32[64,128]{1,0:T(8,128)} custom-call(s32[2]{0:T(128)S(1)} %copy-done.12, f32[64,128]{1,0:T(8,128)S(1)} %get-tuple-element.41.refs_1_, f32[64,128]{1,0:T(8,128)S(1)} %get-tuple-element.42.refs_2_, f32[64,128]{1,0:T(8,128)S(1)} %collective-permute-done.4.refs_3_), custom_call_target="tpu_custom_call" | custom-call | tf_op jit(solution)/shard_map/paste/pallas_call | solution.py:652
  (19 shorter events, 0.0 us)
Async XLA Ops:
  0.6 5.5 %copy-start.6 = (f32[64,128]{1,0:T(8,128)S(1)}, f32[64,128]{1,0:T(8,128)}, u32[]{:S(2)}) copy-start(f32[64,128]{1,0:T(8,128)} %refs_2_.9) | copy-start | bytes 98308
  0.6 5.5 %copy-start.5 = (s32[192,384]{1,0:T(8,128)S(1)}, s32[192,384]{1,0:T(8,128)}, u32[]{:S(2)}) copy-start(s32[192,384]{1,0:T(8,128)} %refs_7_.5) | copy-start | bytes 884740
  0.7 5.5 %copy-start.4 = (s32[192,384]{1,0:T(8,128)S(1)}, s32[192,384]{1,0:T(8,128)}, u32[]{:S(2)}) copy-start(s32[192,384]{1,0:T(8,128)} %refs_6_.5) | copy-start | bytes 884740
  0.7 5.5 %copy-start.3 = (f32[192,384]{1,0:T(8,128)S(1)}, f32[192,384]{1,0:T(8,128)}, u32[]{:S(2)}) copy-start(f32[192,384]{1,0:T(8,128)} %refs_5_.6) | copy-start | bytes 884740
  0.7 5.5 %copy-start.2 = (f32[192,384]{1,0:T(8,128)S(1)}, f32[192,384]{1,0:T(8,128)}, u32[]{:S(2)}) copy-start(f32[192,384]{1,0:T(8,128)} %refs_4_.6) | copy-start | bytes 884740
  0.7 5.5 %copy-start.1 = (f32[192,384]{1,0:T(8,128)S(1)}, f32[192,384]{1,0:T(8,128)}, u32[]{:S(2)}) copy-start(f32[192,384]{1,0:T(8,128)} %refs_3_.6) | copy-start | bytes 884740
  0.7 5.5 %copy-start = (f32[192,384]{1,0:T(8,128)S(1)}, f32[192,384]{1,0:T(8,128)}, u32[]{:S(2)}) copy-start(f32[192,384]{1,0:T(8,128)} %refs_2_.7) | copy-start | bytes 884740
  0.7 5.5 %copy-start.10 = (s32[64,128]{1,0:T(8,128)S(1)}, s32[64,128]{1,0:T(8,128)}, u32[]{:S(2)}) copy-start(s32[64,128]{1,0:T(8,128)} %refs_5_.7) | copy-start | bytes 98308
  0.7 5.5 %copy-start.9 = (f32[64,128]{1,0:T(8,128)S(1)}, f32[64,128]{1,0:T(8,128)}, u32[]{:S(2)}) copy-start(f32[64,128]{1,0:T(8,128)} %refs_4_.7) | copy-start | bytes 98308
  0.7 5.5 %copy-start.8 = (f32[64,128]{1,0:T(8,128)S(1)}, f32[64,128]{1,0:T(8,128)}, u32[]{:S(2)}) copy-start(f32[64,128]{1,0:T(8,128)} %refs_3_.7) | copy-start | bytes 98308
  0.7 5.5 %copy-start.7 = (f32[64,128]{1,0:T(8,128)S(1)}, f32[64,128]{1,0:T(8,128)}, u32[]{:S(2)}) copy-start(f32[64,128]{1,0:T(8,128)} %refs_1_.7) | copy-start | bytes 98308
  3.3 3.0 %copy-start.11 = (f32[6]{0:T(128)S(1)}, f32[6]{0:T(128)}, u32[]{:S(2)}) copy-start(f32[6]{0:T(128)} %refs_0_.10) | copy-start | bytes 76
  3.3 5.4 %collective-permute-start = (f32[236,128]{1,0:T(8,128)}, f32[236,128]{1,0:T(8,128)S(1)}, u32[]{:S(2)}, u32[]{:S(2)}) collective-permute-start(f32[236,128]{1,0:T(8,128)} %get-tuple-element.29), channel_id=1, source_target_pairs={{0,4},{4,0},{8,12},{12,8},{1,5},{5,1},{9,13},{13,9},{2,6},{6,2},{1... | collective-permute-start | bytes 362504 | tf_op jit(solution)/shard_map/ppermute | solution.py:33
  5.5 1.9 %collective-permute-start.1 = (f32[20,128]{1,0:T(8,128)}, f32[20,128]{1,0:T(8,128)S(1)}, u32[]{:S(2)}, u32[]{:S(2)}) collective-permute-start(f32[20,128]{1,0:T(8,128)} %get-tuple-element.30), channel_id=1, source_target_pairs={{4,8},{8,4},{5,9},{9,5},{6,10},{10,6},{7,11},{11,7},{20,24},{24,20... | collective-permute-start | bytes 30728 | tf_op jit(solution)/shard_map/ppermute | solution.py:39
  8.9 4.5 %copy-start.12 = (s32[2]{0:T(128)S(1)}, s32[2]{0:T(128)}, u32[]{:S(2)}) copy-start(s32[2]{0:T(128)} %refs_0_.11) | copy-start | bytes 28
  8.9 12.0 %collective-permute-start.2 = (f32[208,128]{1,0:T(8,128)S(1)}, f32[208,128]{1,0:T(8,128)S(1)}, u32[]{:S(2)}, u32[]{:S(2)}) collective-permute-start(f32[208,128]{1,0:T(8,128)S(1)} %get-tuple-element.31), channel_id=1, source_target_pairs={{0,1},{1,0},{2,3},{3,2},{4,5},{5,4},{6,7},{7,6},{8,9},{9,8},{10,11... | collective-permute-start | bytes 319496 | tf_op jit(solution)/shard_map/ppermute | solution.py:33
  10.2 10.7 %collective-permute-start.3 = (f32[208,128]{1,0:T(8,128)S(1)}, f32[208,128]{1,0:T(8,128)S(1)}, u32[]{:S(2)}, u32[]{:S(2)}) collective-permute-start(f32[208,128]{1,0:T(8,128)S(1)} %get-tuple-element.32), channel_id=1, source_target_pairs={{1,2},{2,1},{5,6},{6,5},{9,10},{10,9},{13,14},{14,13},{17,18},{18,... | collective-permute-start | bytes 319496 | tf_op jit(solution)/shard_map/ppermute | solution.py:39
  24.9 7.2 %collective-permute-start.4 = (f32[64,128]{1,0:T(8,128)S(1)}, f32[64,128]{1,0:T(8,128)S(1)}, u32[]{:S(2)}, u32[]{:S(2)}) collective-permute-start(f32[64,128]{1,0:T(8,128)S(1)} %get-tuple-element.42.refs_2_), channel_id=1, source_target_pairs={{0,4},{4,8},{8,12},{1,5},{5,9},{9,13},{2,6},{6,10},{10,14},{3,7},{... | collective-permute-start | bytes 98312 | tf_op jit(solution)/shard_map/ppermute | solution.py:638

commit v3 on v2

--- a/solution.py
+++ b/solution.py
@@ -81,14 +81,15 @@
 
 def pack_rows_kernel(pairs_only, *refs):
     table, fine, ocean = refs[0], refs[1:7], refs[7:12]
-    outs = refs[12:14]
-    held, held_int, ocean_in, ocean_class, sems = refs[14:]
+    count = 1 if pairs_only else 2
+    outs, ocean_out = refs[12 : 12 + count], refs[12 + count]
+    held, held_int, ocean_in, ocean_class, sems = refs[13 + count :]
     rows, cols = fine[0].shape
     tiles = cols // LANES
     ocean_rows = ocean[0].shape[0]
     is_even = lax.rem(lax.axis_index("gx"), 2) == 0
     pairs = []
-    for side in range(1 if pairs_only else 2):
+    for side in range(count):
         last = is_even if side == 0 else jnp.logical_not(is_even)
         at = pl.multiple_of(jnp.where(last, rows - HALO, 0), 8)
         for f in range(6):
@@ -100,24 +101,23 @@
 
     for side, out in enumerate(outs):
         last = is_even if side == 0 else jnp.logical_not(is_even)
-        base = out.shape[0] - 5 * ITERS
-        if base > 0:
-            sources = [held.at[f, side] for f in range(4)] + [held_int.at[f, side] for f in range(2)]
-            for t in range(tiles):
-                at_cols = pl.ds(t * LANES, LANES)
-                low = fine_fields(sources, pl.ds(HALO - REACH, REACH), at_cols, table)
-                top = fine_fields(sources, pl.ds(0, REACH), at_cols, table)
-                for f in range(6):
-                    out[pl.ds((f * tiles + t) * REACH, REACH), :] = jnp.where(last, low[f], top[f])
-        sources = [ocean_in.at[j] for j in range(4)] + [ocean_class]
-        low = ocean_fields(sources, pl.ds(ocean_rows - ITERS, ITERS), pl.ds(0, LANES), table)
-        top = ocean_fields(sources, pl.ds(0, ITERS), pl.ds(0, LANES), table)
-        for j in range(5):
-            out[pl.ds(base + j * ITERS, ITERS), :] = jnp.where(last, low[j], top[j])
+        sources = [held.at[f, side] for f in range(4)] + [held_int.at[f, side] for f in range(2)]
+        for t in range(tiles):
+            at_cols = pl.ds(t * LANES, LANES)
+            low = fine_fields(sources, pl.ds(HALO - REACH, REACH), at_cols, table)
+            top = fine_fields(sources, pl.ds(0, REACH), at_cols, table)
+            for f in range(6):
+                out[pl.ds((f * tiles + t) * REACH, REACH), :] = jnp.where(last, low[f], top[f])
+    sources = [ocean_in.at[j] for j in range(4)] + [ocean_class]
+    low = ocean_fields(sources, pl.ds(ocean_rows - ITERS, ITERS), pl.ds(0, LANES), table)
+    top = ocean_fields(sources, pl.ds(0, ITERS), pl.ds(0, LANES), table)
+    for j in range(5):
+        outs[0][pl.ds(6 * tiles * REACH + j * ITERS, ITERS), :] = jnp.where(is_even, low[j], top[j])
+        ocean_out[pl.ds(j * ITERS, ITERS), :] = jnp.where(is_even, top[j], low[j])
 
 
 def halo_blocks(pairs_only, messages, block, gx_is_even):
-    rows = [message[pl.ds(block * REACH, REACH), :] for message in messages[: 1 if pairs_only else 2]]
+    rows = [message[pl.ds(block * REACH, REACH), :] for message in messages]
     gap = jnp.zeros((HALO - REACH, LANES), F32)
     if pairs_only:
         return [jnp.where(gx_is_even, jnp.concatenate([rows[0], gap], 0), jnp.concatenate([gap, rows[0]], 0))]
@@ -126,9 +126,12 @@
     return [jnp.concatenate([after, gap], 0), jnp.concatenate([gap, before], 0)]
 
 
-def ocean_halo(messages, j, gx_is_even):
-    even, odd = (m[pl.ds(m.shape[0] - (5 - j) * ITERS, ITERS), :] for m in messages)
+def ocean_halo(even, odd, gx_is_even):
     return jnp.where(gx_is_even, jnp.concatenate([even, odd], 0), jnp.concatenate([odd, even], 0))
+
+
+def ocean_part(message, j):
+    return message[pl.ds(message.shape[0] - (5 - j) * ITERS, ITERS), :]
 
 
 def packed_columns(parts):
@@ -154,27 +157,13 @@
     return jnp.where(lane < 32, first, moved)
 
 
-def prepare_kernel(*refs):
-    table, fine, ocean = refs[0], refs[1:7], refs[7:12]
-    even_out, odd_out, strip = refs[12:]
-    rows, cols = fine[0].shape
-    ocean_rows = ocean[0].shape[0]
-    for r in range(rows // 8):
-        row = pl.ds(8 * r, 8)
-        first = fine_fields(fine, row, pl.ds(0, LANES), table)
-        last = fine_fields(fine, row, pl.ds(cols - LANES, LANES), table)
-        values = ocean_fields(ocean, row, pl.ds(0, LANES), table) if 8 * r < ocean_rows else ()
-        even_out[row, :], odd_out[row, :] = packed_columns(columns_parts(first, last, values))
-        for f in range(6):
-            strip[f, row, :] = strip_lanes(first[f], last[f])
-
-
 def pack_columns_kernel(pairs_only, tiles, ocean_rows, *refs):
-    own, messages, outs = refs[:2], refs[2:4], refs[4:6]
+    own, messages, outs = refs[:2], refs[2:-2], refs[-2:]
     rows = own[0].shape[0]
     gx_is_even = lax.rem(lax.axis_index("gx"), 2) == 0
     extra = pl.ds(ocean_rows, 8)
-    values = [ocean_halo(messages, j, gx_is_even) for j in range(5)]
+    gap = jnp.zeros((ITERS, LANES), F32)
+    values = [ocean_halo(ocean_part(messages[0], j), gap, gx_is_even) for j in range(5)]
     parts = [(OLANE + ITERS * j, ITERS, v, v) for j, v in enumerate(values)]
     ocean_lanes = iota((8, LANES), 1) >= OLANE
     for out, mine, value in zip(outs, own, packed_columns(parts)):
@@ -260,7 +249,7 @@
                 g[t, pl.ds(8 + 8 * n, 8), :] = wet
 
 
-def flux_pass(tiles, n, e, g, x, y, kx, ky, ox, oy, fix, ring=True):
+def flux_pass(tiles, n, e, g, x, y, kx, ky, ox, oy, fix, ring=True, ghost=True):
     for r in range(n):
         here, after = pl.ds(8 + 8 * r, 8), pl.ds(9 + 8 * r, 8)
         eta = [e[t, here, :] for t in range(tiles)]
@@ -272,7 +261,7 @@
             )
             fx = fix(r, t, fx)
             x[t, here, :] = fx
-            if r == n - 1:
+            if ghost and r == n - 1:
                 x[t, pl.ds(0, 8), :] = fx
             y[t, here, :] = new_flux(
                 y[t, here, :], eta[t], eta_next[t], wet[t], wet_next[t], oy[t, here, :], ky[t, here, :]
@@ -295,10 +284,14 @@
     return gx, lax.div(gx, block_size), slot == 0, slot == block_size - 1
 
 
-def grid_edges(mx_tiles, own_offset, ocean_rows, spread_to, wf, rows, edges):
-    picks = iota((8, ocean_rows), 1) == jnp.where(iota((8, ocean_rows), 0) == 0, own_offset - 1, ocean_rows - 1)
-    picks = picks.astype(F32)
-    source = jnp.concatenate([dot(picks, tile) for tile in mx_tiles], 1)
+def grid_edges(ocean_mx, beyond, own_offset, ocean_rows, spread_to, wf, rows, edges):
+    at = own_offset - 1
+    own = [ocean_mx[pl.ds(at, 1), :] * SB, ocean_mx[ocean_rows - 1 : ocean_rows, :] * SB]
+    source = [jnp.concatenate(own + own * 3, 0)]
+    if beyond:
+        picks = iota((8, ocean_rows), 1) == jnp.where(iota((8, ocean_rows), 0) == 0, at, ocean_rows - 1)
+        source += [dot(picks.astype(F32), tile) for tile in beyond]
+    source = jnp.concatenate(source, 1)
     spread = dot(source, spread_to.astype(F32))
     for t in range(edges.shape[1]):
         cut = spread[:, t * LANES : (t + 1) * LANES]
@@ -311,62 +304,123 @@
 def run_coastal(tiles, n, rows, first, last, state, edges, ring):
     e, g, x, y, d, kx, ky, ox, oy = state
     sub = iota((8, LANES), 0)
+    ghost = n > rows // 8
     west_mask = (sub == 7) & first
     east_mask = (sub == 7) & last
 
     def fix(r, t, fx):
         if r == rows // 8 - 1:
             fx = jnp.where(east_mask, edges[1, t, :, :], fx)
-        if r == n - 1:
+        if ghost and r == n - 1:
             fx = jnp.where(west_mask, edges[0, t, :, :], fx)
         return fx
 
     for t in range(tiles):
-        x[t, pl.ds(0, 8), :] = jnp.where(west_mask, edges[0, t, :, :], x[t, pl.ds(8 * n, 8), :])
+        before = x[t, pl.ds(8 * n, 8), :] if ghost else 0.0
+        x[t, pl.ds(0, 8), :] = jnp.where(west_mask, edges[0, t, :, :], before)
 
     def step(_, carry):
         level_pass(tiles, n, e, g, x, y, d, ring)
-        flux_pass(tiles, n, e, g, x, y, kx, ky, ox, oy, fix, ring)
+        flux_pass(tiles, n, e, g, x, y, kx, ky, ox, oy, fix, ring, ghost)
         return carry
 
-    lax.fori_loop(0, FSTEPS, step, 0)
+    lax.fori_loop(0, FSTEPS, step, 0, unroll=4)
 
 
 def interior_kernel(block_size, *refs):
-    table, offsets, fine, ocean_mx = refs[0], refs[1], refs[2:8], refs[8]
-    pairs_only = block_size == 2
-    count = 1 if pairs_only else 2
-    messages = refs[9:11]
-    outs, out_means = refs[11:14], refs[14]
-    e, g, x, y, d, kf, wf, kx, ky, ox, oy, edges = refs[15:]
+    table, offsets, fine, ocean = refs[0], refs[1], refs[2:8], refs[8:13]
+    outs, (even_out, odd_out, strip) = refs[13:16], refs[16:19]
+    e, g, x, y, d, kf, wf, kx, ky, ox, oy, edges = refs[19:]
+    ocean_mx = ocean[1]
+    ocean_rows = ocean_mx.shape[0]
     rows, cols = fine[0].shape
     tiles = cols // LANES
-    n = rows // 8 + (HALO // 8) * count
+    n = rows // 8
     gx, grid, first, last = place_of(block_size)
-    gx_is_even = lax.rem(gx, 2) == 0
     dest = (e, x, y, d, kf, wf)
-    for r in range(rows // 8):
+    for r in range(n):
         src, here = pl.ds(8 * r, 8), pl.ds(8 + 8 * r, 8)
-        for t in range(tiles):
-            for f, value in enumerate(fine_fields(fine, src, pl.ds(t * LANES, LANES), table)):
-                dest[f][t, here, :] = value
-    for f in range(6):
-        for t in range(tiles):
-            for side, block in enumerate(halo_blocks(pairs_only, messages, f * tiles + t, gx_is_even)):
-                dest[f][t, pl.ds(8 + rows + HALO * side, HALO), :] = block
-
-    ocean_rows = ocean_mx.shape[0]
+        values = [fine_fields(fine, src, pl.ds(t * LANES, LANES), table) for t in range(tiles)]
+        for t in range(tiles):
+            for f in range(6):
+                dest[f][t, here, :] = values[t][f]
+        ocean_values = ocean_fields(ocean, src, pl.ds(0, LANES), table) if 8 * r < ocean_rows else ()
+        even_out[src, :], odd_out[src, :] = packed_columns(columns_parts(values[0], values[-1], ocean_values))
+        for f in range(6):
+            strip[f, src, :] = strip_lanes(values[0][f], values[-1][f])
+
     spread_to = iota((LANES, cols), 0) == lax.div(iota((LANES, cols), 1), R)
-    grid_edges([ocean_mx[...] * SB], offsets[grid], ocean_rows, spread_to, wf, rows, edges)
+    grid_edges(ocean_mx, [], offsets[grid], ocean_rows, spread_to, wf, rows, edges)
     prepare_faces(tiles, n, kf, wf, kx, ky, ox, oy, False)
     run_coastal(tiles, n, rows, first, last, (e, g, x, y, d, kx, ky, ox, oy), edges, False)
-    for r in range(rows // 8):
+    for r in range(n):
         to, here = pl.ds(8 * r, 8), pl.ds(8 + 8 * r, 8)
         for t in range(tiles):
             at_cols = pl.ds(t * LANES, LANES)
             outs[0][to, at_cols] = e[t, here, :] * (1.0 / SA)
             outs[1][to, at_cols] = x[t, here, :] * (1.0 / SB)
             outs[2][to, at_cols] = y[t, here, :] * (1.0 / SB)
+
+
+def rows_kernel(block_size, *refs):
+    table, offsets, fine = refs[0], refs[1], refs[2:8]
+    pairs_only = block_size == 2
+    count = 1 if pairs_only else 2
+    messages = refs[8 : 8 + count]
+    inner = refs[8 + count : 11 + count]
+    outs, out_means = refs[11 + count : 14 + count], refs[14 + count]
+    e, g, x, y, d, kf, wf, kx, ky, ox, oy = refs[15 + count :]
+    rows, cols = fine[0].shape
+    ocean_rows = out_means.shape[0]
+    tiles = cols // LANES
+    near = 2 * REACH // 8
+    n = near + HALO // 8
+    gx, grid, first, last = place_of(block_size)
+    gx_is_even = lax.rem(gx, 2) == 0
+    sub = iota((8, LANES), 0)
+    dest = (e, x, y, d, kf, wf)
+    for i in range(3):
+        outs[i][...] = inner[i][...]
+
+    for side in range(count):
+        to_next = gx_is_even if pairs_only else side == 0
+        start = jnp.where(to_next, rows - 8 * near, 0) if pairs_only else (rows - 8 * near) * (side == 0)
+        for r in range(near):
+            src = pl.ds(pl.multiple_of(start + 8 * r, 8), 8) if pairs_only else pl.ds(start + 8 * r, 8)
+            for t in range(tiles):
+                for f, value in enumerate(fine_fields(fine, src, pl.ds(t * LANES, LANES), table)):
+                    dest[f][t, pl.ds(8 + 8 * r, 8), :] = value
+        for f in range(6):
+            for t in range(tiles):
+                block = halo_blocks(pairs_only, messages, f * tiles + t, gx_is_even)[side]
+                dest[f][t, pl.ds(8 + 8 * near, HALO), :] = block
+        prepare_faces(tiles, n, kf, wf, kx, ky, ox, oy, False)
+        for t in range(tiles):
+            x[t, pl.ds(0, 8), :] = x[t, pl.ds(8 * n, 8), :]
+
+        def step(_, carry):
+            level_pass(tiles, n, e, g, x, y, d, False)
+            flux_pass(tiles, n, e, g, x, y, kx, ky, ox, oy, lambda r, t, fx: fx, False)
+            return carry
+
+        lax.fori_loop(0, FSTEPS, step, 0, unroll=4)
+
+        open_end = jnp.logical_not(jnp.where(to_next, last, first))
+        for half in range(2):
+            if pairs_only:
+                src = pl.multiple_of(jnp.where(to_next, 8 * (near - 2 + half), 8 * half), 8)
+                to = pl.multiple_of(jnp.where(to_next, rows - HALO + 8 * half, 8 * half), 8)
+            else:
+                src = 8 * (near - 2 + half) if to_next else 8 * half
+                to = rows - HALO + 8 * half if to_next else 8 * half
+            depth_in = jnp.where(to_next, HALO - 1 - (sub + 8 * half), sub + 8 * half)
+            take = (depth_in < FSTEPS) & open_end
+            for i, (held, scale) in enumerate(((e, 1.0 / SA), (x, 1.0 / SB), (y, 1.0 / SB))):
+                for t in range(tiles):
+                    at_cols = pl.ds(t * LANES, LANES)
+                    value = held[t, pl.ds(8 + src, 8), :] * scale
+                    outs[i][pl.ds(to, 8), at_cols] = jnp.where(take, value, outs[i][pl.ds(to, 8), at_cols])
+
     gather_cols = (lax.div(iota((cols, LANES), 0), R) == iota((cols, LANES), 1)).astype(F32)
     out_means[...] = coarse_means(outs[0][...], gather_cols, offsets[grid], ocean_rows)
 
@@ -379,11 +433,12 @@
 
 
 def border_kernel(block_size, cols, *refs):
-    offsets, strip, ocean_mx, messages = refs[0], refs[1], refs[2], refs[3:5]
-    gy_even, gy_odd, inner_means = refs[5:8]
-    outs, out_means = refs[8:11], refs[11]
-    e, g, x, y, d, kf, wf, kx, ky, ox, oy, edges = refs[12:]
     pairs_only = block_size == 2
+    count = 1 if pairs_only else 2
+    offsets, strip, ocean_mx, messages = refs[0], refs[1], refs[2], refs[3 : 3 + count]
+    gy_even, gy_odd, ocean_odd, inner_means = refs[3 + count : 7 + count]
+    outs, out_even, out_odd = refs[7 + count : 10 + count], refs[10 + count], refs[11 + count]
+    e, g, x, y, d, kf, wf, kx, ky, ox, oy, edges = refs[12 + count :]
     rows = strip.shape[1]
     own = cols // LANES
     n = rows // 8 + (HALO // 8) * (1 if pairs_only else 2)
@@ -427,7 +482,7 @@
     wanted = jnp.where(to < 64, wanted, jnp.where(to < 80, LANES + lax.div(to - 64, R), 0))
     wanted = jnp.where(to < LANES - 16, wanted, 2 * LANES - 1 - lax.div(LANES - 1 - to, R))
     spread_to = iota((2 * LANES, LANES), 0) == wanted
-    grid_edges([ocean_mx[...] * SB, mx_halo], offsets[grid], ocean_rows, spread_to, wf, rows, edges)
+    grid_edges(ocean_mx, [mx_halo], offsets[grid], ocean_rows, spread_to, wf, rows, edges)
     prepare_faces(1, n, kf, wf, kx, ky, ox, oy)
     run_coastal(1, n, rows, first, last, (e, g, x, y, d, kx, ky, ox, oy), edges, True)
 
@@ -439,10 +494,19 @@
     gather = ((lax.div(column, R) == target) & inside).astype(F32)
     means = coarse_means(outs[0][...], gather, offsets[grid], ocean_rows)
     col = iota((ocean_rows, LANES), 1)
-    out_means[...] = jnp.where((col < ITERS) | (col >= LANES - ITERS), means, inner_means[...])
-
-
-def finish_coastal(inner, strips, final, outs, sems):
+    means = jnp.where((col < ITERS) | (col >= LANES - ITERS), means, inner_means[...])
+    out_even[...] = means
+    out_odd[0:ocean_rows, :] = means
+    out_odd[ocean_rows : ocean_rows + 5 * ITERS, :] = ocean_odd[...]
+    for k, side in enumerate((gy_even, gy_odd)):
+        corner = jnp.where(gx_is_even, side[0:ITERS, :], side[ocean_rows - ITERS : ocean_rows, :])
+        out_odd[pl.ds(ocean_rows + (5 + k) * ITERS, ITERS), :] = corner
+
+
+def finish_kernel(*refs):
+    inner, strips, table, ocean = refs[0:3], refs[3:6], refs[6], refs[7:12]
+    gy_even, gy_odd, gx_even = refs[12:15]
+    outs, state, final, sems = refs[15:18], refs[18], refs[19], refs[20]
     rows, cols = final.shape[1:]
     own = cols // LANES
     lane = iota((8, LANES), 1)
@@ -460,44 +524,54 @@
                     kept = jnp.where(lane >= LANES - FSTEPS, roll_to(value, 32, LANES - 32), kept)
                 final[i, to, at_cols] = kept
         copies[i].start()
-    return copies
-
-
-def finish_kernel(*refs):
-    table, ocean = refs[0], refs[1:6]
-    gy_even, gy_odd, gx_even, gx_odd = refs[6:10]
-    inner, strips = refs[10:13], refs[13:16]
-    fine_outs, (out_eta, out_x, out_y) = refs[16:19], refs[19:22]
-    final, sems = refs[22:24]
-    e, g, x, y, d, kf, kx, ky, ox, oy = refs[24:]
-    copies = finish_coastal(inner, strips, final, fine_outs, sems)
-    rows, cols = ocean[0].shape
+
+    ocean_rows = ocean[0].shape[0]
+    gx_is_even = lax.rem(lax.axis_index("gx"), 2) == 0
+    for r in range(ocean_rows // 8):
+        src = pl.ds(8 * r, 8)
+        for j, value in enumerate(ocean_fields(ocean, src, pl.ds(0, LANES), table)):
+            state[j, 0, src, :] = value
+            state[j, 1, src, :] = unpack_ocean(gy_even[src, :], gy_odd[src, :], j)
+    halo = pl.ds(ocean_rows, 8)
+    gap = jnp.zeros((ITERS, LANES), F32)
+    for j in range(5):
+        state[j, 0, halo, :] = ocean_halo(ocean_part(gx_even, j), gap, gx_is_even)
+        state[j, 1, halo, :] = unpack_ocean(gy_even[halo, :], gy_odd[halo, :], j)
+    for copy in copies:
+        copy.wait()
+
+
+def unpack_ocean(from_even, from_odd, j):
+    gy_is_even = lax.rem(lax.axis_index("gy"), 2) == 0
+    lane = iota((8, LANES), 1)
+    from_east = jnp.where(gy_is_even, from_even, from_odd)
+    from_west = jnp.where(gy_is_even, from_odd, from_even)
+    east = roll_to(from_east, OLANE + ITERS * j, 0)
+    west = roll_to(from_west, OLANE + ITERS * j, LANES - ITERS)
+    return jnp.where(lane < ITERS, east, jnp.where(lane >= LANES - ITERS, west, 0.0))
+
+
+def ocean_kernel(block_size, *refs):
+    offsets, state, rolled, got_even, got_odd = refs[:5]
+    out_eta, out_x, out_y = refs[5:8]
+    e, g, x, y, d, kf, kx, ky, ox, oy = refs[8:]
+    rows, cols = out_eta.shape
     tiles = 2
     n = rows // 8 + 1
     gx, gy = lax.axis_index("gx"), lax.axis_index("gy")
     gx_is_even = lax.rem(gx, 2) == 0
-    gy_is_even = lax.rem(gy, 2) == 0
     lane = iota((8, LANES), 1)
     sub = iota((8, LANES), 0)
-
-    def unpack(from_even, from_odd, j):
-        from_east = jnp.where(gy_is_even, from_even, from_odd)
-        from_west = jnp.where(gy_is_even, from_odd, from_even)
-        east = roll_to(from_east, OLANE + ITERS * j, 0)
-        west = roll_to(from_west, OLANE + ITERS * j, LANES - 4)
-        return jnp.where(lane < 4, east, jnp.where(lane >= LANES - 4, west, 0.0))
-
-    dest = (e, x, y, d, kf)
-    for r in range(rows // 8):
-        src, here = pl.ds(8 * r, 8), pl.ds(8 + 8 * r, 8)
-        for j, value in enumerate(ocean_fields(ocean, src, pl.ds(0, LANES), table)):
-            dest[j][0, here, :] = value
-            dest[j][1, here, :] = unpack(gy_even[src, :], gy_odd[src, :], j)
-
-    here, halo = pl.ds(8 + rows, 8), pl.ds(rows, 8)
-    for j in range(5):
-        dest[j][0, here, :] = ocean_halo((gx_even, gx_odd), j, gx_is_even)
-        dest[j][1, here, :] = unpack(gy_even[halo, :], gy_odd[halo, :], j)
+    here = pl.ds(8 + rows, 8)
+    gap = jnp.zeros((ITERS, LANES), F32)
+    corners = [got_odd[pl.ds(rows + (5 + k) * ITERS, ITERS), :] for k in range(2)]
+    corners = [ocean_halo(gap, corner, gx_is_even) for corner in corners]
+    for j, field in enumerate((e, x, y, d, kf)):
+        for t in range(tiles):
+            field[t, 8 : 8 + rows + 8, :] = state[j, t]
+        odd = ocean_halo(gap, got_odd[pl.ds(rows + j * ITERS, ITERS), :], gx_is_even)
+        field[0, here, :] = field[0, here, :] + odd
+        field[1, here, :] = field[1, here, :] + unpack_ocean(*corners, j)
 
     prepare_faces(tiles, n, kf, None, kx, ky, None, None)
     rows_total, cols_total = rows * lax.axis_size("gx"), cols * lax.axis_size("gy")
@@ -518,25 +592,18 @@
         flux_pass(tiles, n, e, g, x, y, kx, ky, ox, oy, lambda r, t, fx: fx)
         return carry
 
-    lax.fori_loop(0, ITERS, step, 0)
+    lax.fori_loop(0, ITERS, step, 0, unroll=4)
+    _, grid, _, _ = place_of(block_size)
+    own_offset = offsets[grid]
+    left_offset = jnp.where(gx >= 1, offsets[lax.div(jnp.maximum(gx - 1, 0), block_size)], 0)
     for r in range(rows // 8):
         to, here = pl.ds(8 * r, 8), pl.ds(8 + 8 * r, 8)
-        out_eta[to, :] = e[0, here, :] * (1.0 / SA)
+        row = sub + 8 * r
+        arrived = jnp.where(gx_is_even, got_odd[to, :], got_even[to, :])
+        level = jnp.where(row < left_offset, arrived, e[0, here, :] * (1.0 / SA))
+        out_eta[to, :] = jnp.where(row >= own_offset, rolled[to, :], level)
         out_x[to, :] = x[0, here, :] * (1.0 / SB)
         out_y[to, :] = y[0, here, :] * (1.0 / SB)
-    for copy in copies:
-        copy.wait()
-
-
-def paste_kernel(block_size, *refs):
-    offsets, eta, rolled, arrived, out = refs
-    gx, grid, _, _ = place_of(block_size)
-    own_offset = offsets[grid]
-    left_offset = jnp.where(gx >= 1, offsets[lax.div(jnp.maximum(gx - 1, 0), block_size)], 0)
-    row = iota(eta.shape, 0)
-    out[...] = jnp.where(
-        row >= own_offset, rolled[...], jnp.where(row < left_offset, arrived[...], eta[...])
-    )
 
 
 def shape(*dims):
@@ -575,12 +642,13 @@
         return pltpu.VMEM(dims, dtype)
 
     count = 1 if pairs_only else 2
-    both = 6 * own * REACH + 5 * ITERS
-    gx_even, gx_odd = pl.pallas_call(
+    fine_length, ocean_length = 6 * own * REACH, 5 * ITERS
+    lengths = [fine_length + ocean_length, fine_length][:count] + [ocean_length]
+    *gx_fine, ocean_odd = pl.pallas_call(
         functools.partial(pack_rows_kernel, pairs_only),
-        out_shape=(shape(both, LANES), shape(5 * ITERS if pairs_only else both, LANES)),
+        out_shape=tuple(shape(length, LANES) for length in lengths),
         in_specs=[SMEM] + [ANY] * 11,
-        out_specs=(VMEM,) * 2,
+        out_specs=(VMEM,) * len(lengths),
         scratch_shapes=[
             vmem(4, count, HALO, cols),
             vmem(2, count, HALO, cols, dtype=jnp.int32),
@@ -590,73 +658,76 @@
         ],
         name="pack_rows",
     )(manning, *fine, *ocean)
-    gx_even = swap_even(gx_even, "gx")
-    gx_odd = swap_odd(gx_odd, "gx")
-
-    own_even, own_odd, strip = pl.pallas_call(
-        prepare_kernel,
-        out_shape=(shape(rows, LANES),) * 2 + (shape(6, rows, LANES),),
-        in_specs=[SMEM] + [VMEM] * 11,
-        out_specs=(VMEM,) * 3,
+    gx_fine = [swap(message, "gx") for swap, message in zip((swap_even, swap_odd), gx_fine)]
+
+    *inner, own_even, own_odd, strip = pl.pallas_call(
+        functools.partial(interior_kernel, block_size),
+        out_shape=(shape(rows, cols),) * 3 + (shape(rows, LANES),) * 2 + (shape(6, rows, LANES),),
+        in_specs=[SMEM, SMEM] + [VMEM] * 11,
+        out_specs=(VMEM,) * 6,
+        scratch_shapes=[vmem(own, rows + 16, LANES)] * 11 + [vmem(2, own, 8, LANES)],
         compiler_params=params(),
-        cost_estimate=pl.CostEstimate(flops=0, bytes_accessed=5_000_000, transcendentals=0),
-        name="prepare",
-    )(manning, *fine, *ocean)
+        cost_estimate=pl.CostEstimate(flops=0, bytes_accessed=20_000_000, transcendentals=0),
+        name="interior",
+    )(manning, fine_offset, *fine, *ocean)
 
     n = rows // 8 + (HALO // 8) * count
     gy_even, gy_odd = pl.pallas_call(
         functools.partial(pack_columns_kernel, pairs_only, own, ocean_rows),
         out_shape=(shape(8 * n, LANES),) * 2,
-        in_specs=[VMEM] * 4,
+        in_specs=[VMEM] * (2 + count),
         out_specs=(VMEM,) * 2,
         compiler_params=params(),
         name="pack_columns",
-    )(own_even, own_odd, gx_even, gx_odd)
+    )(own_even, own_odd, *gx_fine)
     gy_even = swap_even(gy_even, "gy")
     gy_odd = swap_odd(gy_odd, "gy")
 
     *inner, means = pl.pallas_call(
-        functools.partial(interior_kernel, block_size),
+        functools.partial(rows_kernel, block_size),
         out_shape=(shape(rows, cols),) * 3 + (shape(ocean_rows, ocean_cols),),
-        in_specs=[SMEM, SMEM] + [VMEM] * 9,
+        in_specs=[SMEM, SMEM] + [VMEM] * (9 + count),
         out_specs=(VMEM,) * 4,
-        scratch_shapes=[vmem(own, 8 * n + 16, LANES)] * 11 + [vmem(2, own, 8, LANES)],
+        scratch_shapes=[vmem(own, 2 * REACH + HALO + 16, LANES)] * 11,
         compiler_params=params(),
-        cost_estimate=pl.CostEstimate(flops=0, bytes_accessed=20_000_000, transcendentals=0),
-        name="interior",
-    )(manning, fine_offset, *fine, ocean_mx, gx_even, gx_odd)
-
-    *strips, rolled = pl.pallas_call(
+        cost_estimate=pl.CostEstimate(flops=0, bytes_accessed=10_000_000, transcendentals=0),
+        name="rows",
+    )(manning, fine_offset, *fine, *gx_fine, *inner)
+
+    odd_length = ocean_rows + 7 * ITERS
+    *strips, rolled, to_odd = pl.pallas_call(
         functools.partial(border_kernel, block_size, cols),
-        out_shape=(shape(rows, LANES),) * 3 + (shape(ocean_rows, ocean_cols),),
-        in_specs=[SMEM] + [VMEM] * 7,
-        out_specs=(VMEM,) * 4,
+        out_shape=(shape(rows, LANES),) * 3 + (shape(ocean_rows, ocean_cols), shape(odd_length, LANES)),
+        in_specs=[SMEM] + [VMEM] * (6 + count),
+        out_specs=(VMEM,) * 5,
         scratch_shapes=[vmem(1, 8 * n + 16, LANES)] * 11 + [vmem(2, 1, 8, LANES)],
         compiler_params=params(),
         name="border",
-    )(fine_offset, strip, ocean_mx, gx_even, gx_odd, gy_even, gy_odd, means)
-    arrived = lax.ppermute(rolled, "gx", [(i, i + 1) for i in range(gx_count - 1)])
+    )(fine_offset, strip, ocean_mx, *gx_fine, gy_even, gy_odd, ocean_odd, means)
+    got_even = swap_even(rolled, "gx")
+    got_odd = swap_odd(to_odd, "gx")
 
     n = ocean_rows // 8 + 1
-    feta, fqx, fqy, eta, mx, ny = pl.pallas_call(
+    feta, fqx, fqy, state = pl.pallas_call(
         finish_kernel,
-        out_shape=(shape(rows, cols),) * 3 + (shape(ocean_rows, ocean_cols),) * 3,
-        in_specs=[SMEM] + [VMEM] * 15,
-        out_specs=(ANY,) * 3 + (VMEM,) * 3,
-        scratch_shapes=[vmem(3, rows, cols), pltpu.SemaphoreType.DMA((3,))] + [vmem(2, 8 * n + 16, LANES)] * 10,
+        out_shape=(shape(rows, cols),) * 3 + (shape(5, 2, 8 * n, LANES),),
+        in_specs=[VMEM] * 6 + [SMEM] + [VMEM] * 8,
+        out_specs=(ANY,) * 3 + (VMEM,),
+        scratch_shapes=[vmem(3, rows, cols), pltpu.SemaphoreType.DMA((3,))],
         compiler_params=params(),
         cost_estimate=pl.CostEstimate(flops=0, bytes_accessed=5_000_000, transcendentals=0),
         name="finish",
-    )(manning, *ocean, gy_even, gy_odd, gx_even, gx_odd, *inner, *strips)
-
-    eta = pl.pallas_call(
-        functools.partial(paste_kernel, block_size),
-        out_shape=shape(ocean_rows, ocean_cols),
-        in_specs=[SMEM] + [VMEM] * 3,
-        out_specs=VMEM,
+    )(*inner, *strips, manning, *ocean, gy_even, gy_odd, gx_fine[0])
+
+    eta, mx, ny = pl.pallas_call(
+        functools.partial(ocean_kernel, block_size),
+        out_shape=(shape(ocean_rows, ocean_cols),) * 3,
+        in_specs=[SMEM] + [VMEM] * 4,
+        out_specs=(VMEM,) * 3,
+        scratch_shapes=[vmem(2, 8 * n + 16, LANES)] * 10,
         compiler_params=params(),
-        name="paste",
-    )(fine_offset, eta, rolled, arrived)
+        name="ocean",
+    )(fine_offset, state, rolled, got_even, got_odd)
     return (eta, mx, ny, feta, fqx, fqy)
 
 

time: 33.5 us -> 31.4 us (0.937)
  starting transfers between devices: 12.2 us -> 10.8 us
  waiting for transfers between devices: 1.37 us -> 0.01 us
  Pallas kernels: 18.7 us -> 19.4 us
    ppermute x1 -> x0, starting transfers between devices: 4.86 us -> none  [shards(): lax.ppermute(rolled, 'gx', [(i, i + 1) for i in range(gx_count - 1)])]
    ppermute x2 -> x3, starting transfers between devices: 3.49 us -> 7.11 us  [swap_even(): lax.ppermute(value, axis, [(i, i ^ 1) for i in range(count) if i ^ 1 < co...]
    pallas_call x2, Pallas kernels: 2.28 us -> 5.49 us  [the longest x1 3.54 us: shards(): pl.pallas_call(functools.partial(rows_kernel, block_size), out_shape=(sha...]
    pallas_call x1, Pallas kernels: 7.52 us -> 6 us  [shards(): pl.pallas_call(functools.partial(interior_kernel, block_size), out_shape=...]
    ppermute x2 -> x3, waiting for transfers between devices: 1.37 us -> 0.01 us  [swap_even(): lax.ppermute(value, axis, [(i, i ^ 1) for i in range(count) if i ^ 1 < co...]
    pallas_call x1, Pallas kernels: 2.35 us -> 1.57 us  [shards(): pl.pallas_call(finish_kernel, out_shape=(shape(rows, cols),) * 3 + (shape...]
  transfers between devices with their start and end apart: 5 -> 5, of which waited for: 1 -> 0; matrix products, arithmetic and copies ran while one was open for 0% -> 0% of each run, Pallas kernels for 33% -> 36%
where the time goes in v3:
time: 31.4 us; the launch traced here: 31.2 us
  Pallas kernels  19.4 us (62%)
  starting transfers between devices  10.8 us (34%)
  between operations  0.93 us (3%)
    ppermute x3, starting transfers between devices, swap_even(): lax.ppermute(value, axis, [(i, i ^ 1) for i in range(count) if i ^ 1 < co...  7.11 us
    pallas_call x1, Pallas kernels, shards(): pl.pallas_call(functools.partial(interior_kernel, block_size), out_shape=...  6 us
    pallas_call x1, Pallas kernels, shards(): pl.pallas_call(functools.partial(border_kernel, block_size, cols), out_sh...  3.75 us
    ppermute x2, starting transfers between devices, swap_odd(): return lax.ppermute(value, axis, [(a, b) for a, b in pairs if b < count])  3.68 us
    pallas_call x1, Pallas kernels, shards(): pl.pallas_call(functools.partial(rows_kernel, block_size), out_shape=(sha...  3.54 us
    pallas_call x1, Pallas kernels, shards(): pl.pallas_call(functools.partial(pack_rows_kernel, pairs_only), out_shape...  2.52 us
    pallas_call x1, Pallas kernels, shards(): pl.pallas_call(functools.partial(ocean_kernel, block_size), out_shape=(sh...  1.95 us
    pallas_call x1, Pallas kernels, shards(): pl.pallas_call(finish_kernel, out_shape=(shape(rows, cols),) * 3 + (shape...  1.57 us
  transfers between devices with their start and end apart: 5, of which 0 were waited for; matrix products, arithmetic and copies ran while one was open for 0% of the time, Pallas kernels for 36%

profile of v3, /device:TPU:1, one launch (start us, length us, event | category | flops | bytes accessed | tf_op | source)
XLA Modules:
  0.0 31.2 jit_solution(17676170556503509545)
XLA Ops:
  0.6 0.0 copy-start.6
  0.6 0.0 copy-start.5
  0.7 0.0 copy-start.4
  0.7 0.0 copy-start.3
  0.7 2.5 %pack_rows.1 = (f32[236,128]{1,0:T(8,128)}, f32[20,128]{1,0:T(8,128)}) custom-call(f32[6]{0:T(128)} %refs_6_.7, f32[192,384]{1,0:T(8,128)} %refs_2_.6, f32[192,384]{1,0:T(8,128)} %refs_3_.5, f32[192,384]{1,0:T(8,128)} %refs_4_.5, f32[192,384]{1,0:T(8,128)} %refs_5_.5, s32[192,384]{1,0:T(8,128)} %refs_6_.6, s32[192,384]{1,0:T(8,128)} %refs_7_.6, ...), custom_call_target="tpu_custom_call" | custom-call | tf_op jit(solution)/shard_map/pack_rows/pallas_call | solution.py:647
  3.3 0.0 copy-start.12
  3.3 0.0 copy-start.13
  3.3 2.2 %collective-permute-start = (f32[236,128]{1,0:T(8,128)}, f32[236,128]{1,0:T(8,128)S(1)}, u32[]{:S(2)}, u32[]{:S(2)}) collective-permute-start(f32[236,128]{1,0:T(8,128)} %get-tuple-element.32), channel_id=1, source_target_pairs={{0,4},{4,0},{8,12},{12,8},{1,5},{5,1},{9,13},{13,9},{2,6},{6,2},{1... | collective-permute-start | bytes 362504 | tf_op jit(solution)/shard_map/ppermute | solution.py:33
  5.6 6.0 %interior.1 = (f32[192,384]{1,0:T(8,128)S(1)}, f32[192,384]{1,0:T(8,128)S(1)}, f32[192,384]{1,0:T(8,128)S(1)}, f32[192,128]{1,0:T(8,128)S(1)}, f32[192,128]{1,0:T(8,128)S(1)}, /*index=5*/f32[6,192,128]{2,1,0:T(8,128)S(1)}) custom-call(f32[6]{0:T(128)S(1)} %copy-done.13, s32[2]{0:T(128)S(1)} %copy-done.12, f32[192,384]{1,0:T(8,128)S(1)} %copy-done, ...), custom_call_target="tpu_custom_call" | custom-call | bytes 20000000 | tf_op jit(solution)/shard_map/interior/pallas_call | solution.py:663
  11.6 0.0 collective-permute-done.refs_8_.refs_2_.refs_3_.refs_14_
  11.6 0.1 pack_columns.1
  11.7 1.0 %collective-permute-start.1 = (f32[208,128]{1,0:T(8,128)S(1)}, f32[208,128]{1,0:T(8,128)S(1)}, u32[]{:S(2)}, u32[]{:S(2)}) collective-permute-start(f32[208,128]{1,0:T(8,128)S(1)} %get-tuple-element.42), channel_id=1, source_target_pairs={{0,1},{1,0},{2,3},{3,2},{4,5},{5,4},{6,7},{7,6},{8,9},{9,8},{10,11... | collective-permute-start | bytes 319496 | tf_op jit(solution)/shard_map/ppermute | solution.py:33
  12.8 3.0 %collective-permute-start.2 = (f32[208,128]{1,0:T(8,128)S(1)}, f32[208,128]{1,0:T(8,128)S(1)}, u32[]{:S(2)}, u32[]{:S(2)}) collective-permute-start(f32[208,128]{1,0:T(8,128)S(1)} %get-tuple-element.43), channel_id=1, source_target_pairs={{1,2},{2,1},{5,6},{6,5},{9,10},{10,9},{13,14},{14,13},{17,18},{18,... | collective-permute-start | bytes 319496 | tf_op jit(solution)/shard_map/ppermute | solution.py:39
  15.8 0.0 copy-start.11
  15.8 3.5 %rows.1 = (f32[192,384]{1,0:T(8,128)S(1)}, f32[192,384]{1,0:T(8,128)S(1)}, f32[192,384]{1,0:T(8,128)S(1)}, f32[64,128]{1,0:T(8,128)S(1)}) custom-call(f32[6]{0:T(128)S(1)} %copy-done.13, s32[2]{0:T(128)S(1)} %copy-done.12, f32[192,384]{1,0:T(8,128)S(1)} %copy-done, f32[192,384]{1,0:T(8,128)S(1)} %copy-done.1, f32[192,384]{1,0:T(8,128)S(1)} %copy-done.2, ...), custom_call_target="tpu_custom_call" | custom-call | bytes 10000000 | tf_op jit(solution)/shard_map/rows/pallas_call | solution.py:686
  19.3 0.0 collective-permute-done.1.refs_4_.refs_12_
  19.4 0.0 collective-permute-done.2.refs_5_.refs_13_
  19.4 3.7 %border.1 = (f32[192,128]{1,0:T(8,128)S(1)}, f32[192,128]{1,0:T(8,128)S(1)}, f32[192,128]{1,0:T(8,128)S(1)}, f32[64,128]{1,0:T(8,128)S(1)}, f32[92,128]{1,0:T(8,128)S(1)}) custom-call(s32[2]{0:T(128)S(1)} %copy-done.12, f32[6,192,128]{2,1,0:T(8,128)S(1)} %get-tuple-element.39.refs_1_, f32[64,128]{1,0:T(8,128)S(1)} %copy-done.6, ...), custom_call_target="tpu_custom_call" | custom-call | tf_op jit(solution)/shard_map/border/pallas_call | solution.py:698
  23.1 0.7 %collective-permute-start.4 = (f32[92,128]{1,0:T(8,128)S(1)}, f32[92,128]{1,0:T(8,128)S(1)}, u32[]{:S(2)}, u32[]{:S(2)}) collective-permute-start(f32[92,128]{1,0:T(8,128)S(1)} %get-tuple-element.51), channel_id=1, source_target_pairs={{4,8},{8,4},{5,9},{9,5},{6,10},{10,6},{7,11},{11,7},{20,24},{24,20... | collective-permute-start | bytes 141320 | tf_op jit(solution)/shard_map/ppermute | solution.py:39
  23.8 3.9 %collective-permute-start.3 = (f32[64,128]{1,0:T(8,128)S(1)}, f32[64,128]{1,0:T(8,128)S(1)}, u32[]{:S(2)}, u32[]{:S(2)}) collective-permute-start(f32[64,128]{1,0:T(8,128)S(1)} %get-tuple-element.50.refs_2_), channel_id=1, source_target_pairs={{0,4},{4,0},{8,12},{12,8},{1,5},{5,1},{9,13},{13,9},{2,6},{6,2},{1... | collective-permute-start | bytes 98312 | tf_op jit(solution)/shard_map/ppermute | solution.py:33
  27.7 1.6 %finish.1 = (f32[192,384]{1,0:T(8,128)}, f32[192,384]{1,0:T(8,128)}, f32[192,384]{1,0:T(8,128)}, f32[5,2,72,128]{3,2,1,0:T(8,128)S(1)}) custom-call(f32[192,384]{1,0:T(8,128)S(1)} %get-tuple-element.36.refs_0_, f32[192,384]{1,0:T(8,128)S(1)} %get-tuple-element.37.refs_1_, f32[192,384]{1,0:T(8,128)S(1)} %get-tuple-element.38.refs_2_, ...), custom_call_target="tpu_custom_call" | custom-call | bytes 5000000 | tf_op jit(solution)/shard_map/finish/pallas_call | solution.py:711
  29.3 0.0 collective-permute-done.3.refs_3_
  29.3 0.0 collective-permute-done.4.refs_4_
  29.3 1.9 %ocean.1 = (f32[64,128]{1,0:T(8,128)}, f32[64,128]{1,0:T(8,128)}, f32[64,128]{1,0:T(8,128)}) custom-call(s32[2]{0:T(128)S(1)} %copy-done.12, f32[5,2,72,128]{3,2,1,0:T(8,128)S(1)} %get-tuple-element.49.refs_1_, f32[64,128]{1,0:T(8,128)S(1)} %get-tuple-element.50.refs_2_, f32[64,128]{1,0:T(8,128)S(1)} %collective-permute-done.3.refs_3_, ...), custom_call_target="tpu_custom_call" | custom-call | tf_op jit(solution)/shard_map/ocean/pallas_call | solution.py:722
  (21 shorter events, 0.0 us)
Async XLA Ops:
  0.6 4.9 %copy-start.6 = (f32[64,128]{1,0:T(8,128)S(1)}, f32[64,128]{1,0:T(8,128)}, u32[]{:S(2)}) copy-start(f32[64,128]{1,0:T(8,128)} %refs_8_.5) | copy-start | bytes 98308
  0.6 4.9 %copy-start.5 = (s32[192,384]{1,0:T(8,128)S(1)}, s32[192,384]{1,0:T(8,128)}, u32[]{:S(2)}) copy-start(s32[192,384]{1,0:T(8,128)} %refs_7_.6) | copy-start | bytes 884740
  0.7 4.8 %copy-start.4 = (s32[192,384]{1,0:T(8,128)S(1)}, s32[192,384]{1,0:T(8,128)}, u32[]{:S(2)}) copy-start(s32[192,384]{1,0:T(8,128)} %refs_6_.6) | copy-start | bytes 884740
  0.7 4.8 %copy-start.3 = (f32[192,384]{1,0:T(8,128)S(1)}, f32[192,384]{1,0:T(8,128)}, u32[]{:S(2)}) copy-start(f32[192,384]{1,0:T(8,128)} %refs_5_.5) | copy-start | bytes 884740
  0.7 4.8 %copy-start.2 = (f32[192,384]{1,0:T(8,128)S(1)}, f32[192,384]{1,0:T(8,128)}, u32[]{:S(2)}) copy-start(f32[192,384]{1,0:T(8,128)} %refs_4_.5) | copy-start | bytes 884740
  0.7 4.8 %copy-start.1 = (f32[192,384]{1,0:T(8,128)S(1)}, f32[192,384]{1,0:T(8,128)}, u32[]{:S(2)}) copy-start(f32[192,384]{1,0:T(8,128)} %refs_3_.5) | copy-start | bytes 884740
  0.7 4.8 %copy-start = (f32[192,384]{1,0:T(8,128)S(1)}, f32[192,384]{1,0:T(8,128)}, u32[]{:S(2)}) copy-start(f32[192,384]{1,0:T(8,128)} %refs_2_.6) | copy-start | bytes 884740
  0.7 4.8 %copy-start.10 = (s32[64,128]{1,0:T(8,128)S(1)}, s32[64,128]{1,0:T(8,128)}, u32[]{:S(2)}) copy-start(s32[64,128]{1,0:T(8,128)} %refs_11_.5) | copy-start | bytes 98308
  0.7 4.8 %copy-start.9 = (f32[64,128]{1,0:T(8,128)S(1)}, f32[64,128]{1,0:T(8,128)}, u32[]{:S(2)}) copy-start(f32[64,128]{1,0:T(8,128)} %refs_10_.5) | copy-start | bytes 98308
  0.7 4.8 %copy-start.8 = (f32[64,128]{1,0:T(8,128)S(1)}, f32[64,128]{1,0:T(8,128)}, u32[]{:S(2)}) copy-start(f32[64,128]{1,0:T(8,128)} %refs_9_.5) | copy-start | bytes 98308
  0.7 4.8 %copy-start.7 = (f32[64,128]{1,0:T(8,128)S(1)}, f32[64,128]{1,0:T(8,128)}, u32[]{:S(2)}) copy-start(f32[64,128]{1,0:T(8,128)} %refs_7_.7) | copy-start | bytes 98308
  3.3 2.3 %copy-start.12 = (s32[2]{0:T(128)S(1)}, s32[2]{0:T(128)}, u32[]{:S(2)}) copy-start(s32[2]{0:T(128)} %refs_0_.9) | copy-start | bytes 28
  3.3 2.3 %copy-start.13 = (f32[6]{0:T(128)S(1)}, f32[6]{0:T(128)}, u32[]{:S(2)}) copy-start(f32[6]{0:T(128)} %refs_6_.7) | copy-start | bytes 76
  3.3 8.3 %collective-permute-start = (f32[236,128]{1,0:T(8,128)}, f32[236,128]{1,0:T(8,128)S(1)}, u32[]{:S(2)}, u32[]{:S(2)}) collective-permute-start(f32[236,128]{1,0:T(8,128)} %get-tuple-element.32), channel_id=1, source_target_pairs={{0,4},{4,0},{8,12},{12,8},{1,5},{5,1},{9,13},{13,9},{2,6},{6,2},{1... | collective-permute-start | bytes 362504 | tf_op jit(solution)/shard_map/ppermute | solution.py:33
  11.7 7.6 %collective-permute-start.1 = (f32[208,128]{1,0:T(8,128)S(1)}, f32[208,128]{1,0:T(8,128)S(1)}, u32[]{:S(2)}, u32[]{:S(2)}) collective-permute-start(f32[208,128]{1,0:T(8,128)S(1)} %get-tuple-element.42), channel_id=1, source_target_pairs={{0,1},{1,0},{2,3},{3,2},{4,5},{5,4},{6,7},{7,6},{8,9},{9,8},{10,11... | collective-permute-start | bytes 319496 | tf_op jit(solution)/shard_map/ppermute | solution.py:33
  12.8 6.6 %collective-permute-start.2 = (f32[208,128]{1,0:T(8,128)S(1)}, f32[208,128]{1,0:T(8,128)S(1)}, u32[]{:S(2)}, u32[]{:S(2)}) collective-permute-start(f32[208,128]{1,0:T(8,128)S(1)} %get-tuple-element.43), channel_id=1, source_target_pairs={{1,2},{2,1},{5,6},{6,5},{9,10},{10,9},{13,14},{14,13},{17,18},{18,... | collective-permute-start | bytes 319496 | tf_op jit(solution)/shard_map/ppermute | solution.py:39
  15.8 3.6 %copy-start.11 = (f32[20,128]{1,0:T(8,128)S(1)}, f32[20,128]{1,0:T(8,128)}, u32[]{:S(2)}) copy-start(f32[20,128]{1,0:T(8,128)} %get-tuple-element.44.refs_6_) | copy-start | bytes 30724
  23.1 6.2 %collective-permute-start.4 = (f32[92,128]{1,0:T(8,128)S(1)}, f32[92,128]{1,0:T(8,128)S(1)}, u32[]{:S(2)}, u32[]{:S(2)}) collective-permute-start(f32[92,128]{1,0:T(8,128)S(1)} %get-tuple-element.51), channel_id=1, source_target_pairs={{4,8},{8,4},{5,9},{9,5},{6,10},{10,6},{7,11},{11,7},{20,24},{24,20... | collective-permute-start | bytes 141320 | tf_op jit(solution)/shard_map/ppermute | solution.py:39
  23.8 5.5 %collective-permute-start.3 = (f32[64,128]{1,0:T(8,128)S(1)}, f32[64,128]{1,0:T(8,128)S(1)}, u32[]{:S(2)}, u32[]{:S(2)}) collective-permute-start(f32[64,128]{1,0:T(8,128)S(1)} %get-tuple-element.50.refs_2_), channel_id=1, source_target_pairs={{0,4},{4,0},{8,12},{12,8},{1,5},{5,1},{9,13},{13,9},{2,6},{6,2},{1... | collective-permute-start | bytes 98312 | tf_op jit(solution)/shard_map/ppermute | solution.py:33

commit v4 on v3

--- a/solution.py
+++ b/solution.py
@@ -268,10 +268,27 @@
             )
 
 
+def pieces(value):
+    high = value.astype(jnp.bfloat16)
+    rest = value - high.astype(F32)
+    middle = rest.astype(jnp.bfloat16)
+    return high, middle, (rest - middle.astype(F32)).astype(jnp.bfloat16)
+
+
 def dot(a, b):
-    return lax.dot_general(
-        a, b, (((1,), (0,)), ((), ())), precision=lax.Precision.HIGHEST, preferred_element_type=F32
-    )
+    return lax.dot_general(a, b, (((1,), (0,)), ((), ())), preferred_element_type=F32)
+
+
+def pick_columns(value, picks):
+    rows = value.shape[0]
+    result = dot(jnp.concatenate(pieces(value), 0), picks.astype(jnp.bfloat16))
+    return (result[2 * rows :] + result[rows : 2 * rows]) + result[:rows]
+
+
+def pick_rows(picks, value):
+    cols = value.shape[1]
+    result = dot(picks.astype(jnp.bfloat16), jnp.concatenate(pieces(value), 1))
+    return (result[:, 2 * cols :] + result[:, cols : 2 * cols]) + result[:, :cols]
 
 
 def iota(shape, dim):
@@ -284,15 +301,13 @@
     return gx, lax.div(gx, block_size), slot == 0, slot == block_size - 1
 
 
-def grid_edges(ocean_mx, beyond, own_offset, ocean_rows, spread_to, wf, rows, edges):
-    at = own_offset - 1
-    own = [ocean_mx[pl.ds(at, 1), :] * SB, ocean_mx[ocean_rows - 1 : ocean_rows, :] * SB]
-    source = [jnp.concatenate(own + own * 3, 0)]
-    if beyond:
-        picks = iota((8, ocean_rows), 1) == jnp.where(iota((8, ocean_rows), 0) == 0, at, ocean_rows - 1)
-        source += [dot(picks.astype(F32), tile) for tile in beyond]
-    source = jnp.concatenate(source, 1)
-    spread = dot(source, spread_to.astype(F32))
+def edge_rows(load, own_offset, ocean_rows):
+    west, east = load(own_offset - 1), load(ocean_rows - 1)
+    return jnp.concatenate([west, east] + [east] * 14, 0)
+
+
+def grid_edges(sources, spread_to, wf, rows, edges):
+    spread = pick_columns(jnp.concatenate(sources, 1), spread_to.astype(F32))
     for t in range(edges.shape[1]):
         cut = spread[:, t * LANES : (t + 1) * LANES]
         wet_first = wf[t, pl.ds(8, 8), :]
@@ -301,7 +316,7 @@
         edges[1, t, :, :] = jnp.broadcast_to(cut[1:2, :] * wet_last[7:8, :], (8, LANES))
 
 
-def run_coastal(tiles, n, rows, first, last, state, edges, ring):
+def run_coastal(tiles, n, rows, first, last, state, edges, ring, unroll):
     e, g, x, y, d, kx, ky, ox, oy = state
     sub = iota((8, LANES), 0)
     ghost = n > rows // 8
@@ -324,7 +339,7 @@
         flux_pass(tiles, n, e, g, x, y, kx, ky, ox, oy, fix, ring, ghost)
         return carry
 
-    lax.fori_loop(0, FSTEPS, step, 0, unroll=4)
+    lax.fori_loop(0, FSTEPS, step, 0, unroll=unroll)
 
 
 def interior_kernel(block_size, *refs):
@@ -350,9 +365,10 @@
             strip[f, src, :] = strip_lanes(values[0][f], values[-1][f])
 
     spread_to = iota((LANES, cols), 0) == lax.div(iota((LANES, cols), 1), R)
-    grid_edges(ocean_mx, [], offsets[grid], ocean_rows, spread_to, wf, rows, edges)
+    sources = [edge_rows(lambda at: ocean_mx[pl.ds(at, 1), :] * SB, offsets[grid], ocean_rows)]
+    grid_edges(sources, spread_to, wf, rows, edges)
     prepare_faces(tiles, n, kf, wf, kx, ky, ox, oy, False)
-    run_coastal(tiles, n, rows, first, last, (e, g, x, y, d, kx, ky, ox, oy), edges, False)
+    run_coastal(tiles, n, rows, first, last, (e, g, x, y, d, kx, ky, ox, oy), edges, False, 4)
     for r in range(n):
         to, here = pl.ds(8 * r, 8), pl.ds(8 + 8 * r, 8)
         for t in range(tiles):
@@ -403,7 +419,7 @@
             flux_pass(tiles, n, e, g, x, y, kx, ky, ox, oy, lambda r, t, fx: fx, False)
             return carry
 
-        lax.fori_loop(0, FSTEPS, step, 0, unroll=4)
+        lax.fori_loop(0, FSTEPS, step, 0, unroll=FSTEPS)
 
         open_end = jnp.logical_not(jnp.where(to_next, last, first))
         for half in range(2):
@@ -429,7 +445,7 @@
     shape = (ocean_rows, eta.shape[0])
     coarse_row = lax.rem(lax.div(iota(shape, 1), R) + own_offset, ocean_rows)
     gather_rows = (coarse_row == iota(shape, 0)).astype(F32)
-    return dot(dot(gather_rows, eta), gather_cols) * (1.0 / (R * R))
+    return pick_rows(gather_rows, pick_columns(eta, gather_cols)) * (1.0 / (R * R))
 
 
 def border_kernel(block_size, cols, *refs):
@@ -468,12 +484,12 @@
             dest[f][0, here, :] = jnp.where(lane < LANES - 16, value, west)
 
     ocean_rows = ocean_mx.shape[0]
-    from_even, from_odd = gy_even[0:ocean_rows, :], gy_odd[0:ocean_rows, :]
+    from_even = edge_rows(lambda at: gy_even[pl.ds(at, 1), :], offsets[grid], ocean_rows)
+    from_odd = edge_rows(lambda at: gy_odd[pl.ds(at, 1), :], offsets[grid], ocean_rows)
     from_east = jnp.where(gy_is_even, from_even, from_odd)
     from_west = jnp.where(gy_is_even, from_odd, from_even)
-    lanes = iota((ocean_rows, LANES), 1)
     mx_halo = jnp.where(
-        lanes < ITERS,
+        iota((16, LANES), 1) < ITERS,
         roll_to(from_east, OLANE + ITERS, 0),
         roll_to(from_west, OLANE + ITERS, LANES - ITERS),
     )
@@ -482,9 +498,10 @@
     wanted = jnp.where(to < 64, wanted, jnp.where(to < 80, LANES + lax.div(to - 64, R), 0))
     wanted = jnp.where(to < LANES - 16, wanted, 2 * LANES - 1 - lax.div(LANES - 1 - to, R))
     spread_to = iota((2 * LANES, LANES), 0) == wanted
-    grid_edges(ocean_mx, [mx_halo], offsets[grid], ocean_rows, spread_to, wf, rows, edges)
+    own_rows = edge_rows(lambda at: ocean_mx[pl.ds(at, 1), :] * SB, offsets[grid], ocean_rows)
+    grid_edges([own_rows, mx_halo], spread_to, wf, rows, edges)
     prepare_faces(1, n, kf, wf, kx, ky, ox, oy)
-    run_coastal(1, n, rows, first, last, (e, g, x, y, d, kx, ky, ox, oy), edges, True)
+    run_coastal(1, n, rows, first, last, (e, g, x, y, d, kx, ky, ox, oy), edges, True, FSTEPS)
 
     for i, (held, scale) in enumerate(((e, 1.0 / SA), (x, 1.0 / SB), (y, 1.0 / SB))):
         outs[i][...] = held[0, 8 : 8 + rows, :] * scale

time: 31.4 us -> 30.7 us (0.978)
  Pallas kernels: 19.4 us -> 18.7 us
    pallas_call x1, Pallas kernels: 3.54 us -> 3.06 us  [shards(): pl.pallas_call(functools.partial(rows_kernel, block_size), out_shape=(sha...]
  transfers between devices with their start and end apart: 5 -> 5, of which waited for: 0 -> 0; matrix products, arithmetic and copies ran while one was open for 0% -> 0% of each run, Pallas kernels for 36% -> 35%
where the time goes in v4:
time: 30.7 us; the launch traced here: 30.5 us
  Pallas kernels  18.7 us (61%)
  starting transfers between devices  10.8 us (35%)
  between operations  0.93 us (3%)
    ppermute x3, starting transfers between devices, swap_even(): lax.ppermute(value, axis, [(i, i ^ 1) for i in range(count) if i ^ 1 < co...  7.11 us
    pallas_call x1, Pallas kernels, shards(): pl.pallas_call(functools.partial(interior_kernel, block_size), out_shape=...  5.97 us
    ppermute x2, starting transfers between devices, swap_odd(): return lax.ppermute(value, axis, [(a, b) for a, b in pairs if b < count])  3.68 us
    pallas_call x1, Pallas kernels, shards(): pl.pallas_call(functools.partial(border_kernel, block_size, cols), out_sh...  3.52 us
    pallas_call x1, Pallas kernels, shards(): pl.pallas_call(functools.partial(rows_kernel, block_size), out_shape=(sha...  3.06 us
    pallas_call x1, Pallas kernels, shards(): pl.pallas_call(functools.partial(pack_rows_kernel, pairs_only), out_shape...  2.52 us
    pallas_call x1, Pallas kernels, shards(): pl.pallas_call(functools.partial(ocean_kernel, block_size), out_shape=(sh...  1.95 us
    pallas_call x1, Pallas kernels, shards(): pl.pallas_call(finish_kernel, out_shape=(shape(rows, cols),) * 3 + (shape...  1.57 us
  transfers between devices with their start and end apart: 5, of which 0 were waited for; matrix products, arithmetic and copies ran while one was open for 0% of the time, Pallas kernels for 35%

profile of v4, /device:TPU:1, one launch (start us, length us, event | category | flops | bytes accessed | tf_op | source)
XLA Modules:
  0.0 30.5 jit_solution(13134062601839348672)
XLA Ops:
  0.6 0.0 copy-start.6
  0.6 0.0 copy-start.5
  0.7 0.0 copy-start.4
  0.7 0.0 copy-start.3
  0.7 2.5 %pack_rows.1 = (f32[236,128]{1,0:T(8,128)}, f32[20,128]{1,0:T(8,128)}) custom-call(f32[6]{0:T(128)} %refs_6_.7, f32[192,384]{1,0:T(8,128)} %refs_2_.6, f32[192,384]{1,0:T(8,128)} %refs_3_.5, f32[192,384]{1,0:T(8,128)} %refs_4_.5, f32[192,384]{1,0:T(8,128)} %refs_5_.5, s32[192,384]{1,0:T(8,128)} %refs_6_.6, s32[192,384]{1,0:T(8,128)} %refs_7_.6, ...), custom_call_target="tpu_custom_call" | custom-call | tf_op jit(solution)/shard_map/pack_rows/pallas_call | solution.py:664
  3.3 0.0 copy-start.12
  3.3 0.0 copy-start.13
  3.3 2.2 %collective-permute-start = (f32[236,128]{1,0:T(8,128)}, f32[236,128]{1,0:T(8,128)S(1)}, u32[]{:S(2)}, u32[]{:S(2)}) collective-permute-start(f32[236,128]{1,0:T(8,128)} %get-tuple-element.32), channel_id=1, source_target_pairs={{0,4},{4,0},{8,12},{12,8},{1,5},{5,1},{9,13},{13,9},{2,6},{6,2},{1... | collective-permute-start | bytes 362504 | tf_op jit(solution)/shard_map/ppermute | solution.py:33
  5.6 6.0 %interior.1 = (f32[192,384]{1,0:T(8,128)S(1)}, f32[192,384]{1,0:T(8,128)S(1)}, f32[192,384]{1,0:T(8,128)S(1)}, f32[192,128]{1,0:T(8,128)S(1)}, f32[192,128]{1,0:T(8,128)S(1)}, /*index=5*/f32[6,192,128]{2,1,0:T(8,128)S(1)}) custom-call(f32[6]{0:T(128)S(1)} %copy-done.13, s32[2]{0:T(128)S(1)} %copy-done.12, f32[192,384]{1,0:T(8,128)S(1)} %copy-done, ...), custom_call_target="tpu_custom_call" | custom-call | bytes 20000000 | tf_op jit(solution)/shard_map/interior/pallas_call | solution.py:680
  11.6 0.0 collective-permute-done.refs_8_.refs_2_.refs_3_.refs_14_
  11.6 0.1 pack_columns.1
  11.7 1.0 %collective-permute-start.1 = (f32[208,128]{1,0:T(8,128)S(1)}, f32[208,128]{1,0:T(8,128)S(1)}, u32[]{:S(2)}, u32[]{:S(2)}) collective-permute-start(f32[208,128]{1,0:T(8,128)S(1)} %get-tuple-element.42), channel_id=1, source_target_pairs={{0,1},{1,0},{2,3},{3,2},{4,5},{5,4},{6,7},{7,6},{8,9},{9,8},{10,11... | collective-permute-start | bytes 319496 | tf_op jit(solution)/shard_map/ppermute | solution.py:33
  12.7 3.0 %collective-permute-start.2 = (f32[208,128]{1,0:T(8,128)S(1)}, f32[208,128]{1,0:T(8,128)S(1)}, u32[]{:S(2)}, u32[]{:S(2)}) collective-permute-start(f32[208,128]{1,0:T(8,128)S(1)} %get-tuple-element.43), channel_id=1, source_target_pairs={{1,2},{2,1},{5,6},{6,5},{9,10},{10,9},{13,14},{14,13},{17,18},{18,... | collective-permute-start | bytes 319496 | tf_op jit(solution)/shard_map/ppermute | solution.py:39
  15.8 0.0 copy-start.11
  15.8 3.1 %rows.1 = (f32[192,384]{1,0:T(8,128)S(1)}, f32[192,384]{1,0:T(8,128)S(1)}, f32[192,384]{1,0:T(8,128)S(1)}, f32[64,128]{1,0:T(8,128)S(1)}) custom-call(f32[6]{0:T(128)S(1)} %copy-done.13, s32[2]{0:T(128)S(1)} %copy-done.12, f32[192,384]{1,0:T(8,128)S(1)} %copy-done, f32[192,384]{1,0:T(8,128)S(1)} %copy-done.1, f32[192,384]{1,0:T(8,128)S(1)} %copy-done.2, ...), custom_call_target="tpu_custom_call" | custom-call | bytes 10000000 | tf_op jit(solution)/shard_map/rows/pallas_call | solution.py:703
  18.8 0.0 collective-permute-done.1.refs_4_.refs_12_
  18.8 0.0 collective-permute-done.2.refs_5_.refs_13_
  18.9 3.5 %border.1 = (f32[192,128]{1,0:T(8,128)S(1)}, f32[192,128]{1,0:T(8,128)S(1)}, f32[192,128]{1,0:T(8,128)S(1)}, f32[64,128]{1,0:T(8,128)S(1)}, f32[92,128]{1,0:T(8,128)S(1)}) custom-call(s32[2]{0:T(128)S(1)} %copy-done.12, f32[6,192,128]{2,1,0:T(8,128)S(1)} %get-tuple-element.39.refs_1_, f32[64,128]{1,0:T(8,128)S(1)} %copy-done.6, ...), custom_call_target="tpu_custom_call" | custom-call | tf_op jit(solution)/shard_map/border/pallas_call | solution.py:715
  22.4 0.7 %collective-permute-start.4 = (f32[92,128]{1,0:T(8,128)S(1)}, f32[92,128]{1,0:T(8,128)S(1)}, u32[]{:S(2)}, u32[]{:S(2)}) collective-permute-start(f32[92,128]{1,0:T(8,128)S(1)} %get-tuple-element.51), channel_id=1, source_target_pairs={{4,8},{8,4},{5,9},{9,5},{6,10},{10,6},{7,11},{11,7},{20,24},{24,20... | collective-permute-start | bytes 141320 | tf_op jit(solution)/shard_map/ppermute | solution.py:39
  23.1 3.9 %collective-permute-start.3 = (f32[64,128]{1,0:T(8,128)S(1)}, f32[64,128]{1,0:T(8,128)S(1)}, u32[]{:S(2)}, u32[]{:S(2)}) collective-permute-start(f32[64,128]{1,0:T(8,128)S(1)} %get-tuple-element.50.refs_2_), channel_id=1, source_target_pairs={{0,4},{4,0},{8,12},{12,8},{1,5},{5,1},{9,13},{13,9},{2,6},{6,2},{1... | collective-permute-start | bytes 98312 | tf_op jit(solution)/shard_map/ppermute | solution.py:33
  27.0 1.6 %finish.1 = (f32[192,384]{1,0:T(8,128)}, f32[192,384]{1,0:T(8,128)}, f32[192,384]{1,0:T(8,128)}, f32[5,2,72,128]{3,2,1,0:T(8,128)S(1)}) custom-call(f32[192,384]{1,0:T(8,128)S(1)} %get-tuple-element.36.refs_0_, f32[192,384]{1,0:T(8,128)S(1)} %get-tuple-element.37.refs_1_, f32[192,384]{1,0:T(8,128)S(1)} %get-tuple-element.38.refs_2_, ...), custom_call_target="tpu_custom_call" | custom-call | bytes 5000000 | tf_op jit(solution)/shard_map/finish/pallas_call | solution.py:728
  28.5 0.0 collective-permute-done.3.refs_3_
  28.5 0.0 collective-permute-done.4.refs_4_
  28.6 1.9 %ocean.1 = (f32[64,128]{1,0:T(8,128)}, f32[64,128]{1,0:T(8,128)}, f32[64,128]{1,0:T(8,128)}) custom-call(s32[2]{0:T(128)S(1)} %copy-done.12, f32[5,2,72,128]{3,2,1,0:T(8,128)S(1)} %get-tuple-element.49.refs_1_, f32[64,128]{1,0:T(8,128)S(1)} %get-tuple-element.50.refs_2_, f32[64,128]{1,0:T(8,128)S(1)} %collective-permute-done.3.refs_3_, ...), custom_call_target="tpu_custom_call" | custom-call | tf_op jit(solution)/shard_map/ocean/pallas_call | solution.py:739
  (21 shorter events, 0.0 us)
Async XLA Ops:
  0.6 4.9 %copy-start.6 = (f32[64,128]{1,0:T(8,128)S(1)}, f32[64,128]{1,0:T(8,128)}, u32[]{:S(2)}) copy-start(f32[64,128]{1,0:T(8,128)} %refs_8_.5) | copy-start | bytes 98308
  0.6 4.9 %copy-start.5 = (s32[192,384]{1,0:T(8,128)S(1)}, s32[192,384]{1,0:T(8,128)}, u32[]{:S(2)}) copy-start(s32[192,384]{1,0:T(8,128)} %refs_7_.6) | copy-start | bytes 884740
  0.7 4.8 %copy-start.4 = (s32[192,384]{1,0:T(8,128)S(1)}, s32[192,384]{1,0:T(8,128)}, u32[]{:S(2)}) copy-start(s32[192,384]{1,0:T(8,128)} %refs_6_.6) | copy-start | bytes 884740
  0.7 4.8 %copy-start.3 = (f32[192,384]{1,0:T(8,128)S(1)}, f32[192,384]{1,0:T(8,128)}, u32[]{:S(2)}) copy-start(f32[192,384]{1,0:T(8,128)} %refs_5_.5) | copy-start | bytes 884740
  0.7 4.8 %copy-start.2 = (f32[192,384]{1,0:T(8,128)S(1)}, f32[192,384]{1,0:T(8,128)}, u32[]{:S(2)}) copy-start(f32[192,384]{1,0:T(8,128)} %refs_4_.5) | copy-start | bytes 884740
  0.7 4.8 %copy-start.1 = (f32[192,384]{1,0:T(8,128)S(1)}, f32[192,384]{1,0:T(8,128)}, u32[]{:S(2)}) copy-start(f32[192,384]{1,0:T(8,128)} %refs_3_.5) | copy-start | bytes 884740
  0.7 4.8 %copy-start = (f32[192,384]{1,0:T(8,128)S(1)}, f32[192,384]{1,0:T(8,128)}, u32[]{:S(2)}) copy-start(f32[192,384]{1,0:T(8,128)} %refs_2_.6) | copy-start | bytes 884740
  0.7 4.8 %copy-start.10 = (s32[64,128]{1,0:T(8,128)S(1)}, s32[64,128]{1,0:T(8,128)}, u32[]{:S(2)}) copy-start(s32[64,128]{1,0:T(8,128)} %refs_11_.5) | copy-start | bytes 98308
  0.7 4.8 %copy-start.9 = (f32[64,128]{1,0:T(8,128)S(1)}, f32[64,128]{1,0:T(8,128)}, u32[]{:S(2)}) copy-start(f32[64,128]{1,0:T(8,128)} %refs_10_.5) | copy-start | bytes 98308
  0.7 4.8 %copy-start.8 = (f32[64,128]{1,0:T(8,128)S(1)}, f32[64,128]{1,0:T(8,128)}, u32[]{:S(2)}) copy-start(f32[64,128]{1,0:T(8,128)} %refs_9_.5) | copy-start | bytes 98308
  0.7 4.8 %copy-start.7 = (f32[64,128]{1,0:T(8,128)S(1)}, f32[64,128]{1,0:T(8,128)}, u32[]{:S(2)}) copy-start(f32[64,128]{1,0:T(8,128)} %refs_7_.7) | copy-start | bytes 98308
  3.3 2.3 %copy-start.12 = (s32[2]{0:T(128)S(1)}, s32[2]{0:T(128)}, u32[]{:S(2)}) copy-start(s32[2]{0:T(128)} %refs_0_.9) | copy-start | bytes 28
  3.3 2.3 %copy-start.13 = (f32[6]{0:T(128)S(1)}, f32[6]{0:T(128)}, u32[]{:S(2)}) copy-start(f32[6]{0:T(128)} %refs_6_.7) | copy-start | bytes 76
  3.3 8.3 %collective-permute-start = (f32[236,128]{1,0:T(8,128)}, f32[236,128]{1,0:T(8,128)S(1)}, u32[]{:S(2)}, u32[]{:S(2)}) collective-permute-start(f32[236,128]{1,0:T(8,128)} %get-tuple-element.32), channel_id=1, source_target_pairs={{0,4},{4,0},{8,12},{12,8},{1,5},{5,1},{9,13},{13,9},{2,6},{6,2},{1... | collective-permute-start | bytes 362504 | tf_op jit(solution)/shard_map/ppermute | solution.py:33
  11.7 7.1 %collective-permute-start.1 = (f32[208,128]{1,0:T(8,128)S(1)}, f32[208,128]{1,0:T(8,128)S(1)}, u32[]{:S(2)}, u32[]{:S(2)}) collective-permute-start(f32[208,128]{1,0:T(8,128)S(1)} %get-tuple-element.42), channel_id=1, source_target_pairs={{0,1},{1,0},{2,3},{3,2},{4,5},{5,4},{6,7},{7,6},{8,9},{9,8},{10,11... | collective-permute-start | bytes 319496 | tf_op jit(solution)/shard_map/ppermute | solution.py:33
  12.7 6.1 %collective-permute-start.2 = (f32[208,128]{1,0:T(8,128)S(1)}, f32[208,128]{1,0:T(8,128)S(1)}, u32[]{:S(2)}, u32[]{:S(2)}) collective-permute-start(f32[208,128]{1,0:T(8,128)S(1)} %get-tuple-element.43), channel_id=1, source_target_pairs={{1,2},{2,1},{5,6},{6,5},{9,10},{10,9},{13,14},{14,13},{17,18},{18,... | collective-permute-start | bytes 319496 | tf_op jit(solution)/shard_map/ppermute | solution.py:39
  15.8 3.1 %copy-start.11 = (f32[20,128]{1,0:T(8,128)S(1)}, f32[20,128]{1,0:T(8,128)}, u32[]{:S(2)}) copy-start(f32[20,128]{1,0:T(8,128)} %get-tuple-element.44.refs_6_) | copy-start | bytes 30724
  22.4 6.2 %collective-permute-start.4 = (f32[92,128]{1,0:T(8,128)S(1)}, f32[92,128]{1,0:T(8,128)S(1)}, u32[]{:S(2)}, u32[]{:S(2)}) collective-permute-start(f32[92,128]{1,0:T(8,128)S(1)} %get-tuple-element.51), channel_id=1, source_target_pairs={{4,8},{8,4},{5,9},{9,5},{6,10},{10,6},{7,11},{11,7},{20,24},{24,20... | collective-permute-start | bytes 141320 | tf_op jit(solution)/shard_map/ppermute | solution.py:39
  23.1 5.5 %collective-permute-start.3 = (f32[64,128]{1,0:T(8,128)S(1)}, f32[64,128]{1,0:T(8,128)S(1)}, u32[]{:S(2)}, u32[]{:S(2)}) collective-permute-start(f32[64,128]{1,0:T(8,128)S(1)} %get-tuple-element.50.refs_2_), channel_id=1, source_target_pairs={{0,4},{4,0},{8,12},{12,8},{1,5},{5,1},{9,13},{13,9},{2,6},{6,2},{1... | collective-permute-start | bytes 98312 | tf_op jit(solution)/shard_map/ppermute | solution.py:33

commit v5 on v4

--- a/solution.py
+++ b/solution.py
@@ -368,7 +368,7 @@
     sources = [edge_rows(lambda at: ocean_mx[pl.ds(at, 1), :] * SB, offsets[grid], ocean_rows)]
     grid_edges(sources, spread_to, wf, rows, edges)
     prepare_faces(tiles, n, kf, wf, kx, ky, ox, oy, False)
-    run_coastal(tiles, n, rows, first, last, (e, g, x, y, d, kx, ky, ox, oy), edges, False, 4)
+    run_coastal(tiles, n, rows, first, last, (e, g, x, y, d, kx, ky, ox, oy), edges, False, 6)
     for r in range(n):
         to, here = pl.ds(8 * r, 8), pl.ds(8 + 8 * r, 8)
         for t in range(tiles):

time: 30.7 us -> 30.7 us (level)
  no operation moved by 1% of the time
where the time goes in v5:
time: 30.7 us; the launch traced here: 30.5 us
  Pallas kernels  18.6 us (61%)
  starting transfers between devices  10.8 us (35%)
  between operations  0.93 us (3%)
    ppermute x3, starting transfers between devices, swap_even(): lax.ppermute(value, axis, [(i, i ^ 1) for i in range(count) if i ^ 1 < co...  7.11 us
    pallas_call x1, Pallas kernels, shards(): pl.pallas_call(functools.partial(interior_kernel, block_size), out_shape=...  5.91 us
    ppermute x2, starting transfers between devices, swap_odd(): return lax.ppermute(value, axis, [(a, b) for a, b in pairs if b < count])  3.68 us
    pallas_call x1, Pallas kernels, shards(): pl.pallas_call(functools.partial(border_kernel, block_size, cols), out_sh...  3.52 us
    pallas_call x1, Pallas kernels, shards(): pl.pallas_call(functools.partial(rows_kernel, block_size), out_shape=(sha...  3.06 us
    pallas_call x1, Pallas kernels, shards(): pl.pallas_call(functools.partial(pack_rows_kernel, pairs_only), out_shape...  2.52 us
    pallas_call x1, Pallas kernels, shards(): pl.pallas_call(functools.partial(ocean_kernel, block_size), out_shape=(sh...  1.95 us
    pallas_call x1, Pallas kernels, shards(): pl.pallas_call(finish_kernel, out_shape=(shape(rows, cols),) * 3 + (shape...  1.57 us
  transfers between devices with their start and end apart: 5, of which 0 were waited for; matrix products, arithmetic and copies ran while one was open for 0% of the time, Pallas kernels for 35%

profile of v5, /device:TPU:1, one launch (start us, length us, event | category | flops | bytes accessed | tf_op | source)
XLA Modules:
  0.0 30.5 jit_solution(9554694370366405627)
XLA Ops:
  0.6 0.0 copy-start.6
  0.6 0.0 copy-start.5
  0.7 0.0 copy-start.4
  0.7 0.0 copy-start.3
  0.7 2.5 %pack_rows.1 = (f32[236,128]{1,0:T(8,128)}, f32[20,128]{1,0:T(8,128)}) custom-call(f32[6]{0:T(128)} %refs_6_.7, f32[192,384]{1,0:T(8,128)} %refs_2_.6, f32[192,384]{1,0:T(8,128)} %refs_3_.5, f32[192,384]{1,0:T(8,128)} %refs_4_.5, f32[192,384]{1,0:T(8,128)} %refs_5_.5, s32[192,384]{1,0:T(8,128)} %refs_6_.6, s32[192,384]{1,0:T(8,128)} %refs_7_.6, ...), custom_call_target="tpu_custom_call" | custom-call | tf_op jit(solution)/shard_map/pack_rows/pallas_call | solution.py:664
  3.3 0.0 copy-start.12
  3.3 0.0 copy-start.13
  3.3 2.2 %collective-permute-start = (f32[236,128]{1,0:T(8,128)}, f32[236,128]{1,0:T(8,128)S(1)}, u32[]{:S(2)}, u32[]{:S(2)}) collective-permute-start(f32[236,128]{1,0:T(8,128)} %get-tuple-element.32), channel_id=1, source_target_pairs={{0,4},{4,0},{8,12},{12,8},{1,5},{5,1},{9,13},{13,9},{2,6},{6,2},{1... | collective-permute-start | bytes 362504 | tf_op jit(solution)/shard_map/ppermute | solution.py:33
  5.6 5.9 %interior.1 = (f32[192,384]{1,0:T(8,128)S(1)}, f32[192,384]{1,0:T(8,128)S(1)}, f32[192,384]{1,0:T(8,128)S(1)}, f32[192,128]{1,0:T(8,128)S(1)}, f32[192,128]{1,0:T(8,128)S(1)}, /*index=5*/f32[6,192,128]{2,1,0:T(8,128)S(1)}) custom-call(f32[6]{0:T(128)S(1)} %copy-done.13, s32[2]{0:T(128)S(1)} %copy-done.12, f32[192,384]{1,0:T(8,128)S(1)} %copy-done, ...), custom_call_target="tpu_custom_call" | custom-call | bytes 20000000 | tf_op jit(solution)/shard_map/interior/pallas_call | solution.py:680
  11.5 0.0 collective-permute-done.refs_8_.refs_2_.refs_3_.refs_14_
  11.5 0.1 pack_columns.1
  11.6 1.0 %collective-permute-start.1 = (f32[208,128]{1,0:T(8,128)S(1)}, f32[208,128]{1,0:T(8,128)S(1)}, u32[]{:S(2)}, u32[]{:S(2)}) collective-permute-start(f32[208,128]{1,0:T(8,128)S(1)} %get-tuple-element.42), channel_id=1, source_target_pairs={{0,1},{1,0},{2,3},{3,2},{4,5},{5,4},{6,7},{7,6},{8,9},{9,8},{10,11... | collective-permute-start | bytes 319496 | tf_op jit(solution)/shard_map/ppermute | solution.py:33
  12.7 3.0 %collective-permute-start.2 = (f32[208,128]{1,0:T(8,128)S(1)}, f32[208,128]{1,0:T(8,128)S(1)}, u32[]{:S(2)}, u32[]{:S(2)}) collective-permute-start(f32[208,128]{1,0:T(8,128)S(1)} %get-tuple-element.43), channel_id=1, source_target_pairs={{1,2},{2,1},{5,6},{6,5},{9,10},{10,9},{13,14},{14,13},{17,18},{18,... | collective-permute-start | bytes 319496 | tf_op jit(solution)/shard_map/ppermute | solution.py:39
  15.7 0.0 copy-start.11
  15.7 3.1 %rows.1 = (f32[192,384]{1,0:T(8,128)S(1)}, f32[192,384]{1,0:T(8,128)S(1)}, f32[192,384]{1,0:T(8,128)S(1)}, f32[64,128]{1,0:T(8,128)S(1)}) custom-call(f32[6]{0:T(128)S(1)} %copy-done.13, s32[2]{0:T(128)S(1)} %copy-done.12, f32[192,384]{1,0:T(8,128)S(1)} %copy-done, f32[192,384]{1,0:T(8,128)S(1)} %copy-done.1, f32[192,384]{1,0:T(8,128)S(1)} %copy-done.2, ...), custom_call_target="tpu_custom_call" | custom-call | bytes 10000000 | tf_op jit(solution)/shard_map/rows/pallas_call | solution.py:703
  18.8 0.0 collective-permute-done.1.refs_4_.refs_12_
  18.8 0.0 collective-permute-done.2.refs_5_.refs_13_
  18.8 3.5 %border.1 = (f32[192,128]{1,0:T(8,128)S(1)}, f32[192,128]{1,0:T(8,128)S(1)}, f32[192,128]{1,0:T(8,128)S(1)}, f32[64,128]{1,0:T(8,128)S(1)}, f32[92,128]{1,0:T(8,128)S(1)}) custom-call(s32[2]{0:T(128)S(1)} %copy-done.12, f32[6,192,128]{2,1,0:T(8,128)S(1)} %get-tuple-element.39.refs_1_, f32[64,128]{1,0:T(8,128)S(1)} %copy-done.6, ...), custom_call_target="tpu_custom_call" | custom-call | tf_op jit(solution)/shard_map/border/pallas_call | solution.py:715
  22.3 0.7 %collective-permute-start.4 = (f32[92,128]{1,0:T(8,128)S(1)}, f32[92,128]{1,0:T(8,128)S(1)}, u32[]{:S(2)}, u32[]{:S(2)}) collective-permute-start(f32[92,128]{1,0:T(8,128)S(1)} %get-tuple-element.51), channel_id=1, source_target_pairs={{4,8},{8,4},{5,9},{9,5},{6,10},{10,6},{7,11},{11,7},{20,24},{24,20... | collective-permute-start | bytes 141320 | tf_op jit(solution)/shard_map/ppermute | solution.py:39
  23.0 3.9 %collective-permute-start.3 = (f32[64,128]{1,0:T(8,128)S(1)}, f32[64,128]{1,0:T(8,128)S(1)}, u32[]{:S(2)}, u32[]{:S(2)}) collective-permute-start(f32[64,128]{1,0:T(8,128)S(1)} %get-tuple-element.50.refs_2_), channel_id=1, source_target_pairs={{0,4},{4,0},{8,12},{12,8},{1,5},{5,1},{9,13},{13,9},{2,6},{6,2},{1... | collective-permute-start | bytes 98312 | tf_op jit(solution)/shard_map/ppermute | solution.py:33
  26.9 1.6 %finish.1 = (f32[192,384]{1,0:T(8,128)}, f32[192,384]{1,0:T(8,128)}, f32[192,384]{1,0:T(8,128)}, f32[5,2,72,128]{3,2,1,0:T(8,128)S(1)}) custom-call(f32[192,384]{1,0:T(8,128)S(1)} %get-tuple-element.36.refs_0_, f32[192,384]{1,0:T(8,128)S(1)} %get-tuple-element.37.refs_1_, f32[192,384]{1,0:T(8,128)S(1)} %get-tuple-element.38.refs_2_, ...), custom_call_target="tpu_custom_call" | custom-call | bytes 5000000 | tf_op jit(solution)/shard_map/finish/pallas_call | solution.py:728
  28.5 0.0 collective-permute-done.3.refs_3_
  28.5 0.0 collective-permute-done.4.refs_4_
  28.5 1.9 %ocean.1 = (f32[64,128]{1,0:T(8,128)}, f32[64,128]{1,0:T(8,128)}, f32[64,128]{1,0:T(8,128)}) custom-call(s32[2]{0:T(128)S(1)} %copy-done.12, f32[5,2,72,128]{3,2,1,0:T(8,128)S(1)} %get-tuple-element.49.refs_1_, f32[64,128]{1,0:T(8,128)S(1)} %get-tuple-element.50.refs_2_, f32[64,128]{1,0:T(8,128)S(1)} %collective-permute-done.3.refs_3_, ...), custom_call_target="tpu_custom_call" | custom-call | tf_op jit(solution)/shard_map/ocean/pallas_call | solution.py:739
  (21 shorter events, 0.0 us)
Async XLA Ops:
  0.6 4.9 %copy-start.6 = (f32[64,128]{1,0:T(8,128)S(1)}, f32[64,128]{1,0:T(8,128)}, u32[]{:S(2)}) copy-start(f32[64,128]{1,0:T(8,128)} %refs_8_.5) | copy-start | bytes 98308
  0.6 4.9 %copy-start.5 = (s32[192,384]{1,0:T(8,128)S(1)}, s32[192,384]{1,0:T(8,128)}, u32[]{:S(2)}) copy-start(s32[192,384]{1,0:T(8,128)} %refs_7_.6) | copy-start | bytes 884740
  0.7 4.8 %copy-start.4 = (s32[192,384]{1,0:T(8,128)S(1)}, s32[192,384]{1,0:T(8,128)}, u32[]{:S(2)}) copy-start(s32[192,384]{1,0:T(8,128)} %refs_6_.6) | copy-start | bytes 884740
  0.7 4.8 %copy-start.3 = (f32[192,384]{1,0:T(8,128)S(1)}, f32[192,384]{1,0:T(8,128)}, u32[]{:S(2)}) copy-start(f32[192,384]{1,0:T(8,128)} %refs_5_.5) | copy-start | bytes 884740
  0.7 4.8 %copy-start.2 = (f32[192,384]{1,0:T(8,128)S(1)}, f32[192,384]{1,0:T(8,128)}, u32[]{:S(2)}) copy-start(f32[192,384]{1,0:T(8,128)} %refs_4_.5) | copy-start | bytes 884740
  0.7 4.8 %copy-start.1 = (f32[192,384]{1,0:T(8,128)S(1)}, f32[192,384]{1,0:T(8,128)}, u32[]{:S(2)}) copy-start(f32[192,384]{1,0:T(8,128)} %refs_3_.5) | copy-start | bytes 884740
  0.7 4.8 %copy-start = (f32[192,384]{1,0:T(8,128)S(1)}, f32[192,384]{1,0:T(8,128)}, u32[]{:S(2)}) copy-start(f32[192,384]{1,0:T(8,128)} %refs_2_.6) | copy-start | bytes 884740
  0.7 4.8 %copy-start.10 = (s32[64,128]{1,0:T(8,128)S(1)}, s32[64,128]{1,0:T(8,128)}, u32[]{:S(2)}) copy-start(s32[64,128]{1,0:T(8,128)} %refs_11_.5) | copy-start | bytes 98308
  0.7 4.8 %copy-start.9 = (f32[64,128]{1,0:T(8,128)S(1)}, f32[64,128]{1,0:T(8,128)}, u32[]{:S(2)}) copy-start(f32[64,128]{1,0:T(8,128)} %refs_10_.5) | copy-start | bytes 98308
  0.7 4.8 %copy-start.8 = (f32[64,128]{1,0:T(8,128)S(1)}, f32[64,128]{1,0:T(8,128)}, u32[]{:S(2)}) copy-start(f32[64,128]{1,0:T(8,128)} %refs_9_.5) | copy-start | bytes 98308
  0.7 4.8 %copy-start.7 = (f32[64,128]{1,0:T(8,128)S(1)}, f32[64,128]{1,0:T(8,128)}, u32[]{:S(2)}) copy-start(f32[64,128]{1,0:T(8,128)} %refs_7_.7) | copy-start | bytes 98308
  3.3 2.3 %copy-start.12 = (s32[2]{0:T(128)S(1)}, s32[2]{0:T(128)}, u32[]{:S(2)}) copy-start(s32[2]{0:T(128)} %refs_0_.9) | copy-start | bytes 28
  3.3 2.3 %copy-start.13 = (f32[6]{0:T(128)S(1)}, f32[6]{0:T(128)}, u32[]{:S(2)}) copy-start(f32[6]{0:T(128)} %refs_6_.7) | copy-start | bytes 76
  3.3 8.2 %collective-permute-start = (f32[236,128]{1,0:T(8,128)}, f32[236,128]{1,0:T(8,128)S(1)}, u32[]{:S(2)}, u32[]{:S(2)}) collective-permute-start(f32[236,128]{1,0:T(8,128)} %get-tuple-element.32), channel_id=1, source_target_pairs={{0,4},{4,0},{8,12},{12,8},{1,5},{5,1},{9,13},{13,9},{2,6},{6,2},{1... | collective-permute-start | bytes 362504 | tf_op jit(solution)/shard_map/ppermute | solution.py:33
  11.6 7.1 %collective-permute-start.1 = (f32[208,128]{1,0:T(8,128)S(1)}, f32[208,128]{1,0:T(8,128)S(1)}, u32[]{:S(2)}, u32[]{:S(2)}) collective-permute-start(f32[208,128]{1,0:T(8,128)S(1)} %get-tuple-element.42), channel_id=1, source_target_pairs={{0,1},{1,0},{2,3},{3,2},{4,5},{5,4},{6,7},{7,6},{8,9},{9,8},{10,11... | collective-permute-start | bytes 319496 | tf_op jit(solution)/shard_map/ppermute | solution.py:33
  12.7 6.1 %collective-permute-start.2 = (f32[208,128]{1,0:T(8,128)S(1)}, f32[208,128]{1,0:T(8,128)S(1)}, u32[]{:S(2)}, u32[]{:S(2)}) collective-permute-start(f32[208,128]{1,0:T(8,128)S(1)} %get-tuple-element.43), channel_id=1, source_target_pairs={{1,2},{2,1},{5,6},{6,5},{9,10},{10,9},{13,14},{14,13},{17,18},{18,... | collective-permute-start | bytes 319496 | tf_op jit(solution)/shard_map/ppermute | solution.py:39
  15.7 3.1 %copy-start.11 = (f32[20,128]{1,0:T(8,128)S(1)}, f32[20,128]{1,0:T(8,128)}, u32[]{:S(2)}) copy-start(f32[20,128]{1,0:T(8,128)} %get-tuple-element.44.refs_6_) | copy-start | bytes 30724
  22.3 6.2 %collective-permute-start.4 = (f32[92,128]{1,0:T(8,128)S(1)}, f32[92,128]{1,0:T(8,128)S(1)}, u32[]{:S(2)}, u32[]{:S(2)}) collective-permute-start(f32[92,128]{1,0:T(8,128)S(1)} %get-tuple-element.51), channel_id=1, source_target_pairs={{4,8},{8,4},{5,9},{9,5},{6,10},{10,6},{7,11},{11,7},{20,24},{24,20... | collective-permute-start | bytes 141320 | tf_op jit(solution)/shard_map/ppermute | solution.py:39
  23.0 5.5 %collective-permute-start.3 = (f32[64,128]{1,0:T(8,128)S(1)}, f32[64,128]{1,0:T(8,128)S(1)}, u32[]{:S(2)}, u32[]{:S(2)}) collective-permute-start(f32[64,128]{1,0:T(8,128)S(1)} %get-tuple-element.50.refs_2_), channel_id=1, source_target_pairs={{0,4},{4,0},{8,12},{12,8},{1,5},{5,1},{9,13},{13,9},{2,6},{6,2},{1... | collective-permute-start | bytes 98312 | tf_op jit(solution)/shard_map/ppermute | solution.py:33
